TPU v7x, 256 devices: a whole 4x4x8 slice. The times are simulated.
256 devices in a mesh: tile: 64 (over z, y, x_hi), orient: 4 (over x_lo, core).
Axes of the slice: x: 4 (x_hi: 2, x_lo: 2; x = x_hi * 2 + x_lo), y: 4, z: 8, core: 2. Of those that a mesh axis runs over, the one named last changes fastest.
Arguments:
- micrograph: bfloat16 [64, 384, 384], P('tile'), may hold values from -6 to 6
- template_stack: bfloat16 [256, 16384], P(None, 'tile'), as said below
- orient_list: int32 [32], replicated, may hold values from 0 to 255
Outputs:
- peak: float32 [64, 384, 384], P('tile', 'orient')
- excess: float32 [64, 384, 384], P('tile', 'orient')
Inputs may be any that keep to these rules, and one draw needn't show every extreme that they name: `template_stack`: template pixels, finite.
All inputs are finite; a program needn't handle non-finite values.
Results may differ from a plain program's by a relative error of at most 0.0065.
Values may be sent and summed in bfloat16 or wider, within the bound.
No kernel may reach another device: no remote copies, remote signals or barrier semaphores. Data moves between devices by JAX's collectives and lax.ppermute only.
A program may use at most 64 MiB of HBM per device.

v0:
```python
import math

import jax
import jax.numpy as jnp
from jax import lax
from jax.sharding import PartitionSpec as P

TILE = 512
TS = 128
CORE = 384
GRID_W = 8
ORI_DEV = 8


def shifted(block, axis, distance):
    devices = range(lax.axis_size(axis))
    route = [(i - distance, i) for i in devices if i - distance in devices]
    return lax.ppermute(block, axis, route)


def merged(array, axis, combine):
    everything = jax.tree.map(lambda part: lax.all_gather(part, axis), array)
    leading = jax.tree.map(lambda part: part[0], everything)

    def lap(k, so_far):
        return combine(so_far, jax.tree.map(lambda part: part[k], everything))

    return lax.fori_loop(1, lax.axis_size(axis), lap, leading)


def fourier_tables():
    steps_index = jnp.arange(TILE, dtype=jnp.int32)
    product = steps_index[:, None] * steps_index[None, :] % TILE
    angle = product.astype(jnp.float32) * (2.0 * math.pi / TILE)
    return (jnp.cos(angle).astype(jnp.bfloat16), jnp.sin(angle).astype(jnp.bfloat16))


def spectrum(pixels, row_cos, row_sin, col_cos, col_sin):
    first_real = jnp.dot(pixels, col_cos, preferred_element_type=jnp.float32)
    first_imaginary = -jnp.dot(pixels, col_sin, preferred_element_type=jnp.float32)
    stacked = jnp.concatenate([first_real, first_imaginary], 0).astype(jnp.bfloat16)
    left_real = jnp.concatenate([row_cos, row_sin], 1)
    left_imaginary = jnp.concatenate([-row_sin, row_cos], 1)
    out_real = jnp.dot(left_real, stacked, preferred_element_type=jnp.float32).astype(jnp.bfloat16)
    out_imaginary = jnp.dot(left_imaginary, stacked, preferred_element_type=jnp.float32).astype(
        jnp.bfloat16
    )
    return (out_real, out_imaginary)


def normalize(flat_pixels):
    values = flat_pixels.astype(jnp.float32)
    centered = values - jnp.mean(values)
    spread = jnp.sqrt(jnp.mean(centered * centered) + 1e-06)
    return (centered / (spread * TS)).astype(jnp.bfloat16).reshape(TS, TS)


def cross_spectrum(image_real, image_imaginary, piece_real, piece_imaginary):
    a_real = image_real.astype(jnp.float32)
    a_imaginary = image_imaginary.astype(jnp.float32)
    b_real = piece_real.astype(jnp.float32)
    b_imaginary = piece_imaginary.astype(jnp.float32)
    cross_real = (a_real * b_real + a_imaginary * b_imaginary).astype(jnp.bfloat16)
    cross_imaginary = (a_imaginary * b_real - a_real * b_imaginary).astype(jnp.bfloat16)
    return (cross_real, cross_imaginary)


def larger_pair(first_pair, second_pair):
    return (jnp.maximum(first_pair[0], second_pair[0]), first_pair[1] + second_pair[1])


def shards(micrograph, template_stack, orient_list):
    cosine, sine_table = fourier_tables()
    core_block = micrograph[0]
    below = shifted(micrograph[:, :TS, :], "tile", -GRID_W)
    extended = jnp.concatenate([core_block, below[0]], 0)
    beside = shifted(extended[:, :TS], "tile", -1)
    interior = lax.axis_index("tile") % GRID_W != GRID_W - 1
    beside = jnp.where(interior, beside, jnp.zeros_like(beside))
    padded = jnp.concatenate([extended, beside], 1)
    image_real, image_imaginary = spectrum(padded, cosine, sine_table, cosine, sine_table)
    group_index = lax.axis_index("orient")
    quarter = CORE // lax.axis_size("orient")
    total_orients = orient_list.shape[0]
    inverse_right = jnp.concatenate([cosine[:, :CORE], -sine_table[:, :CORE]], 0)
    my_orients = lax.dynamic_slice_in_dim(orient_list, group_index * ORI_DEV, ORI_DEV)
    selected = jnp.take(template_stack, my_orients, axis=0)
    whole_pixels = lax.all_gather(selected, "tile", axis=1, tiled=True)
    shapes = lax.map(normalize, whole_pixels)

    def full_spectrum(shaped):
        return spectrum(
            shaped, cosine[:, :TS], sine_table[:, :TS], cosine[:TS, :], sine_table[:TS, :]
        )

    template_real, template_imaginary = lax.map(full_spectrum, shapes)
    cross_real, cross_imaginary = cross_spectrum(
        image_real, image_imaginary, template_real, template_imaginary
    )
    stacked = jnp.concatenate([cross_real, cross_imaginary], 1)
    left_real = jnp.concatenate([cosine[:CORE], -sine_table[:CORE]], 1)
    left_imaginary = jnp.concatenate([sine_table[:CORE], cosine[:CORE]], 1)
    inner_real = jnp.einsum(
        "ck,okx->ocx", left_real, stacked, preferred_element_type=jnp.float32
    ).astype(jnp.bfloat16)
    inner_imaginary = jnp.einsum(
        "ck,okx->ocx", left_imaginary, stacked, preferred_element_type=jnp.float32
    ).astype(jnp.bfloat16)
    joined = jnp.concatenate([inner_real, inner_imaginary], 2)
    corr = jnp.einsum("ock,kx->ocx", joined, inverse_right, preferred_element_type=jnp.float32) * (
        1.0 / (TILE * TILE)
    )
    highest = jnp.max(corr, 0)
    running = jnp.sum(corr, 0)
    highest, running = merged((highest, running), "orient", larger_pair)
    highest = lax.dynamic_slice_in_dim(highest, group_index * quarter, quarter, 0)
    running = lax.dynamic_slice_in_dim(running, group_index * quarter, quarter, 0)
    excess = highest - running / total_orients
    return (highest[None], excess[None])


def solution(mesh):
    placed = (P("tile", None, None), P(None, "tile"), P())
    return jax.shard_map(
        shards,
        mesh=mesh,
        in_specs=placed,
        out_specs=(P("tile", "orient", None), P("tile", "orient", None)),
        check_vma=False,
    )
```

profile of v0, /device:TPU:1, one launch (start us, length us, event | category | flops | bytes accessed | tf_op | source)
XLA Modules:
  0.0 368.0 jit_solution(1768310286467690235)
XLA Ops:
  8.2 1.3 collective-permute-start
  9.5 4.3 %sine_convert_fusion = (bf16[512,512]{1,0:T(8,128)(2,1)S(1)}, bf16[512,512]{1,0:T(8,128)(2,1)S(1)}) fusion(), kind=kLoop, calls=%fused_computation.67 | loop fusion | flops 4194304 | bytes 1048576 | tf_op jit(solution)/shard_map/convert_element_type | solution.py:35
  15.2 160.3 %all_gather.15 = bf16[8,16384]{1,0:T(8,128)(2,1)S(1)} all-gather(bf16[8,256]{1,0:T(8,128)(2,1)S(1)} %broadcast_select_fusion.1), channel_id=1, replica_groups=mesh['tile'=64,'orient'=4] {'tile'}, dimensions={1}, use_global_device_ids=true | all-gather | bytes 266240 | tf_op jit(solution)/shard_map/all_gather | solution.py:88
  175.5 26.8 %while.41 = (s32[]{:T(128)}, bf16[8,128,128]{2,1,0:T(8,128)(2,1)S(1)}, bf16[8,16384]{1,0:T(8,128)(2,1)S(1)}, s32[]{:T(128)}, f32[]{:T(128)}, /*index=5*/f32[]{:T(128)}, f32[]{:T(128)}) while((s32[]{:T(128)}, bf16[8,128,128]{2,1,0:T(8,128)(2,1)S(1)}, bf16[8,16384]{1,0:T(8,128)(2,1)S(1)}, s32[]{:T(128)}, f32[]{:T(128)}, /*index=5*/f32[]{:T(128)}, ...), condition=%wide.region_3.4_spmd, body=%wide.region_0.3_spmd.sunk | while | flops 163844 | bytes 196785 | solution.py:89
  202.5 21.4 %while.42 = (s32[]{:T(128)}, bf16[8,512,512]{1,2,0:T(8,128)(2,1)}, bf16[8,512,512]{1,2,0:T(8,128)(2,1)}, bf16[8,128,128]{2,1,0:T(8,128)(2,1)S(1)}, bf16[512,512]...) while((s32[]{:T(128)}, bf16[8,512,512]{1,2,0:T(8,128)(2,1)}, ...), condition=%wide.region_5.6_spmd, body=%wide.region_4.5_spmd.sunk | while | flops 303759360 | bytes 2687093 | solution.py:96
  202.8 1.2 fusion.80
  204.0 1.1 fusion.81
  205.5 1.2 fusion.80
  206.7 1.1 fusion.81
  208.2 1.2 fusion.80
  209.3 1.2 fusion.81
  210.9 1.2 fusion.80
  213.5 1.2 fusion.80
  214.7 1.2 fusion.81
  216.2 1.2 fusion.80
  218.9 1.2 fusion.80
  221.6 1.2 fusion.80
  222.7 1.2 fusion.81
  224.9 1.3 collective-permute-start.1
  228.6 4.0 %fusion.46 = bf16[512,512]{1,0:T(8,128)(2,1)S(1)} fusion(), kind=kLoop, calls=%fused_computation.82 | loop fusion | flops 4718592 | bytes 524288 | tf_op jit(solution)/shard_map/neg | solution.py:43
  232.6 4.2 %fusion.25 = bf16[512,512]{1,0:T(8,128)(2,1)S(1)} fusion(bf16[512,128]{1,0:T(8,128)(2,1)S(1)} %broadcast_select_fusion, bf16[128,384]{1,0:T(8,128)(2,1)S(1)} %bitcast.70, bf16[384,384]{1,0:T(8,128)(2,1)S(1)} %bitcast.67), kind=kOutput, calls=%fused_computation.51 | convolution fusion | flops 274464768 | bytes 1048576 | tf_op jit(solution)/shard_map/dot_general | solution.py:40
  236.8 4.2 %convolution_convert_fusion.3 = bf16[512,512]{1,0:T(8,128)(2,1)S(1)} fusion(bf16[512,128]{1,0:T(8,128)(2,1)S(1)} %broadcast_select_fusion, bf16[128,384]{1,0:T(8,128)(2,1)S(1)} %bitcast.71, bf16[384,384]{1,0:T(8,128)(2,1)S(1)} %bitcast.68), kind=kOutput, calls=%fused_computation.52 | convolution fusion | flops 274202624 | bytes 1048576 | tf_op jit(solution)/shard_map/dot_general | solution.py:39
  243.1 4.8 %fusion.16 = (bf16[8,512,512]{1,2,0:T(8,128)(2,1)S(1)}, bf16[8,512,512]{1,2,0:T(8,128)(2,1)S(1)}) fusion(bf16[8,512,512]{1,2,0:T(8,128)(2,1)} %get-tuple-element.237, bf16[8,512,512]{1,2,0:T(8,128)(2,1)} %get-tuple-element.238, f32[512,512]{0,1:T(8,128)S(1)} %copy.6, f32[512,512]{0,1:T(8,128)S(1)} %copy.5), kind=kLoop, calls=%fused_computation.33 | loop fusion | flops 20971520 | bytes 18874368 | tf_op jit(solution)/shard_map/convert_element_type | solution.py:63
  248.0 4.0 %convert_bitcast_fusion = bf16[8,384,512]{2,1,0:T(8,128)(2,1)S(1)} fusion(bf16[8,512,512]{1,2,0:T(8,128)(2,1)S(1)} %get-tuple-element.280, bf16[8,512,512]{1,2,0:T(8,128)(2,1)S(1)} %get-tuple-element.279, bf16[384,512]{1,0:T(8,128)(2,1)S(1)} %copy-done.4, bf16[384,512]{1,0:T(8,128)(2,1)S(1)} %copy-done.6), kind=kOutput, calls=%fused_computation.45 | convolution fusion | flops 3241148416 | bytes 12320768 | tf_op jit(solution)/shard_map/ck,okx->ocx/dot_general | solution.py:106
  252.0 3.7 %convert_bitcast_fusion.1 = bf16[8,384,512]{2,1,0:T(8,128)(2,1)S(1)} fusion(bf16[8,512,512]{1,2,0:T(8,128)(2,1)S(1)} %get-tuple-element.280, bf16[8,512,512]{1,2,0:T(8,128)(2,1)S(1)} %get-tuple-element.279, bf16[384,512]{1,0:T(8,128)(2,1)S(1)} %copy-done.5, bf16[384,512]{1,0:T(8,128)(2,1)S(1)} %copy-done.4), kind=kOutput, calls=%fused_computation.46 | convolution fusion | flops 3241148416 | bytes 12320768 | tf_op jit(solution)/shard_map/ck,okx->ocx/dot_general | solution.py:103
  255.8 4.9 %multiply_reduce_fusion.1 = (f32[384,384]{1,0:T(8,128)}, f32[384,384]{1,0:T(8,128)}) fusion(bf16[512,384]{1,0:T(8,128)(2,1)S(1)} %copy-done.2, bf16[512,384]{1,0:T(8,128)(2,1)S(1)} %copy-done.3, bf16[8,384,512]{2,1,0:T(8,128)(2,1)S(1)} %convert_bitcast_fusion, bf16[8,384,512]{2,1,0:T(8,128)(2,1)S(1)} %convert_bitcast_fusion.1), kind=kOutput, calls=%fused_computation.43 | convolution fusion | flops 2433318912 | bytes 8257536 | tf_op jit(solution)/shard_map/ock,kx->ocx/dot_general | solution.py:110
  261.4 56.6 %all-gather.5.cloned.1.call-done = f32[1536,384]{1,0:T(8,128)} async-done(((f32[384,384]{1,0:T(8,128)}), f32[1536,384]{1,0:T(8,128)}) %all-gather.5.cloned.1.call-update) | async-done | bytes 2359312 | tf_op jit(solution)/shard_map/all_gather | solution.py:22
  319.2 35.5 %all-gather.7.cloned.1.call-done = f32[1536,384]{1,0:T(8,128)} async-done(((f32[384,384]{1,0:T(8,128)}), f32[1536,384]{1,0:T(8,128)}) %all-gather.7.cloned.1.call-update) | async-done | bytes 2359312 | tf_op jit(solution)/shard_map/all_gather | solution.py:22
  355.7 4.7 %while.43 = (s32[]{:T(128)}, f32[384,384]{1,0:T(8,128)S(1)}, f32[384,384]{1,0:T(8,128)S(1)}, f32[4,384,384]{2,1,0:T(8,128)}, f32[4,384,384]{2,1,0:T(8,128)}, /*index=5*/s32[]{:T(128)}, s32[]{:T(128)}, s32[]{:T(128)}) while((s32[]{:T(128)}, f32[384,384]{1,0:T(8,128)S(1)}, f32[384,384]{1,0:T(8,128)S(1)}, f32[4,384,384]{2,1,0:T(8,128)}, ...), condition=%wide.region_9.10_spmd, body=%wide.region_8.9_spmd.sunk | while | flops 294917 | bytes 3539075 | solution.py:28
  355.7 1.6 bitcast_add_fusion.2
  357.3 1.6 bitcast_add_fusion.2
  358.9 1.6 bitcast_add_fusion.2
  (95 shorter events, 32.9 us)
Async XLA Ops:
  7.2 7.4 %copy-start = (bf16[256,256]{1,0:T(8,128)(2,1)S(1)}, bf16[256,256]{1,0:T(8,128)(2,1)}, u32[]{:S(2)}) copy-start(bf16[256,256]{1,0:T(8,128)(2,1)} %param.10) | copy-start | bytes 393220
  7.2 310.9 %all-gather.5.cloned.1.call-start = ((), (), s32[]{:S(2)}) async-start(), calls=%async_computation | async-start | bytes 2949120 | tf_op jit(solution)/shard_map/all_gather | solution.py:22
  8.2 216.7 %collective-permute-start = (bf16[1,128,384]{2,1,0:T(8,128)(2,1)S(1)}, bf16[1,128,384]{2,1,0:T(8,128)(2,1)S(1)}, u32[]{:S(2)}, u32[]{:S(2)}) collective-permute-start(bf16[1,128,384]{2,1,0:T(8,128)(2,1)S(1)} %slice.54), channel_id=1, source_target_pairs={{32,0},{36,4},{40,8},{44,12},{48,16},{52,20},{56,24},{60,28},{64,3... | collective-permute-start | bytes 294920 | tf_op jit(solution)/shard_map/ppermute | solution.py:18
  202.5 22.4 %copy-start.1 = (bf16[1,384,384]{2,1,0:T(8,128)(2,1)S(1)}, bf16[1,384,384]{2,1,0:T(8,128)(2,1)}, u32[]{:S(2)}) copy-start(bf16[1,384,384]{2,1,0:T(8,128)(2,1)} %param.9) | copy-start | bytes 884740
  224.9 7.7 %collective-permute-start.1 = (bf16[512,128]{1,0:T(8,128)(2,1)S(1)}, bf16[512,128]{1,0:T(8,128)(2,1)S(1)}, u32[]{:S(2)}, u32[]{:S(2)}) collective-permute-start(bf16[512,128]{1,0:T(8,128)(2,1)S(1)} %pad_maximum_fusion.18), channel_id=1, source_target_pairs={{4,0},{8,4},{12,8},{16,12},{20,16},{24,20},{28,24},{32,28},{36,32}... | collective-permute-start | bytes 393224 | tf_op jit(solution)/shard_map/ppermute | solution.py:18
  243.1 4.9 %copy-start.4 = (bf16[384,512]{1,0:T(8,128)(2,1)S(1)}, bf16[384,512]{1,0:T(8,128)(2,1)}, u32[]{:S(2)}) copy-start(bf16[384,512]{1,0:T(8,128)(2,1)} %slice.70) | copy-start | bytes 1179652
  243.1 4.9 %copy-start.6 = (bf16[384,512]{1,0:T(8,128)(2,1)S(1)}, bf16[384,512]{1,0:T(8,128)(2,1)}, u32[]{:S(2)}) copy-start(bf16[384,512]{1,0:T(8,128)(2,1)} %get-tuple-element.284) | copy-start | bytes 1179652
  248.0 4.0 %copy-start.5 = (bf16[384,512]{1,0:T(8,128)(2,1)S(1)}, bf16[384,512]{1,0:T(8,128)(2,1)}, u32[]{:S(2)}) copy-start(bf16[384,512]{1,0:T(8,128)(2,1)} %get-tuple-element.283) | copy-start | bytes 1179652
  252.0 3.8 %copy-start.2 = (bf16[512,384]{1,0:T(8,128)(2,1)S(1)}, bf16[512,384]{1,0:T(8,128)(2,1)}, u32[]{:S(2)}) copy-start(bf16[512,384]{1,0:T(8,128)(2,1)} %slice_negate_fusion) | copy-start | bytes 1179652
  252.0 3.8 %copy-start.3 = (bf16[512,384]{1,0:T(8,128)(2,1)S(1)}, bf16[512,384]{1,0:T(8,128)(2,1)}, u32[]{:S(2)}) copy-start(bf16[512,384]{1,0:T(8,128)(2,1)} %slice.72) | copy-start | bytes 1179652
  260.7 94.0 %all-gather.7.cloned.1.call-start = ((), (), s32[]{:S(2)}) async-start(), calls=%async_computation.1 | async-start | bytes 2949120 | tf_op jit(solution)/shard_map/all_gather | solution.py:22
Sparse Core Ops, SparseCore 0:
  260.8 57.2 all-gather.4
  319.9 34.7 all-gather.6
where the time goes:
time: 369 us; the launch traced here: 368 us
  blocking collectives  160 us (43%)
  waiting for transfers between devices  92.8 us (25%)
  matrix products  43.7 us (12%)
  other arithmetic  36.3 us (10%)
  between operations  14.3 us (4%)
  loops' own time  11.8 us (3%)
  local copies, waits for them, and re-layouts  6.13 us (2%)
    all_gather x1, blocking collectives, shards(): whole_pixels = lax.all_gather(selected, 'tile', axis=1, tiled=True)  160 us
    all_gather x2, waiting for transfers between devices, merged(): everything = jax.tree.map(lambda part: lax.all_gather(part, axis), array)  92.1 us
    another operation x1, loops' own time, shards(): shapes = lax.map(normalize, whole_pixels)  11.6 us
    dot_general x9, matrix products, spectrum(): jnp.dot(left_real, stacked, preferred_element_type=jnp.float32)  10 us
    dot_general x9, matrix products, spectrum(): jnp.dot(left_imaginary, stacked, preferred_element_type=jnp.float32)  9.99 us
  transfers between devices with their start and end apart: 4, of which 2 were waited for; matrix products, arithmetic and copies ran while one was open for 14% of the time, Pallas kernels for 0%

commit v1 on v0

v1 whole, which is shorter than its diff:
```python
import functools
import math

import jax
import jax.numpy as jnp
import numpy as np
from jax import lax
from jax.experimental import pallas as pl
from jax.experimental.pallas import tpu as pltpu
from jax.sharding import PartitionSpec as P

TILE = 512
TS = 128
CORE = 384
GRID_W = 8
TILES = 64
ORI_DEV = 8
MEMBERS = 4
ROWS = 96
ROWS_IN = 224
LENGTH = 256
PAIRS = LENGTH // 2
HALF = TILE // 2
ORDER = (2, 3, 1, 0)


def bf16(table):
    return np.asarray(table, np.float64).astype(jnp.bfloat16)


def column_table():
    n = np.arange(TILE)[:, None]
    k = np.arange(HALF)[None, :]
    angle = (math.pi / TILE) * ((n * (2 * k + 1)) % (2 * TILE))
    return bf16(np.concatenate([np.cos(angle), -np.sin(angle)], 1))


def row_table(rows):
    j = np.arange(PAIRS)[:, None]
    m = np.arange(rows)[None, :]
    angle = (math.pi / LENGTH) * ((m * (2 * j + 1)) % (2 * LENGTH))
    c, s = np.cos(angle), np.sin(angle)
    return bf16(np.block([[c, s], [-s, c], [c, -s], [s, c]]))


def inverse_row_table():
    j = np.arange(PAIRS)[None, :]
    c = np.arange(ROWS)[:, None]
    angle = (math.pi / LENGTH) * ((c * (2 * j + 1)) % (2 * LENGTH))
    return bf16(np.concatenate([np.cos(angle), np.sin(angle)], 1))


def inverse_column_table():
    k = np.arange(HALF)[:, None]
    c = np.arange(CORE)[None, :]
    angle = (math.pi / TILE) * ((c * (2 * k + 1)) % (2 * TILE))
    scale = 2.0 / (LENGTH * TILE)
    return bf16(np.concatenate([np.cos(angle), -np.sin(angle)], 0) * scale)


def dot(a, b):
    return jnp.dot(a, b, preferred_element_type=jnp.float32)


def select_kernel(ids_ref, stack_ref, out_ref):
    row = lax.broadcasted_iota(jnp.int32, (2 * ORI_DEV, 256), 0)
    lane = lax.broadcasted_iota(jnp.int32, (2 * ORI_DEV, 256), 1)
    wanted = jnp.zeros((2 * ORI_DEV, 256), jnp.int32)
    for o in range(ORI_DEV):
        wanted = jnp.where(row % ORI_DEV == o, ids_ref[o], wanted)
    hot = jnp.where(lane == wanted, 1.0, 0.0).astype(jnp.bfloat16)
    picked = dot(hot, stack_ref[...])
    both = jnp.concatenate([picked[:ORI_DEV, :TS], picked[ORI_DEV:, TS:]], 0).astype(jnp.bfloat16)
    out_ref[...] = jnp.broadcast_to(both[None], out_ref.shape)


def image_kernel(member_ref, own_ref, right_ref, below_ref, corner_ref, col_ref, row_ref, out_ref, g_ref):
    def columns(first, second, start, count):
        g = dot(first, col_ref[:CORE]) + dot(second, col_ref[CORE:])
        g_ref[0, start : start + count] = g[:, :HALF].astype(jnp.bfloat16)
        g_ref[1, start : start + count] = g[:, HALF:].astype(jnp.bfloat16)

    columns(own_ref[...], right_ref[...], 0, CORE)
    columns(below_ref[...], corner_ref[...], CORE, TS)
    for s, bits in enumerate(ORDER):
        start = pl.multiple_of((member_ref[0] ^ bits) * ROWS, 32)
        piece = jnp.concatenate([g_ref[0, pl.ds(start, ROWS_IN)], g_ref[1, pl.ds(start, ROWS_IN)]], 0)
        out_ref[s] = dot(row_ref[...], piece).astype(jnp.bfloat16)


def template_kernel(pixels_ref, col_ref, row_ref, out_ref, shape_ref):
    values = pixels_ref[...].astype(jnp.float32).reshape(TS, ORI_DEV, TS)
    mean = jnp.sum(jnp.sum(values, 0), 1, keepdims=True) / (TS * TS)
    centered = values - mean[None]
    square = jnp.sum(jnp.sum(centered * centered, 0), 1, keepdims=True) / (TS * TS)
    spread = jnp.sqrt(square + 1e-06) * TS
    shape_ref[...] = (centered / spread[None]).reshape(TS * ORI_DEV, TS)
    for o in range(ORI_DEV):
        shape = shape_ref[pl.ds(o, TS, stride=ORI_DEV), :].astype(jnp.bfloat16)
        g = dot(shape, col_ref[...]).astype(jnp.bfloat16)
        g = jnp.concatenate([g[:, :HALF], g[:, HALF:]], 0)
        out_ref[o] = dot(row_ref[...], g).astype(jnp.bfloat16)


def block_kernel(image_ref, template_ref, inv_row_ref, inv_col_ref, high_ref, sum_ref, inner_ref):
    def part(ref, p):
        return ref[0, p * PAIRS : (p + 1) * PAIRS].astype(jnp.float32)

    for o in range(ORI_DEV):
        tr = template_ref.at[o : o + 1]

        def cross(p):
            a, b = part(image_ref, 2 * p), part(image_ref, 2 * p + 1)
            c, d = part(tr, 2 * p), part(tr, 2 * p + 1)
            return a * c + b * d, b * c - a * d

        plus_re, plus_im = cross(0)
        minus_re, minus_im = cross(1)
        mixed = jnp.concatenate(
            [
                jnp.concatenate([plus_re + minus_re, plus_im + minus_im], 1),
                jnp.concatenate([minus_im - plus_im, plus_re - minus_re], 1),
            ],
            0,
        ).astype(jnp.bfloat16)
        inner_ref[o * ROWS : (o + 1) * ROWS] = dot(inv_row_ref[...], mixed).astype(jnp.bfloat16)
    corr = dot(inner_ref[...], inv_col_ref[...]).reshape(ORI_DEV, ROWS, CORE)
    high_ref[...] = jnp.max(corr, 0).astype(high_ref.dtype)
    sum_ref[...] = jnp.sum(corr, 0).astype(sum_ref.dtype)


VMEM = pl.BlockSpec(memory_space=pltpu.VMEM)
SMEM = pl.BlockSpec(memory_space=pltpu.SMEM)
LIMIT = 40 * 1024 * 1024


def call(kernel, outs, specs, scratch=(), flops=0):
    return pl.pallas_call(
        kernel,
        out_shape=outs,
        in_specs=specs,
        out_specs=jax.tree.map(lambda _: VMEM, outs),
        scratch_shapes=list(scratch),
        compiler_params=pltpu.CompilerParams(vmem_limit_bytes=LIMIT),
        cost_estimate=pl.CostEstimate(flops=flops, bytes_accessed=2**21, transcendentals=0),
    )


def shape_of(dims, dtype=jnp.bfloat16):
    return jax.ShapeDtypeStruct(dims, dtype)


def halo(block, distance):
    route = []
    for t in range(TILES):
        column = t % GRID_W + distance % GRID_W
        source = t + distance
        if column < GRID_W and source < TILES:
            route.append((source, t))
    return lax.ppermute(block, "tile", route)


def shards(micrograph, template_stack, orient_list):
    member = lax.axis_index("orient")
    ids = lax.dynamic_slice_in_dim(orient_list, member * ORI_DEV, ORI_DEV)
    spread = call(select_kernel, shape_of((TILES, 2 * ORI_DEV, TS)), [SMEM, VMEM])(ids, template_stack)
    pixels = lax.all_to_all(spread, "tile", 0, 0)
    own = micrograph[0]
    right = halo(own[:, :TS], 1)
    below = halo(own[:TS], GRID_W)
    corner = halo(own[:TS, :TS], GRID_W + 1)
    columns = column_table()
    image = call(
        image_kernel,
        shape_of((MEMBERS, 4 * PAIRS, HALF)),
        [SMEM] + [VMEM] * 6,
        [pltpu.VMEM((2, TILE, HALF), jnp.bfloat16)],
        flops=1600000000,
    )(member[None], own, right, below, corner, columns, row_table(ROWS_IN))
    templates = call(
        template_kernel,
        shape_of((ORI_DEV, 4 * PAIRS, HALF)),
        [VMEM] * 3,
        [pltpu.VMEM((TS * ORI_DEV, TS), jnp.float32)],
        flops=1000000000,
    )(pixels, columns[:TS], row_table(TS))
    inverse_rows, inverse_columns = inverse_row_table(), inverse_column_table()
    highs, sums = [], []
    for s, bits in enumerate(ORDER):
        kind = jnp.bfloat16 if bits else jnp.float32
        high, total = call(
            block_kernel,
            (shape_of((ROWS, CORE), kind), shape_of((ROWS, CORE), kind)),
            [VMEM] * 4,
            [pltpu.VMEM((ORI_DEV * ROWS, TILE), jnp.bfloat16)],
            flops=1000000000,
        )(image[s : s + 1], templates, inverse_rows, inverse_columns)
        if bits:
            route = [(i, i ^ bits) for i in range(MEMBERS)]
            high, total = lax.ppermute((high, total), "orient", route)
        highs.append(high.astype(jnp.float32))
        sums.append(total.astype(jnp.float32))
    peak = functools.reduce(jnp.maximum, highs)
    excess = peak - functools.reduce(jnp.add, sums) / (MEMBERS * ORI_DEV)
    return (peak[None], excess[None])


def solution(mesh):
    placed = (P("tile", None, None), P(None, "tile"), P())
    return jax.shard_map(
        shards,
        mesh=mesh,
        in_specs=placed,
        out_specs=(P("tile", "orient", None), P("tile", "orient", None)),
        check_vma=False,
    )
```

time: 369 us -> 57.6 us (0.16)
  the two profiles are of different devices: /device:TPU:1 before, /device:TPU:120 now
where the time goes in v1:
time: 57.6 us; the launch traced here: 57.1 us
  starting transfers between devices  27.5 us (48%)
  Pallas kernels  11.6 us (20%)
  waiting for transfers between devices  9 us (16%)
  local copies, waits for them, and re-layouts  7.34 us (13%)
  between operations  0.83 us (1%)
  other arithmetic  0.79 us (1%)
    all_to_all x1, starting transfers between devices, shards(): pixels = lax.all_to_all(spread, 'tile', 0, 0)  13.1 us
    ppermute x3, starting transfers between devices, halo(): return lax.ppermute(block, 'tile', route)  10 us
    pallas_call x4, Pallas kernels, shards(): call(block_kernel, (shape_of((ROWS, CORE), kind), shape_of((ROWS, CORE),...  7 us
    ppermute x3, waiting for transfers between devices, halo(): return lax.ppermute(block, 'tile', route)  6.97 us
    ppermute x6, starting transfers between devices, shards(): high, total = lax.ppermute((high, total), 'orient', route)  4.47 us
    unnamed x16, local copies, waits for them, and re-layouts  3.97 us
    ppermute x6, waiting for transfers between devices, shards(): high, total = lax.ppermute((high, total), 'orient', route)  2.03 us
    pallas_call x1, Pallas kernels, shards(): call(template_kernel, shape_of((ORI_DEV, 4 * PAIRS, HALF)), [VMEM] * 3, [...  1.94 us
  transfers between devices with their start and end apart: 10, of which 3 were waited for; matrix products, arithmetic and copies ran while one was open for 5% of the time, Pallas kernels for 8%

profile of v1, /device:TPU:120, one launch (start us, length us, event | category | flops | bytes accessed | tf_op | source)
XLA Modules:
  0.0 57.1 jit_solution(5089512182319349667)
XLA Ops:
  0.6 0.7 %dynamic_slice.3.ids_ref = s32[8]{0:T(128)S(1)} dynamic-slice(s32[32]{0:T(128)} %param.11, s32[]{:T(128)S(6)} %select_n.3), dynamic_slice_sizes={8} | dynamic-slice | bytes 68 | tf_op jit(solution)/shard_map/dynamic_slice | solution.py:165
  1.4 0.9 %copy-done.1 = bf16[256,256]{1,0:T(8,128)(2,1)S(1)} copy-done((bf16[256,256]{1,0:T(8,128)(2,1)S(1)}, bf16[256,256]{1,0:T(8,128)(2,1)}, u32[]{:S(2)}) %copy-start.1) | copy-done | bytes 131096
  2.3 1.4 %shard_map.105 = bf16[64,16,128]{2,1,0:T(8,128)(2,1)} custom-call(s32[8]{0:T(128)S(1)} %dynamic_slice.3.ids_ref, bf16[256,256]{1,0:T(8,128)(2,1)S(1)} %copy-done.1), custom_call_target="tpu_custom_call" | custom-call | bytes 2097152 | tf_op jit(solution)/shard_map/pallas_call | solution.py:166
  3.7 13.1 %all-to-all-start = ((bf16[64,16,128]{2,1,0:T(8,128)(2,1)}), bf16[64,16,128]{2,1,0:T(8,128)(2,1)S(1)}, u32[]{:S(2)}, u32[]{:S(2)}) async-start(bf16[64,16,128]{2,1,0:T(8,128)(2,1)} %shard_map.105), calls=%async_computation | async-start | bytes 524288 | tf_op jit(solution)/shard_map/all_to_all | solution.py:167
  16.8 0.9 %slice_bitcast_fusion = bf16[128,384]{1,0:T(8,128)(2,1)S(1)} fusion(bf16[1,384,384]{2,1,0:T(8,128)(2,1)} %param.9), kind=kLoop, calls=%fused_computation.2 | loop fusion | bytes 196608 | tf_op jit(solution)/shard_map/slice | solution.py:170
  17.7 2.4 %collective-permute-start.1 = (bf16[128,384]{1,0:T(8,128)(2,1)S(1)}, bf16[128,384]{1,0:T(8,128)(2,1)S(1)}, u32[]{:S(2)}, u32[]{:S(2)}) collective-permute-start(bf16[128,384]{1,0:T(8,128)(2,1)S(1)} %slice_bitcast_fusion), channel_id=1, source_target_pairs={{32,0},{36,4},{40,8},{44,12},{48,16},{52,20},{56,24},{60,28},{64,3... | collective-permute-start | bytes 294920 | tf_op jit(solution)/shard_map/ppermute | solution.py:160
  20.1 0.9 %slice.32 = bf16[384,128]{1,0:T(8,128)(2,1)S(1)} slice(bf16[384,384]{1,0:T(8,128)(2,1)} %bitcast.8), slice={[0:384], [0:128]} | slice | bytes 196608 | tf_op jit(solution)/shard_map/slice | solution.py:169
  21.0 5.1 %collective-permute-start = (bf16[384,128]{1,0:T(8,128)(2,1)S(1)}, bf16[384,128]{1,0:T(8,128)(2,1)S(1)}, u32[]{:S(2)}, u32[]{:S(2)}) collective-permute-start(bf16[384,128]{1,0:T(8,128)(2,1)S(1)} %slice.32), channel_id=1, source_target_pairs={{4,0},{8,4},{12,8},{16,12},{20,16},{24,20},{28,24},{36,32},{40,36}... | collective-permute-start | bytes 294920 | tf_op jit(solution)/shard_map/ppermute | solution.py:160
  26.1 0.8 %slice.33 = bf16[128,128]{1,0:T(8,128)(2,1)S(1)} slice(bf16[384,384]{1,0:T(8,128)(2,1)} %bitcast.9), slice={[0:128], [0:128]} | slice | bytes 65536 | tf_op jit(solution)/shard_map/slice | solution.py:171
  26.9 2.4 %collective-permute-start.2 = (bf16[128,128]{1,0:T(8,128)(2,1)S(1)}, bf16[128,128]{1,0:T(8,128)(2,1)S(1)}, u32[]{:S(2)}, u32[]{:S(2)}) collective-permute-start(bf16[128,128]{1,0:T(8,128)(2,1)S(1)} %slice.33), channel_id=1, source_target_pairs={{36,0},{40,4},{44,8},{48,12},{52,16},{56,20},{60,24},{68,32},{72,3... | collective-permute-start | bytes 98312 | tf_op jit(solution)/shard_map/ppermute | solution.py:160
  29.4 7.0 %collective-permute-done.2.corner_ref = bf16[128,128]{1,0:T(8,128)(2,1)S(1)} collective-permute-done((bf16[128,128]{1,0:T(8,128)(2,1)S(1)}, bf16[128,128]{1,0:T(8,128)(2,1)S(1)}, u32[]{:S(2)}, u32[]{:S(2)}) %collective-permute-start.2) | collective-permute-done | bytes 32800 | tf_op jit(solution)/shard_map/ppermute | solution.py:160
  36.3 1.0 %copy-done = bf16[1,384,384]{2,1,0:T(8,128)(2,1)S(1)} copy-done((bf16[1,384,384]{2,1,0:T(8,128)(2,1)S(1)}, bf16[1,384,384]{2,1,0:T(8,128)(2,1)}, u32[]{:S(2)}) %copy-start) | copy-done | bytes 294936
  37.3 1.0 %copy-done.2 = bf16[512,448]{1,0:T(8,128)(2,1)S(1)} copy-done((bf16[512,448]{1,0:T(8,128)(2,1)S(1)}, bf16[512,448]{1,0:T(8,128)(2,1)}, u32[]{:S(2)}) %copy-start.2) | copy-done | bytes 458776
  38.3 1.0 %copy-done.3 = bf16[512,512]{1,0:T(8,128)(2,1)S(1)} copy-done((bf16[512,512]{1,0:T(8,128)(2,1)S(1)}, bf16[512,512]{1,0:T(8,128)(2,1)}, u32[]{:S(2)}) %copy-start.3) | copy-done | bytes 524312
  39.4 1.3 %shard_map.104 = bf16[4,512,256]{2,1,0:T(8,128)(2,1)S(1)} custom-call(s32[1]{0:T(128)} %bitcast.member_ref, bf16[384,384]{1,0:T(8,128)(2,1)S(1)} %bitcast.10, bf16[384,128]{1,0:T(8,128)(2,1)S(1)} %collective-permute-done.right_ref, bf16[128,384]{1,0:T(8,128)(2,1)S(1)} %collective-permute-done.1.below_ref, ...), custom_call_target="tpu_custom_call" | custom-call | flops 1600000000 | bytes 2097152 | tf_op jit(solution)/shard_map/pallas_call | solution.py:173
  40.7 0.1 fusion.1
  40.7 0.0 copy-start.4
  40.7 0.0 copy-start.7
  40.8 1.9 %shard_map.106.template_ref = bf16[8,512,256]{2,1,0:T(8,128)(2,1)S(1)} custom-call(bf16[64,16,128]{2,1,0:T(8,128)(2,1)S(1)} %all-to-all-done.pixels_ref, bf16[128,512]{1,0:T(8,128)(2,1)S(1)} %copy-done.6, bf16[512,256]{1,0:T(8,128)(2,1)S(1)} %copy-done.5), custom_call_target="tpu_custom_call" | custom-call | flops 1000000000 | bytes 2097152 | tf_op jit(solution)/shard_map/pallas_call | solution.py:180
  42.7 1.8 %shard_map.109 = (bf16[96,384]{1,0:T(8,128)(2,1)S(1)}, bf16[96,384]{1,0:T(8,128)(2,1)S(1)}) custom-call(bf16[1,512,256]{2,1,0:T(8,128)(2,1)S(1)} %get-tuple-element.20.image_ref, bf16[8,512,256]{2,1,0:T(8,128)(2,1)S(1)} %shard_map.106.template_ref, bf16[96,256]{1,0:T(8,128)(2,1)S(1)} %copy-done.7, bf16[512,384]{1,0:T(8,128)(2,1)S(1)} %copy-done.4), custom_call_target="tpu_custom_call" | custom-call | flops 1000000000 | bytes 2097152 | tf_op jit(solution)/shard_map/pallas_call | solution.py:191
  44.5 1.8 %shard_map.108 = (bf16[96,384]{1,0:T(8,128)(2,1)S(1)}, bf16[96,384]{1,0:T(8,128)(2,1)S(1)}) custom-call(bf16[1,512,256]{2,1,0:T(8,128)(2,1)S(1)} %get-tuple-element.21.image_ref, bf16[8,512,256]{2,1,0:T(8,128)(2,1)S(1)} %shard_map.106.template_ref, bf16[96,256]{1,0:T(8,128)(2,1)S(1)} %copy-done.7, bf16[512,384]{1,0:T(8,128)(2,1)S(1)} %copy-done.4), custom_call_target="tpu_custom_call" | custom-call | flops 1000000000 | bytes 2097152 | tf_op jit(solution)/shard_map/pallas_call | solution.py:191
  46.3 0.1 collective-permute-start.5
  46.4 0.5 collective-permute-start.8
  46.9 0.3 collective-permute-start.4
  47.2 1.5 %collective-permute-start.7 = (bf16[96,384]{1,0:T(8,128)(2,1)S(1)}, bf16[96,384]{1,0:T(8,128)(2,1)S(1)}, u32[]{:S(2)}, u32[]{:S(2)}) collective-permute-start(bf16[96,384]{1,0:T(8,128)(2,1)S(1)} %get-tuple-element.15), channel_id=1, source_target_pairs={{0,3},{1,2},{2,1},{3,0},{4,7},{5,6},{6,5},{7,4},{8,11},{9,10},{10,... | collective-permute-start | bytes 221192 | tf_op jit(solution)/shard_map/ppermute | solution.py:200
  48.6 1.7 %shard_map.107 = (bf16[96,384]{1,0:T(8,128)(2,1)S(1)}, bf16[96,384]{1,0:T(8,128)(2,1)S(1)}) custom-call(bf16[1,512,256]{2,1,0:T(8,128)(2,1)S(1)} %get-tuple-element.18.image_ref, bf16[8,512,256]{2,1,0:T(8,128)(2,1)S(1)} %shard_map.106.template_ref, bf16[96,256]{1,0:T(8,128)(2,1)S(1)} %copy-done.7, bf16[512,384]{1,0:T(8,128)(2,1)S(1)} %copy-done.4), custom_call_target="tpu_custom_call" | custom-call | flops 1000000000 | bytes 2097152 | tf_op jit(solution)/shard_map/pallas_call | solution.py:191
  50.4 0.7 %collective-permute-start.3 = (bf16[96,384]{1,0:T(8,128)(2,1)S(1)}, bf16[96,384]{1,0:T(8,128)(2,1)S(1)}, u32[]{:S(2)}, u32[]{:S(2)}) collective-permute-start(bf16[96,384]{1,0:T(8,128)(2,1)S(1)} %get-tuple-element.10), channel_id=1, source_target_pairs={{0,2},{1,3},{2,0},{3,1},{4,6},{5,7},{6,4},{7,5},{8,10},{9,11},{10,... | collective-permute-start | bytes 221192 | tf_op jit(solution)/shard_map/ppermute | solution.py:200
  51.1 1.4 %collective-permute-start.6 = (bf16[96,384]{1,0:T(8,128)(2,1)S(1)}, bf16[96,384]{1,0:T(8,128)(2,1)S(1)}, u32[]{:S(2)}, u32[]{:S(2)}) collective-permute-start(bf16[96,384]{1,0:T(8,128)(2,1)S(1)} %get-tuple-element.14), channel_id=1, source_target_pairs={{0,2},{1,3},{2,0},{3,1},{4,6},{5,7},{6,4},{7,5},{8,10},{9,11},{10,... | collective-permute-start | bytes 221192 | tf_op jit(solution)/shard_map/ppermute | solution.py:200
  52.5 1.7 %shard_map.110 = (f32[96,384]{1,0:T(8,128)S(1)}, f32[96,384]{1,0:T(8,128)S(1)}) custom-call(bf16[1,512,256]{2,1,0:T(8,128)(2,1)S(1)} %get-tuple-element.19.image_ref, bf16[8,512,256]{2,1,0:T(8,128)(2,1)S(1)} %shard_map.106.template_ref, bf16[96,256]{1,0:T(8,128)(2,1)S(1)} %copy-done.7, bf16[512,384]{1,0:T(8,128)(2,1)S(1)} %copy-done.4), custom_call_target="tpu_custom_call" | custom-call | flops 1000000000 | bytes 2097152 | tf_op jit(solution)/shard_map/pallas_call | solution.py:191
  54.3 1.2 %collective-permute-done.3 = bf16[96,384]{1,0:T(8,128)(2,1)S(1)} collective-permute-done((bf16[96,384]{1,0:T(8,128)(2,1)S(1)}, bf16[96,384]{1,0:T(8,128)(2,1)S(1)}, u32[]{:S(2)}, u32[]{:S(2)}) %collective-permute-start.3) | collective-permute-done | bytes 73760 | tf_op jit(solution)/shard_map/ppermute | solution.py:200
  55.5 0.8 %collective-permute-done.6 = bf16[96,384]{1,0:T(8,128)(2,1)S(1)} collective-permute-done((bf16[96,384]{1,0:T(8,128)(2,1)S(1)}, bf16[96,384]{1,0:T(8,128)(2,1)S(1)}, u32[]{:S(2)}, u32[]{:S(2)}) %collective-permute-start.6) | collective-permute-done | bytes 73760 | tf_op jit(solution)/shard_map/ppermute | solution.py:200
  56.3 0.8 %subtract_bitcast_fusion = (f32[1,96,384]{2,1,0:T(8,128)}, f32[1,96,384]{2,1,0:T(8,128)}) fusion(f32[96,384]{1,0:T(8,128)S(1)} %get-tuple-element.17, bf16[96,384]{1,0:T(8,128)(2,1)S(1)} %collective-permute-done.8, bf16[96,384]{1,0:T(8,128)(2,1)S(1)} %collective-permute-done.7, bf16[96,384]{1,0:T(8,128)(2,1)S(1)} %collective-permute-done.6, ...), kind=kLoop, calls=%fused_computation | loop fusion | flops 516096 | bytes 1032192 | tf_op jit(solution)/shard_map/broadcast_in_dim | solution.py:205
  (17 shorter events, 0.0 us)
Async XLA Ops:
  1.4 0.9 %copy-start.1 = (bf16[256,256]{1,0:T(8,128)(2,1)S(1)}, bf16[256,256]{1,0:T(8,128)(2,1)}, u32[]{:S(2)}) copy-start(bf16[256,256]{1,0:T(8,128)(2,1)} %stack_ref.1) | copy-start | bytes 393220
  3.7 37.1 %all-to-all-start = ((bf16[64,16,128]{2,1,0:T(8,128)(2,1)}), bf16[64,16,128]{2,1,0:T(8,128)(2,1)S(1)}, u32[]{:S(2)}, u32[]{:S(2)}) async-start(bf16[64,16,128]{2,1,0:T(8,128)(2,1)} %shard_map.105), calls=%async_computation | async-start | bytes 524288 | tf_op jit(solution)/shard_map/all_to_all | solution.py:167
  17.7 18.7 %collective-permute-start.1 = (bf16[128,384]{1,0:T(8,128)(2,1)S(1)}, bf16[128,384]{1,0:T(8,128)(2,1)S(1)}, u32[]{:S(2)}, u32[]{:S(2)}) collective-permute-start(bf16[128,384]{1,0:T(8,128)(2,1)S(1)} %slice_bitcast_fusion), channel_id=1, source_target_pairs={{32,0},{36,4},{40,8},{44,12},{48,16},{52,20},{56,24},{60,28},{64,3... | collective-permute-start | bytes 294920 | tf_op jit(solution)/shard_map/ppermute | solution.py:160
  21.0 15.3 %collective-permute-start = (bf16[384,128]{1,0:T(8,128)(2,1)S(1)}, bf16[384,128]{1,0:T(8,128)(2,1)S(1)}, u32[]{:S(2)}, u32[]{:S(2)}) collective-permute-start(bf16[384,128]{1,0:T(8,128)(2,1)S(1)} %slice.32), channel_id=1, source_target_pairs={{4,0},{8,4},{12,8},{16,12},{20,16},{24,20},{28,24},{36,32},{40,36}... | collective-permute-start | bytes 294920 | tf_op jit(solution)/shard_map/ppermute | solution.py:160
  26.9 9.4 %collective-permute-start.2 = (bf16[128,128]{1,0:T(8,128)(2,1)S(1)}, bf16[128,128]{1,0:T(8,128)(2,1)S(1)}, u32[]{:S(2)}, u32[]{:S(2)}) collective-permute-start(bf16[128,128]{1,0:T(8,128)(2,1)S(1)} %slice.33), channel_id=1, source_target_pairs={{36,0},{40,4},{44,8},{48,12},{52,16},{56,20},{60,24},{68,32},{72,3... | collective-permute-start | bytes 98312 | tf_op jit(solution)/shard_map/ppermute | solution.py:160
  36.3 1.0 %copy-start = (bf16[1,384,384]{2,1,0:T(8,128)(2,1)S(1)}, bf16[1,384,384]{2,1,0:T(8,128)(2,1)}, u32[]{:S(2)}) copy-start(bf16[1,384,384]{2,1,0:T(8,128)(2,1)} %param.9) | copy-start | bytes 884740
  37.3 1.0 %copy-start.2 = (bf16[512,448]{1,0:T(8,128)(2,1)S(1)}, bf16[512,448]{1,0:T(8,128)(2,1)}, u32[]{:S(2)}) copy-start(bf16[512,448]{1,0:T(8,128)(2,1)} %constant.26.clone.row_ref) | copy-start | bytes 1376260
  38.3 1.0 %copy-start.3 = (bf16[512,512]{1,0:T(8,128)(2,1)S(1)}, bf16[512,512]{1,0:T(8,128)(2,1)}, u32[]{:S(2)}) copy-start(bf16[512,512]{1,0:T(8,128)(2,1)} %constant.25.clone.col_ref) | copy-start | bytes 1572868
  39.4 1.4 %copy-start.5 = (bf16[512,256]{1,0:T(8,128)(2,1)S(1)}, bf16[512,256]{1,0:T(8,128)(2,1)}, u32[]{:S(2)}) copy-start(bf16[512,256]{1,0:T(8,128)(2,1)} %constant.28.clone.row_ref) | copy-start | bytes 786436
  39.4 1.4 %copy-start.6 = (bf16[128,512]{1,0:T(8,128)(2,1)S(1)}, bf16[128,512]{1,0:T(8,128)(2,1)}, u32[]{:S(2)}) copy-start(bf16[128,512]{1,0:T(8,128)(2,1)} %constant.27.clone.col_ref) | copy-start | bytes 393220
  40.7 2.0 %copy-start.4 = (bf16[512,384]{1,0:T(8,128)(2,1)S(1)}, bf16[512,384]{1,0:T(8,128)(2,1)}, u32[]{:S(2)}) copy-start(bf16[512,384]{1,0:T(8,128)(2,1)} %constant.30.clone.inv_col_ref) | copy-start | bytes 1179652
  40.7 2.0 %copy-start.7 = (bf16[96,256]{1,0:T(8,128)(2,1)S(1)}, bf16[96,256]{1,0:T(8,128)(2,1)}, u32[]{:S(2)}) copy-start(bf16[96,256]{1,0:T(8,128)(2,1)} %constant.29.clone.inv_row_ref) | copy-start | bytes 147460
  46.3 4.8 %collective-permute-start.5 = (bf16[96,384]{1,0:T(8,128)(2,1)S(1)}, bf16[96,384]{1,0:T(8,128)(2,1)S(1)}, u32[]{:S(2)}, u32[]{:S(2)}) collective-permute-start(bf16[96,384]{1,0:T(8,128)(2,1)S(1)} %get-tuple-element.12), channel_id=1, source_target_pairs={{0,1},{1,0},{2,3},{3,2},{4,5},{5,4},{6,7},{7,6},{8,9},{9,8},{10,11... | collective-permute-start | bytes 221192 | tf_op jit(solution)/shard_map/ppermute | solution.py:200
  46.4 7.9 %collective-permute-start.8 = (bf16[96,384]{1,0:T(8,128)(2,1)S(1)}, bf16[96,384]{1,0:T(8,128)(2,1)S(1)}, u32[]{:S(2)}, u32[]{:S(2)}) collective-permute-start(bf16[96,384]{1,0:T(8,128)(2,1)S(1)} %get-tuple-element.16), channel_id=1, source_target_pairs={{0,1},{1,0},{2,3},{3,2},{4,5},{5,4},{6,7},{7,6},{8,9},{9,8},{10,11... | collective-permute-start | bytes 221192 | tf_op jit(solution)/shard_map/ppermute | solution.py:200
  46.9 7.4 %collective-permute-start.4 = (bf16[96,384]{1,0:T(8,128)(2,1)S(1)}, bf16[96,384]{1,0:T(8,128)(2,1)S(1)}, u32[]{:S(2)}, u32[]{:S(2)}) collective-permute-start(bf16[96,384]{1,0:T(8,128)(2,1)S(1)} %get-tuple-element.11), channel_id=1, source_target_pairs={{0,3},{1,2},{2,1},{3,0},{4,7},{5,6},{6,5},{7,4},{8,11},{9,10},{10,... | collective-permute-start | bytes 221192 | tf_op jit(solution)/shard_map/ppermute | solution.py:200
  47.2 7.1 %collective-permute-start.7 = (bf16[96,384]{1,0:T(8,128)(2,1)S(1)}, bf16[96,384]{1,0:T(8,128)(2,1)S(1)}, u32[]{:S(2)}, u32[]{:S(2)}) collective-permute-start(bf16[96,384]{1,0:T(8,128)(2,1)S(1)} %get-tuple-element.15), channel_id=1, source_target_pairs={{0,3},{1,2},{2,1},{3,0},{4,7},{5,6},{6,5},{7,4},{8,11},{9,10},{10,... | collective-permute-start | bytes 221192 | tf_op jit(solution)/shard_map/ppermute | solution.py:200
  50.4 5.1 %collective-permute-start.3 = (bf16[96,384]{1,0:T(8,128)(2,1)S(1)}, bf16[96,384]{1,0:T(8,128)(2,1)S(1)}, u32[]{:S(2)}, u32[]{:S(2)}) collective-permute-start(bf16[96,384]{1,0:T(8,128)(2,1)S(1)} %get-tuple-element.10), channel_id=1, source_target_pairs={{0,2},{1,3},{2,0},{3,1},{4,6},{5,7},{6,4},{7,5},{8,10},{9,11},{10,... | collective-permute-start | bytes 221192 | tf_op jit(solution)/shard_map/ppermute | solution.py:200
  51.1 5.2 %collective-permute-start.6 = (bf16[96,384]{1,0:T(8,128)(2,1)S(1)}, bf16[96,384]{1,0:T(8,128)(2,1)S(1)}, u32[]{:S(2)}, u32[]{:S(2)}) collective-permute-start(bf16[96,384]{1,0:T(8,128)(2,1)S(1)} %get-tuple-element.14), channel_id=1, source_target_pairs={{0,2},{1,3},{2,0},{3,1},{4,6},{5,7},{6,4},{7,5},{8,10},{9,11},{10,... | collective-permute-start | bytes 221192 | tf_op jit(solution)/shard_map/ppermute | solution.py:200

commit v2 on v1

v2 whole, which is shorter than its diff:
```python
import math

import jax
import jax.numpy as jnp
import numpy as np
from jax import lax
from jax.experimental import pallas as pl
from jax.experimental.pallas import tpu as pltpu
from jax.sharding import PartitionSpec as P

TILE = 512
TS = 128
CORE = 384
GRID_W = 8
TILES = 64
ORI_DEV = 8
MEMBERS = 4
ROWS = 96
ROWS_IN = 224
LENGTH = 256
PAIRS = LENGTH // 2
HALF = TILE // 2
ORDER = (2, 3, 1, 0)


def bf16(table):
    return np.asarray(table, np.float64).astype(jnp.bfloat16)


def column_table():
    n = np.arange(TILE)[:, None]
    k = np.arange(HALF)[None, :]
    angle = (math.pi / TILE) * ((n * (2 * k + 1)) % (2 * TILE))
    return bf16(np.concatenate([np.cos(angle), -np.sin(angle)], 1))


def row_table(rows):
    j = np.arange(PAIRS)[:, None]
    m = np.arange(rows)[None, :]
    angle = (math.pi / LENGTH) * ((m * (2 * j + 1)) % (2 * LENGTH))
    c, s = np.cos(angle), np.sin(angle)
    return bf16(np.block([[c, s], [-s, c], [c, -s], [s, c]]))


def inverse_row_table():
    j = np.arange(PAIRS)[None, :]
    c = np.arange(ROWS)[:, None]
    angle = (math.pi / LENGTH) * ((c * (2 * j + 1)) % (2 * LENGTH))
    return bf16(np.concatenate([np.cos(angle), np.sin(angle)], 1))


def inverse_column_table():
    k = np.arange(HALF)[:, None]
    c = np.arange(CORE)[None, :]
    angle = (math.pi / TILE) * ((c * (2 * k + 1)) % (2 * TILE))
    scale = 2.0 / (LENGTH * TILE)
    return bf16(np.concatenate([np.cos(angle), -np.sin(angle)], 0) * scale)


def dot(a, b):
    return jnp.dot(a, b, preferred_element_type=jnp.float32)


def prepare_kernel(ids_ref, micro_ref, stack_ref, out_ref, right_ref, below_ref, corner_ref, sems):
    own = micro_ref.at[0]
    copies = [
        pltpu.make_async_copy(own.at[:, :TS], right_ref, sems.at[0]),
        pltpu.make_async_copy(own.at[:TS, :], below_ref, sems.at[1]),
        pltpu.make_async_copy(own.at[:TS, :TS], corner_ref, sems.at[2]),
    ]
    for copy in copies:
        copy.start()
    row = lax.broadcasted_iota(jnp.int32, (2 * ORI_DEV, 256), 0)
    lane = lax.broadcasted_iota(jnp.int32, (2 * ORI_DEV, 256), 1)
    wanted = jnp.zeros((2 * ORI_DEV, 256), jnp.int32)
    first = lax.axis_index("orient") * ORI_DEV
    for o in range(ORI_DEV):
        wanted = jnp.where(row % ORI_DEV == o, ids_ref[first + o], wanted)
    hot = jnp.where(lane == wanted, 1.0, 0.0).astype(jnp.bfloat16)
    picked = dot(hot, stack_ref[...])
    both = jnp.concatenate([picked[:ORI_DEV, :TS], picked[ORI_DEV:, TS:]], 0).astype(jnp.bfloat16)
    out_ref[...] = jnp.broadcast_to(both[None], out_ref.shape)
    for copy in copies:
        copy.wait()


def image_kernel(member_ref, own_ref, right_ref, below_ref, corner_ref, col_ref, row_ref, *rest):
    *out_refs, g_ref = rest

    def columns(first, second, start, count):
        g = dot(first, col_ref[:CORE]) + dot(second, col_ref[CORE:])
        g_ref[0, start : start + count] = g[:, :HALF].astype(jnp.bfloat16)
        g_ref[1, start : start + count] = g[:, HALF:].astype(jnp.bfloat16)

    columns(own_ref[...], right_ref[...], 0, CORE)
    columns(below_ref[...], corner_ref[...], CORE, TS)
    for s, bits in enumerate(ORDER):
        start = pl.multiple_of((member_ref[0] ^ bits) * ROWS, 32)
        piece = jnp.concatenate([g_ref[0, pl.ds(start, ROWS_IN)], g_ref[1, pl.ds(start, ROWS_IN)]], 0)
        out_refs[s][...] = dot(row_ref[...], piece).astype(jnp.bfloat16)


def template_kernel(pixels_ref, col_ref, row_ref, out_ref, shape_ref):
    values = pixels_ref[...].astype(jnp.float32).reshape(TS, ORI_DEV, TS)
    mean = jnp.sum(jnp.sum(values, 0), 1, keepdims=True) / (TS * TS)
    centered = values - mean[None]
    square = jnp.sum(jnp.sum(centered * centered, 0), 1, keepdims=True) / (TS * TS)
    spread = jnp.sqrt(square + 1e-06) * TS
    shape_ref[...] = (centered / spread[None]).reshape(TS * ORI_DEV, TS)
    for o in range(ORI_DEV):
        shape = shape_ref[pl.ds(o, TS, stride=ORI_DEV), :].astype(jnp.bfloat16)
        g = dot(shape, col_ref[...]).astype(jnp.bfloat16)
        g = jnp.concatenate([g[:, :HALF], g[:, HALF:]], 0)
        out_ref[o] = dot(row_ref[...], g).astype(jnp.bfloat16)


def block(image_ref, template_ref, inv_row_ref, inv_col_ref, out_ref, inner_ref):
    def part(ref, p):
        return ref[p * PAIRS : (p + 1) * PAIRS]

    for o in range(ORI_DEV):

        def cross(p):
            a, b = part(image_ref, 2 * p), part(image_ref, 2 * p + 1)
            c, d = part(template_ref.at[o], 2 * p), part(template_ref.at[o], 2 * p + 1)
            return a * c + b * d, b * c - a * d

        plus_re, plus_im = cross(0)
        minus_re, minus_im = cross(1)
        mixed = jnp.concatenate(
            [
                jnp.concatenate([plus_re + minus_re, plus_im + minus_im], 1),
                jnp.concatenate([minus_im - plus_im, plus_re - minus_re], 1),
            ],
            0,
        )
        inner_ref[o * ROWS : (o + 1) * ROWS] = dot(inv_row_ref[...], mixed).astype(jnp.bfloat16)
    corr = dot(inner_ref[...], inv_col_ref[...]).reshape(ORI_DEV, ROWS, CORE)
    out_ref[0] = jnp.max(corr, 0).astype(out_ref.dtype)
    out_ref[1] = jnp.sum(corr, 0).astype(out_ref.dtype)


def pair_kernel(first_ref, second_ref, template_ref, inv_row_ref, inv_col_ref, out_a, out_b, inner_a, inner_b):
    block(first_ref, template_ref, inv_row_ref, inv_col_ref, out_a, inner_a)
    block(second_ref, template_ref, inv_row_ref, inv_col_ref, out_b, inner_b)


def finish_kernel(own_ref, a_ref, b_ref, c_ref, peak_ref, excess_ref):
    others = [ref[...].astype(jnp.float32) for ref in (a_ref, b_ref, c_ref)]
    peak, total = own_ref[0], own_ref[1]
    for other in others:
        peak = jnp.maximum(peak, other[0])
        total = total + other[1]
    peak_ref[0] = peak
    excess_ref[0] = peak - total / (MEMBERS * ORI_DEV)


VMEM = pl.BlockSpec(memory_space=pltpu.VMEM)
SMEM = pl.BlockSpec(memory_space=pltpu.SMEM)
ANY = pl.BlockSpec(memory_space=pl.ANY)
LIMIT = 24 * 1024 * 1024
WHOLE = 60 * 1024 * 1024


def call(kernel, outs, specs, scratch=(), flops=0, out_specs=None, limit=LIMIT, moved=2**21):
    return pl.pallas_call(
        kernel,
        out_shape=outs,
        in_specs=specs,
        out_specs=out_specs or jax.tree.map(lambda _: VMEM, outs),
        scratch_shapes=list(scratch),
        compiler_params=pltpu.CompilerParams(vmem_limit_bytes=limit),
        cost_estimate=pl.CostEstimate(flops=flops, bytes_accessed=moved, transcendentals=0),
    )


def shape_of(dims, dtype=jnp.bfloat16):
    return jax.ShapeDtypeStruct(dims, dtype)


def halo(block, distance):
    route = []
    crosses = distance % GRID_W
    for t in range(TILES):
        source = t + distance
        if t % GRID_W + crosses < GRID_W and source < TILES:
            for o in range(MEMBERS):
                route.append((source * MEMBERS + (o ^ 2 if crosses else o), t * MEMBERS + o))
    return lax.ppermute(block, ("tile", "orient"), route)


def shards(micrograph, template_stack, orient_list):
    spread, right, below, corner = call(
        prepare_kernel,
        (
            shape_of((TILES, 2 * ORI_DEV, TS)),
            shape_of((CORE, TS)),
            shape_of((TS, CORE)),
            shape_of((TS, TS)),
        ),
        [SMEM, ANY, VMEM],
        [pltpu.SemaphoreType.DMA((3,))],
        out_specs=(VMEM, ANY, ANY, ANY),
        limit=WHOLE,
    )(orient_list, micrograph, template_stack)
    right = halo(right, 1)
    below = halo(below, GRID_W)
    corner = halo(corner, GRID_W + 1)
    pixels = lax.all_to_all(spread, "tile", 0, 0)
    columns = column_table()
    image = call(
        image_kernel,
        (shape_of((4 * PAIRS, HALF)),) * MEMBERS,
        [SMEM] + [VMEM] * 6,
        [pltpu.VMEM((2, TILE, HALF), jnp.bfloat16)],
        flops=20000000000,
    )(lax.axis_index("orient")[None], micrograph[0], right, below, corner, columns, row_table(ROWS_IN))
    templates = call(
        template_kernel,
        shape_of((ORI_DEV, 4 * PAIRS, HALF)),
        [VMEM] * 3,
        [pltpu.VMEM((TS * ORI_DEV, TS), jnp.float32)],
        flops=1000000000,
    )(pixels, columns[:TS], row_table(TS))
    inverse_rows, inverse_columns = inverse_row_table(), inverse_column_table()
    inner = pltpu.VMEM((ORI_DEV * ROWS, TILE), jnp.bfloat16)

    def pair(first, second, kind):
        return call(
            pair_kernel,
            (shape_of((2, ROWS, CORE)), shape_of((2, ROWS, CORE), kind)),
            [VMEM] * 5,
            [inner, inner],
            flops=2000000000,
        )(image[first], image[second], templates, inverse_rows, inverse_columns)

    def sent(piece, bits):
        return lax.ppermute(piece, "orient", [(i, i ^ bits) for i in range(MEMBERS)])

    far = pair(0, 1, jnp.bfloat16)
    near = pair(2, 3, jnp.float32)
    others = [sent(far[0], ORDER[0]), sent(far[1], ORDER[1]), sent(near[0], ORDER[2])]
    out = shape_of((1, ROWS, CORE), jnp.float32)
    return call(finish_kernel, (out, out), [VMEM] * 4)(near[1], *others)


def solution(mesh):
    placed = (P("tile", None, None), P(None, "tile"), P())
    return jax.shard_map(
        shards,
        mesh=mesh,
        in_specs=placed,
        out_specs=(P("tile", "orient", None), P("tile", "orient", None)),
        check_vma=False,
    )
```

time: 57.6 us -> 61.5 us (1.068)
  the two profiles are of different devices: /device:TPU:120 before, /device:TPU:1 now
where the time goes in v2:
time: 61.5 us; the launch traced here: 61.2 us
  starting transfers between devices  28.2 us (46%)
  Pallas kernels  17.6 us (29%)
  waiting for transfers between devices  11.5 us (19%)
  local copies, waits for them, and re-layouts  3.06 us (5%)
  between operations  0.78 us (1%)
    all_to_all x1, starting transfers between devices, shards(): pixels = lax.all_to_all(spread, 'tile', 0, 0)  18.7 us
    pallas_call x1, Pallas kernels, shards(): call(prepare_kernel, (shape_of((TILES, 2 * ORI_DEV, TS)), shape_of((CORE,...  9.7 us
    all_to_all x1, waiting for transfers between devices, shards(): pixels = lax.all_to_all(spread, 'tile', 0, 0)  7.74 us
    ppermute x3, starting transfers between devices, sent(): lax.ppermute(piece, 'orient', [(i, i ^ bits) for i in range(MEMBERS)])  5.62 us
    pallas_call x2, Pallas kernels, pair(): call(pair_kernel, (shape_of((2, ROWS, CORE)), shape_of((2, ROWS, CORE), k...  4.01 us
    ppermute x3, starting transfers between devices, halo(): return lax.ppermute(block, ('tile', 'orient'), route)  3.88 us
    ppermute x3, waiting for transfers between devices, sent(): lax.ppermute(piece, 'orient', [(i, i ^ bits) for i in range(MEMBERS)])  3.71 us
    unnamed x14, local copies, waits for them, and re-layouts  3.06 us
  transfers between devices with their start and end apart: 7, of which 2 were waited for; matrix products, arithmetic and copies ran while one was open for 0% of the time, Pallas kernels for 5%

profile of v2, /device:TPU:1, one launch (start us, length us, event | category | flops | bytes accessed | tf_op | source)
XLA Modules:
  0.0 61.2 jit_solution(11885143370896647908)
XLA Ops:
  0.6 9.7 %shard_map.104 = (bf16[64,16,128]{2,1,0:T(8,128)(2,1)}, bf16[384,128]{1,0:T(8,128)(2,1)}, bf16[128,384]{1,0:T(8,128)(2,1)}, bf16[128,128]{1,0:T(8,128)(2,1)}) custom-call(s32[32]{0:T(128)} %ids_ref.1, bf16[1,384,384]{2,1,0:T(8,128)(2,1)} %micro_ref.1, bf16[256,256]{1,0:T(8,128)(2,1)} %stack_ref.1), custom_call_target="tpu_custom_call" | custom-call | bytes 2097152 | tf_op jit(solution)/shard_map/pallas_call | solution.py:193
  10.3 1.3 %collective-permute-start = (bf16[384,128]{1,0:T(8,128)(2,1)}, bf16[384,128]{1,0:T(8,128)(2,1)S(1)}, u32[]{:S(2)}, u32[]{:S(2)}) collective-permute-start(bf16[384,128]{1,0:T(8,128)(2,1)} %get-tuple-element.14), channel_id=1, source_target_pairs={{6,0},{7,1},{4,2},{5,3},{10,4},{11,5},{8,6},{9,7},{14,8},{15,9},{1... | collective-permute-start | bytes 294920 | tf_op jit(solution)/shard_map/ppermute | solution.py:189
  11.6 1.3 %collective-permute-start.1 = (bf16[128,384]{1,0:T(8,128)(2,1)}, bf16[128,384]{1,0:T(8,128)(2,1)S(1)}, u32[]{:S(2)}, u32[]{:S(2)}) collective-permute-start(bf16[128,384]{1,0:T(8,128)(2,1)} %get-tuple-element.15), channel_id=1, source_target_pairs={{32,0},{33,1},{34,2},{35,3},{36,4},{37,5},{38,6},{39,7},{40,8},{41... | collective-permute-start | bytes 294920 | tf_op jit(solution)/shard_map/ppermute | solution.py:189
  12.9 1.3 %collective-permute-start.2 = (bf16[128,128]{1,0:T(8,128)(2,1)}, bf16[128,128]{1,0:T(8,128)(2,1)S(1)}, u32[]{:S(2)}, u32[]{:S(2)}) collective-permute-start(bf16[128,128]{1,0:T(8,128)(2,1)} %get-tuple-element.16), channel_id=1, source_target_pairs={{38,0},{39,1},{36,2},{37,3},{42,4},{43,5},{40,6},{41,7},{46,8},{47... | collective-permute-start | bytes 98312 | tf_op jit(solution)/shard_map/ppermute | solution.py:189
  14.2 18.7 %all-to-all-start = ((bf16[64,16,128]{2,1,0:T(8,128)(2,1)}), bf16[64,16,128]{2,1,0:T(8,128)(2,1)S(1)}, u32[]{:S(2)}, u32[]{:S(2)}) async-start(bf16[64,16,128]{2,1,0:T(8,128)(2,1)} %get-tuple-element.19), calls=%async_computation | async-start | bytes 524288 | tf_op jit(solution)/shard_map/all_to_all | solution.py:209
  33.0 0.0 collective-permute-done.2.corner_ref
  33.0 0.0 collective-permute-done.right_ref
  33.0 0.0 collective-permute-done.1.below_ref
  33.0 0.0 copy-start
  33.0 1.0 %copy-done = bf16[1,384,384]{2,1,0:T(8,128)(2,1)S(1)} copy-done((bf16[1,384,384]{2,1,0:T(8,128)(2,1)S(1)}, bf16[1,384,384]{2,1,0:T(8,128)(2,1)}, u32[]{:S(2)}) %copy-start) | copy-done | bytes 294936
  34.0 0.0 copy-start.1
  34.0 1.0 %copy-done.1 = bf16[512,448]{1,0:T(8,128)(2,1)S(1)} copy-done((bf16[512,448]{1,0:T(8,128)(2,1)S(1)}, bf16[512,448]{1,0:T(8,128)(2,1)}, u32[]{:S(2)}) %copy-start.1) | copy-done | bytes 458776
  35.0 0.0 copy-start.2
  35.0 1.0 %copy-done.2 = bf16[512,512]{1,0:T(8,128)(2,1)S(1)} copy-done((bf16[512,512]{1,0:T(8,128)(2,1)S(1)}, bf16[512,512]{1,0:T(8,128)(2,1)}, u32[]{:S(2)}) %copy-start.2) | copy-done | bytes 524312
  36.1 1.3 %shard_map.105 = (bf16[512,256]{1,0:T(8,128)(2,1)S(1)}, bf16[512,256]{1,0:T(8,128)(2,1)S(1)}, bf16[512,256]{1,0:T(8,128)(2,1)S(1)}, bf16[512,256]{1,0:T(8,128)(2,1)S(1)}) custom-call(s32[1]{0:T(128)} %bitcast.member_ref, bf16[384,384]{1,0:T(8,128)(2,1)S(1)} %bitcast.2, bf16[384,128]{1,0:T(8,128)(2,1)S(1)} %collective-permute-done.right_ref, ...), custom_call_target="tpu_custom_call" | custom-call | flops 20000000000 | bytes 2097152 | tf_op jit(solution)/shard_map/pallas_call | solution.py:211
  37.3 0.0 copy-start.3
  37.3 0.0 copy-start.6
  37.3 7.7 %all-to-all-done.pixels_ref = bf16[64,16,128]{2,1,0:T(8,128)(2,1)S(1)} async-done(((bf16[64,16,128]{2,1,0:T(8,128)(2,1)}), bf16[64,16,128]{2,1,0:T(8,128)(2,1)S(1)}, u32[]{:S(2)}, u32[]{:S(2)}) %all-to-all-start) | async-done | bytes 262176 | tf_op jit(solution)/shard_map/all_to_all | solution.py:209
  45.1 0.0 copy-done.4
  45.1 0.0 copy-done.5
  45.1 1.9 %shard_map.106.template_ref = bf16[8,512,256]{2,1,0:T(8,128)(2,1)S(1)} custom-call(bf16[64,16,128]{2,1,0:T(8,128)(2,1)S(1)} %all-to-all-done.pixels_ref, bf16[128,512]{1,0:T(8,128)(2,1)S(1)} %copy-done.5, bf16[512,256]{1,0:T(8,128)(2,1)S(1)} %copy-done.4), custom_call_target="tpu_custom_call" | custom-call | flops 1000000000 | bytes 2097152 | tf_op jit(solution)/shard_map/pallas_call | solution.py:218
  47.0 0.0 copy-done.3
  47.0 0.0 copy-done.6
  47.1 2.0 %shard_map.108 = (bf16[2,96,384]{2,1,0:T(8,128)(2,1)S(1)}, bf16[2,96,384]{2,1,0:T(8,128)(2,1)S(1)}) custom-call(bf16[512,256]{1,0:T(8,128)(2,1)S(1)} %get-tuple-element.21.first_ref, bf16[512,256]{1,0:T(8,128)(2,1)S(1)} %get-tuple-element.22.second_ref, bf16[8,512,256]{2,1,0:T(8,128)(2,1)S(1)} %shard_map.106.template_ref, bf16[96,256]{1,0:T(8,128)(2,1)S(1)} %copy-done.6, ...), custom_call_target="tpu_custom_call" | custom-call | flops 2000000000 | bytes 2097152 | tf_op jit(solution)/shard_map/pallas_call | solution.py:229
  49.1 1.6 %collective-permute-start.3 = (bf16[2,96,384]{2,1,0:T(8,128)(2,1)S(1)}, bf16[2,96,384]{2,1,0:T(8,128)(2,1)S(1)}, u32[]{:S(2)}, u32[]{:S(2)}) collective-permute-start(bf16[2,96,384]{2,1,0:T(8,128)(2,1)S(1)} %get-tuple-element.23), channel_id=1, source_target_pairs={{0,2},{1,3},{2,0},{3,1},{4,6},{5,7},{6,4},{7,5},{8,10},{9,11},{10,... | collective-permute-start | bytes 442376 | tf_op jit(solution)/shard_map/ppermute | solution.py:238
  50.7 3.7 %collective-permute-start.4 = (bf16[2,96,384]{2,1,0:T(8,128)(2,1)S(1)}, bf16[2,96,384]{2,1,0:T(8,128)(2,1)S(1)}, u32[]{:S(2)}, u32[]{:S(2)}) collective-permute-start(bf16[2,96,384]{2,1,0:T(8,128)(2,1)S(1)} %get-tuple-element.24), channel_id=1, source_target_pairs={{0,3},{1,2},{2,1},{3,0},{4,7},{5,6},{6,5},{7,4},{8,11},{9,10},{10,... | collective-permute-start | bytes 442376 | tf_op jit(solution)/shard_map/ppermute | solution.py:238
  54.4 2.0 %shard_map.107 = (bf16[2,96,384]{2,1,0:T(8,128)(2,1)S(1)}, f32[2,96,384]{2,1,0:T(8,128)S(1)}) custom-call(bf16[512,256]{1,0:T(8,128)(2,1)S(1)} %get-tuple-element.17.first_ref, bf16[512,256]{1,0:T(8,128)(2,1)S(1)} %get-tuple-element.18.second_ref, bf16[8,512,256]{2,1,0:T(8,128)(2,1)S(1)} %shard_map.106.template_ref, bf16[96,256]{1,0:T(8,128)(2,1)S(1)} %copy-done.6, ...), custom_call_target="tpu_custom_call" | custom-call | flops 2000000000 | bytes 2097152 | tf_op jit(solution)/shard_map/pallas_call | solution.py:229
  56.4 0.3 collective-permute-start.5
  56.7 0.0 collective-permute-done.3.a_ref
  56.7 3.7 %collective-permute-done.4.b_ref = bf16[2,96,384]{2,1,0:T(8,128)(2,1)S(1)} collective-permute-done((bf16[2,96,384]{2,1,0:T(8,128)(2,1)S(1)}, bf16[2,96,384]{2,1,0:T(8,128)(2,1)S(1)}, u32[]{:S(2)}, u32[]{:S(2)}) %collective-permute-start.4) | collective-permute-done | bytes 147488 | tf_op jit(solution)/shard_map/ppermute | solution.py:238
  60.4 0.0 collective-permute-done.5.c_ref
  60.4 0.7 %shard_map.109 = (f32[1,96,384]{2,1,0:T(8,128)}, f32[1,96,384]{2,1,0:T(8,128)}) custom-call(f32[2,96,384]{2,1,0:T(8,128)S(1)} %get-tuple-element.20.own_ref, bf16[2,96,384]{2,1,0:T(8,128)(2,1)S(1)} %collective-permute-done.3.a_ref, bf16[2,96,384]{2,1,0:T(8,128)(2,1)S(1)} %collective-permute-done.4.b_ref, bf16[2,96,384]{2,1,0:T(8,128)(2,1)S(1)} %collective-permute-done.5.c_ref), custom_call_target="tpu_custom_call" | custom-call | bytes 2097152 | tf_op jit(solution)/shard_map/pallas_call | solution.py:244
  (2 shorter events, 0.0 us)
Async XLA Ops:
  10.3 22.6 %collective-permute-start = (bf16[384,128]{1,0:T(8,128)(2,1)}, bf16[384,128]{1,0:T(8,128)(2,1)S(1)}, u32[]{:S(2)}, u32[]{:S(2)}) collective-permute-start(bf16[384,128]{1,0:T(8,128)(2,1)} %get-tuple-element.14), channel_id=1, source_target_pairs={{6,0},{7,1},{4,2},{5,3},{10,4},{11,5},{8,6},{9,7},{14,8},{15,9},{1... | collective-permute-start | bytes 294920 | tf_op jit(solution)/shard_map/ppermute | solution.py:189
  11.6 21.4 %collective-permute-start.1 = (bf16[128,384]{1,0:T(8,128)(2,1)}, bf16[128,384]{1,0:T(8,128)(2,1)S(1)}, u32[]{:S(2)}, u32[]{:S(2)}) collective-permute-start(bf16[128,384]{1,0:T(8,128)(2,1)} %get-tuple-element.15), channel_id=1, source_target_pairs={{32,0},{33,1},{34,2},{35,3},{36,4},{37,5},{38,6},{39,7},{40,8},{41... | collective-permute-start | bytes 294920 | tf_op jit(solution)/shard_map/ppermute | solution.py:189
  12.9 20.0 %collective-permute-start.2 = (bf16[128,128]{1,0:T(8,128)(2,1)}, bf16[128,128]{1,0:T(8,128)(2,1)S(1)}, u32[]{:S(2)}, u32[]{:S(2)}) collective-permute-start(bf16[128,128]{1,0:T(8,128)(2,1)} %get-tuple-element.16), channel_id=1, source_target_pairs={{38,0},{39,1},{36,2},{37,3},{42,4},{43,5},{40,6},{41,7},{46,8},{47... | collective-permute-start | bytes 98312 | tf_op jit(solution)/shard_map/ppermute | solution.py:189
  14.2 30.9 %all-to-all-start = ((bf16[64,16,128]{2,1,0:T(8,128)(2,1)}), bf16[64,16,128]{2,1,0:T(8,128)(2,1)S(1)}, u32[]{:S(2)}, u32[]{:S(2)}) async-start(bf16[64,16,128]{2,1,0:T(8,128)(2,1)} %get-tuple-element.19), calls=%async_computation | async-start | bytes 524288 | tf_op jit(solution)/shard_map/all_to_all | solution.py:209
  33.0 1.0 %copy-start = (bf16[1,384,384]{2,1,0:T(8,128)(2,1)S(1)}, bf16[1,384,384]{2,1,0:T(8,128)(2,1)}, u32[]{:S(2)}) copy-start(bf16[1,384,384]{2,1,0:T(8,128)(2,1)} %micro_ref.1) | copy-start | bytes 884740
  34.0 1.0 %copy-start.1 = (bf16[512,448]{1,0:T(8,128)(2,1)S(1)}, bf16[512,448]{1,0:T(8,128)(2,1)}, u32[]{:S(2)}) copy-start(bf16[512,448]{1,0:T(8,128)(2,1)} %constant.17.clone.row_ref) | copy-start | bytes 1376260
  35.0 1.0 %copy-start.2 = (bf16[512,512]{1,0:T(8,128)(2,1)S(1)}, bf16[512,512]{1,0:T(8,128)(2,1)}, u32[]{:S(2)}) copy-start(bf16[512,512]{1,0:T(8,128)(2,1)} %constant.16.clone.col_ref) | copy-start | bytes 1572868
  36.0 9.0 %copy-start.4 = (bf16[512,256]{1,0:T(8,128)(2,1)S(1)}, bf16[512,256]{1,0:T(8,128)(2,1)}, u32[]{:S(2)}) copy-start(bf16[512,256]{1,0:T(8,128)(2,1)} %constant.19.clone.row_ref) | copy-start | bytes 786436
  36.0 9.0 %copy-start.5 = (bf16[128,512]{1,0:T(8,128)(2,1)S(1)}, bf16[128,512]{1,0:T(8,128)(2,1)}, u32[]{:S(2)}) copy-start(bf16[128,512]{1,0:T(8,128)(2,1)} %constant.18.clone.col_ref) | copy-start | bytes 393220
  37.3 9.7 %copy-start.3 = (bf16[512,384]{1,0:T(8,128)(2,1)S(1)}, bf16[512,384]{1,0:T(8,128)(2,1)}, u32[]{:S(2)}) copy-start(bf16[512,384]{1,0:T(8,128)(2,1)} %constant.21.clone.inv_col_ref) | copy-start | bytes 1179652
  37.3 9.7 %copy-start.6 = (bf16[96,256]{1,0:T(8,128)(2,1)S(1)}, bf16[96,256]{1,0:T(8,128)(2,1)}, u32[]{:S(2)}) copy-start(bf16[96,256]{1,0:T(8,128)(2,1)} %constant.20.clone.inv_row_ref) | copy-start | bytes 147460
  49.1 7.6 %collective-permute-start.3 = (bf16[2,96,384]{2,1,0:T(8,128)(2,1)S(1)}, bf16[2,96,384]{2,1,0:T(8,128)(2,1)S(1)}, u32[]{:S(2)}, u32[]{:S(2)}) collective-permute-start(bf16[2,96,384]{2,1,0:T(8,128)(2,1)S(1)} %get-tuple-element.23), channel_id=1, source_target_pairs={{0,2},{1,3},{2,0},{3,1},{4,6},{5,7},{6,4},{7,5},{8,10},{9,11},{10,... | collective-permute-start | bytes 442376 | tf_op jit(solution)/shard_map/ppermute | solution.py:238
  50.7 9.7 %collective-permute-start.4 = (bf16[2,96,384]{2,1,0:T(8,128)(2,1)S(1)}, bf16[2,96,384]{2,1,0:T(8,128)(2,1)S(1)}, u32[]{:S(2)}, u32[]{:S(2)}) collective-permute-start(bf16[2,96,384]{2,1,0:T(8,128)(2,1)S(1)} %get-tuple-element.24), channel_id=1, source_target_pairs={{0,3},{1,2},{2,1},{3,0},{4,7},{5,6},{6,5},{7,4},{8,11},{9,10},{10,... | collective-permute-start | bytes 442376 | tf_op jit(solution)/shard_map/ppermute | solution.py:238
  56.4 4.0 %collective-permute-start.5 = (bf16[2,96,384]{2,1,0:T(8,128)(2,1)S(1)}, bf16[2,96,384]{2,1,0:T(8,128)(2,1)S(1)}, u32[]{:S(2)}, u32[]{:S(2)}) collective-permute-start(bf16[2,96,384]{2,1,0:T(8,128)(2,1)S(1)} %get-tuple-element.25), channel_id=1, source_target_pairs={{0,1},{1,0},{2,3},{3,2},{4,5},{5,4},{6,7},{7,6},{8,9},{9,8},{10,11... | collective-permute-start | bytes 442376 | tf_op jit(solution)/shard_map/ppermute | solution.py:238

commit v3 on v2

--- a/solution.py
+++ b/solution.py
@@ -61,15 +61,11 @@
     return jnp.dot(a, b, preferred_element_type=jnp.float32)
 
 
-def prepare_kernel(ids_ref, micro_ref, stack_ref, out_ref, right_ref, below_ref, corner_ref, sems):
-    own = micro_ref.at[0]
-    copies = [
-        pltpu.make_async_copy(own.at[:, :TS], right_ref, sems.at[0]),
-        pltpu.make_async_copy(own.at[:TS, :], below_ref, sems.at[1]),
-        pltpu.make_async_copy(own.at[:TS, :TS], corner_ref, sems.at[2]),
-    ]
-    for copy in copies:
-        copy.start()
+def prepare_kernel(ids_ref, micro_hbm, stack_hbm, out_ref, right_ref, below_ref, corner_ref, micro_ref, stack_ref, sems):
+    load_stack = pltpu.make_async_copy(stack_hbm, stack_ref, sems.at[0])
+    load_micro = pltpu.make_async_copy(micro_hbm.at[0], micro_ref, sems.at[1])
+    load_stack.start()
+    load_micro.start()
     row = lax.broadcasted_iota(jnp.int32, (2 * ORI_DEV, 256), 0)
     lane = lax.broadcasted_iota(jnp.int32, (2 * ORI_DEV, 256), 1)
     wanted = jnp.zeros((2 * ORI_DEV, 256), jnp.int32)
@@ -77,22 +73,23 @@
     for o in range(ORI_DEV):
         wanted = jnp.where(row % ORI_DEV == o, ids_ref[first + o], wanted)
     hot = jnp.where(lane == wanted, 1.0, 0.0).astype(jnp.bfloat16)
+    load_stack.wait()
     picked = dot(hot, stack_ref[...])
     both = jnp.concatenate([picked[:ORI_DEV, :TS], picked[ORI_DEV:, TS:]], 0).astype(jnp.bfloat16)
     out_ref[...] = jnp.broadcast_to(both[None], out_ref.shape)
-    for copy in copies:
-        copy.wait()
-
-
-def image_kernel(member_ref, own_ref, right_ref, below_ref, corner_ref, col_ref, row_ref, *rest):
-    *out_refs, g_ref = rest
-
+    load_micro.wait()
+    right_ref[...] = micro_ref[:, :TS]
+    below_ref[...] = micro_ref[:TS, :]
+    corner_ref[...] = micro_ref[:TS, :TS]
+
+
+def image_spectra(member_ref, own_ref, right_ref, below_ref, corner_ref, col_ref, row_ref, out_refs, g_ref):
     def columns(first, second, start, count):
         g = dot(first, col_ref[:CORE]) + dot(second, col_ref[CORE:])
         g_ref[0, start : start + count] = g[:, :HALF].astype(jnp.bfloat16)
         g_ref[1, start : start + count] = g[:, HALF:].astype(jnp.bfloat16)
 
-    columns(own_ref[...], right_ref[...], 0, CORE)
+    columns(own_ref[0], right_ref[...], 0, CORE)
     columns(below_ref[...], corner_ref[...], CORE, TS)
     for s, bits in enumerate(ORDER):
         start = pl.multiple_of((member_ref[0] ^ bits) * ROWS, 32)
@@ -100,13 +97,21 @@
         out_refs[s][...] = dot(row_ref[...], piece).astype(jnp.bfloat16)
 
 
-def template_kernel(pixels_ref, col_ref, row_ref, out_ref, shape_ref):
+def template_kernel(pixels_ref, col_hbm, row_hbm, out_ref, shape_ref, col_ref, row_ref, sems):
+    loads = [
+        pltpu.make_async_copy(col_hbm, col_ref, sems.at[0]),
+        pltpu.make_async_copy(row_hbm, row_ref, sems.at[1]),
+    ]
+    for load in loads:
+        load.start()
     values = pixels_ref[...].astype(jnp.float32).reshape(TS, ORI_DEV, TS)
     mean = jnp.sum(jnp.sum(values, 0), 1, keepdims=True) / (TS * TS)
     centered = values - mean[None]
     square = jnp.sum(jnp.sum(centered * centered, 0), 1, keepdims=True) / (TS * TS)
     spread = jnp.sqrt(square + 1e-06) * TS
     shape_ref[...] = (centered / spread[None]).reshape(TS * ORI_DEV, TS)
+    for load in loads:
+        load.wait()
     for o in range(ORI_DEV):
         shape = shape_ref[pl.ds(o, TS, stride=ORI_DEV), :].astype(jnp.bfloat16)
         g = dot(shape, col_ref[...]).astype(jnp.bfloat16)
@@ -140,6 +145,10 @@
     out_ref[1] = jnp.sum(corr, 0).astype(out_ref.dtype)
 
 
+def image_kernel(*refs):
+    image_spectra(*refs[:7], refs[8:12], refs[12])
+
+
 def pair_kernel(first_ref, second_ref, template_ref, inv_row_ref, inv_col_ref, out_a, out_b, inner_a, inner_b):
     block(first_ref, template_ref, inv_row_ref, inv_col_ref, out_a, inner_a)
     block(second_ref, template_ref, inv_row_ref, inv_col_ref, out_b, inner_b)
@@ -158,24 +167,28 @@
 VMEM = pl.BlockSpec(memory_space=pltpu.VMEM)
 SMEM = pl.BlockSpec(memory_space=pltpu.SMEM)
 ANY = pl.BlockSpec(memory_space=pl.ANY)
+HBM = pl.BlockSpec(memory_space=pltpu.HBM)
 LIMIT = 24 * 1024 * 1024
-WHOLE = 60 * 1024 * 1024
-
-
-def call(kernel, outs, specs, scratch=(), flops=0, out_specs=None, limit=LIMIT, moved=2**21):
+
+
+def call(kernel, outs, specs, scratch=(), flops=0):
     return pl.pallas_call(
         kernel,
         out_shape=outs,
         in_specs=specs,
-        out_specs=out_specs or jax.tree.map(lambda _: VMEM, outs),
+        out_specs=jax.tree.map(lambda _: VMEM, outs),
         scratch_shapes=list(scratch),
-        compiler_params=pltpu.CompilerParams(vmem_limit_bytes=limit),
-        cost_estimate=pl.CostEstimate(flops=flops, bytes_accessed=moved, transcendentals=0),
+        compiler_params=pltpu.CompilerParams(vmem_limit_bytes=LIMIT),
+        cost_estimate=pl.CostEstimate(flops=flops, bytes_accessed=2**21, transcendentals=0),
     )
 
 
 def shape_of(dims, dtype=jnp.bfloat16):
     return jax.ShapeDtypeStruct(dims, dtype)
+
+
+def pinned(array):
+    return pltpu.with_memory_space_constraint(jnp.asarray(array), pltpu.HBM)
 
 
 def halo(block, distance):
@@ -198,31 +211,38 @@
             shape_of((TS, CORE)),
             shape_of((TS, TS)),
         ),
-        [SMEM, ANY, VMEM],
-        [pltpu.SemaphoreType.DMA((3,))],
-        out_specs=(VMEM, ANY, ANY, ANY),
-        limit=WHOLE,
-    )(orient_list, micrograph, template_stack)
+        [SMEM, HBM, HBM],
+        [
+            pltpu.VMEM((CORE, CORE), jnp.bfloat16),
+            pltpu.VMEM((256, 256), jnp.bfloat16),
+            pltpu.SemaphoreType.DMA((2,)),
+        ],
+    )(orient_list, pinned(micrograph), pinned(template_stack))
+    pixels = lax.all_to_all(spread, "tile", 0, 0)
     right = halo(right, 1)
     below = halo(below, GRID_W)
     corner = halo(corner, GRID_W + 1)
-    pixels = lax.all_to_all(spread, "tile", 0, 0)
     columns = column_table()
+    templates = call(
+        template_kernel,
+        shape_of((ORI_DEV, 4 * PAIRS, HALF)),
+        [VMEM, HBM, HBM],
+        [
+            pltpu.VMEM((TS * ORI_DEV, TS), jnp.float32),
+            pltpu.VMEM((TS, TILE), jnp.bfloat16),
+            pltpu.VMEM((4 * PAIRS, 2 * TS), jnp.bfloat16),
+            pltpu.SemaphoreType.DMA((2,)),
+        ],
+        flops=1000000000,
+    )(pixels, pinned(columns[:TS]), pinned(row_table(TS)))
     image = call(
         image_kernel,
         (shape_of((4 * PAIRS, HALF)),) * MEMBERS,
-        [SMEM] + [VMEM] * 6,
+        [SMEM] + [VMEM] * 6 + [ANY],
         [pltpu.VMEM((2, TILE, HALF), jnp.bfloat16)],
-        flops=20000000000,
-    )(lax.axis_index("orient")[None], micrograph[0], right, below, corner, columns, row_table(ROWS_IN))
-    templates = call(
-        template_kernel,
-        shape_of((ORI_DEV, 4 * PAIRS, HALF)),
-        [VMEM] * 3,
-        [pltpu.VMEM((TS * ORI_DEV, TS), jnp.float32)],
-        flops=1000000000,
-    )(pixels, columns[:TS], row_table(TS))
-    inverse_rows, inverse_columns = inverse_row_table(), inverse_column_table()
+        flops=1600000000,
+    )(lax.axis_index("orient")[None], micrograph, right, below, corner, columns, row_table(ROWS_IN), templates)
+    tables = inverse_row_table(), inverse_column_table()
     inner = pltpu.VMEM((ORI_DEV * ROWS, TILE), jnp.bfloat16)
 
     def pair(first, second, kind):
@@ -232,7 +252,7 @@
             [VMEM] * 5,
             [inner, inner],
             flops=2000000000,
-        )(image[first], image[second], templates, inverse_rows, inverse_columns)
+        )(image[first], image[second], templates, *tables)
 
     def sent(piece, bits):
         return lax.ppermute(piece, "orient", [(i, i ^ bits) for i in range(MEMBERS)])

time: 61.5 us -> 49.3 us (0.80)
  Pallas kernels: 17.6 us -> 11.2 us
  starting transfers between devices: 28.2 us -> 24.3 us
  local copies, waits for them, and re-layouts: 3.06 us -> 0.68 us
    pallas_call x1, Pallas kernels: 9.7 us -> 2.32 us  [shards(): call(prepare_kernel, (shape_of((TILES, 2 * ORI_DEV, TS)), shape_of((CORE,...]
    all_to_all x1, starting transfers between devices: 18.7 us -> 15.3 us  [shards(): pixels = lax.all_to_all(spread, 'tile', 0, 0)]
    unnamed x14 -> x12, local copies, waits for them, and re-layouts: 3.06 us -> 0.68 us
    pallas_call x1, Pallas kernels: 1.94 us -> 2.65 us  [shards(): call(template_kernel, shape_of((ORI_DEV, 4 * PAIRS, HALF)), [VMEM, HBM, H...]
  transfers between devices with their start and end apart: 7 -> 7, of which waited for: 2 -> 2; matrix products, arithmetic and copies ran while one was open for 0% -> 0% of each run, Pallas kernels for 5% -> 10%
where the time goes in v3:
time: 49.3 us; the launch traced here: 49 us
  starting transfers between devices  24.3 us (49%)
  waiting for transfers between devices  12 us (24%)
  Pallas kernels  11.2 us (23%)
  between operations  0.83 us (2%)
  local copies, waits for them, and re-layouts  0.68 us (1%)
    all_to_all x1, starting transfers between devices, shards(): pixels = lax.all_to_all(spread, 'tile', 0, 0)  15.3 us
    all_to_all x1, waiting for transfers between devices, shards(): pixels = lax.all_to_all(spread, 'tile', 0, 0)  8.22 us
    ppermute x3, starting transfers between devices, sent(): lax.ppermute(piece, 'orient', [(i, i ^ bits) for i in range(MEMBERS)])  5.17 us
    pallas_call x2, Pallas kernels, pair(): call(pair_kernel, (shape_of((2, ROWS, CORE)), shape_of((2, ROWS, CORE), k...  4.23 us
    ppermute x3, starting transfers between devices, halo(): return lax.ppermute(block, ('tile', 'orient'), route)  3.88 us
    ppermute x3, waiting for transfers between devices, sent(): lax.ppermute(piece, 'orient', [(i, i ^ bits) for i in range(MEMBERS)])  3.78 us
    pallas_call x1, Pallas kernels, shards(): call(template_kernel, shape_of((ORI_DEV, 4 * PAIRS, HALF)), [VMEM, HBM, H...  2.65 us
    pallas_call x1, Pallas kernels, shards(): call(prepare_kernel, (shape_of((TILES, 2 * ORI_DEV, TS)), shape_of((CORE,...  2.32 us
  transfers between devices with their start and end apart: 7, of which 2 were waited for; matrix products, arithmetic and copies ran while one was open for 0% of the time, Pallas kernels for 10%

profile of v3, /device:TPU:1, one launch (start us, length us, event | category | flops | bytes accessed | tf_op | source)
XLA Modules:
  0.0 49.0 jit_solution(10264575813492114976)
XLA Ops:
  0.6 0.0 copy-start.1
  0.6 0.6 %copy-done.1 = s32[32]{0:T(128)S(1)} copy-done((s32[32]{0:T(128)S(1)}, s32[32]{0:T(128)}, u32[]{:S(2)}) %copy-start.1) | copy-done | bytes 152
  1.3 2.3 %shard_map.104 = (bf16[64,16,128]{2,1,0:T(8,128)(2,1)}, bf16[384,128]{1,0:T(8,128)(2,1)S(1)}, bf16[128,384]{1,0:T(8,128)(2,1)S(1)}, bf16[128,128]{1,0:T(8,128)(2,1)S(1)}) custom-call(s32[32]{0:T(128)S(1)} %copy-done.1, bf16[1,384,384]{2,1,0:T(8,128)(2,1)} %refs_1_.1, bf16[256,256]{1,0:T(8,128)(2,1)} %stack_hbm.1), custom_call_target="tpu_custom_call" | custom-call | bytes 2097152 | tf_op jit(solution)/shard_map/pallas_call | solution.py:206
  3.6 0.0 copy-start
  3.6 0.0 copy-start.2
  3.6 0.0 copy-start.3
  3.6 15.3 %all-to-all-start = ((bf16[64,16,128]{2,1,0:T(8,128)(2,1)}), bf16[64,16,128]{2,1,0:T(8,128)(2,1)S(1)}, u32[]{:S(2)}, u32[]{:S(2)}) async-start(bf16[64,16,128]{2,1,0:T(8,128)(2,1)} %get-tuple-element.17), calls=%async_computation | async-start | bytes 524288 | tf_op jit(solution)/shard_map/all_to_all | solution.py:221
  18.9 1.3 %collective-permute-start = (bf16[384,128]{1,0:T(8,128)(2,1)S(1)}, bf16[384,128]{1,0:T(8,128)(2,1)S(1)}, u32[]{:S(2)}, u32[]{:S(2)}) collective-permute-start(bf16[384,128]{1,0:T(8,128)(2,1)S(1)} %get-tuple-element.14), channel_id=1, source_target_pairs={{6,0},{7,1},{4,2},{5,3},{10,4},{11,5},{8,6},{9,7},{14,8},{15,9},{1... | collective-permute-start | bytes 294920 | tf_op jit(solution)/shard_map/ppermute | solution.py:202
  20.2 1.3 %collective-permute-start.1 = (bf16[128,384]{1,0:T(8,128)(2,1)S(1)}, bf16[128,384]{1,0:T(8,128)(2,1)S(1)}, u32[]{:S(2)}, u32[]{:S(2)}) collective-permute-start(bf16[128,384]{1,0:T(8,128)(2,1)S(1)} %get-tuple-element.15), channel_id=1, source_target_pairs={{32,0},{33,1},{34,2},{35,3},{36,4},{37,5},{38,6},{39,7},{40,8},{41... | collective-permute-start | bytes 294920 | tf_op jit(solution)/shard_map/ppermute | solution.py:202
  21.5 1.3 %collective-permute-start.2 = (bf16[128,128]{1,0:T(8,128)(2,1)S(1)}, bf16[128,128]{1,0:T(8,128)(2,1)S(1)}, u32[]{:S(2)}, u32[]{:S(2)}) collective-permute-start(bf16[128,128]{1,0:T(8,128)(2,1)S(1)} %get-tuple-element.16), channel_id=1, source_target_pairs={{38,0},{39,1},{36,2},{37,3},{42,4},{43,5},{40,6},{41,7},{46,8},{47... | collective-permute-start | bytes 98312 | tf_op jit(solution)/shard_map/ppermute | solution.py:202
  22.8 8.2 %all-to-all-done.pixels_ref = bf16[64,16,128]{2,1,0:T(8,128)(2,1)S(1)} async-done(((bf16[64,16,128]{2,1,0:T(8,128)(2,1)}), bf16[64,16,128]{2,1,0:T(8,128)(2,1)S(1)}, u32[]{:S(2)}, u32[]{:S(2)}) %all-to-all-start) | async-done | bytes 262176 | tf_op jit(solution)/shard_map/all_to_all | solution.py:221
  31.0 2.7 %shard_map.105.refs_7_.template_ref = bf16[8,512,256]{2,1,0:T(8,128)(2,1)S(1)} custom-call(bf16[64,16,128]{2,1,0:T(8,128)(2,1)S(1)} %all-to-all-done.pixels_ref, bf16[128,512]{1,0:T(8,128)(2,1)} %constant.16.clone.col_hbm, bf16[512,256]{1,0:T(8,128)(2,1)} %constant.17.clone.row_hbm), custom_call_target="tpu_custom_call" | custom-call | flops 1000000000 | bytes 2097152 | tf_op jit(solution)/shard_map/pallas_call | solution.py:226
  33.7 0.0 collective-permute-done.2.refs_4_
  33.7 0.0 collective-permute-done.refs_2_
  33.7 0.0 collective-permute-done.1.refs_3_
  33.7 0.0 copy-done
  33.7 0.0 copy-done.2
  33.8 0.0 copy-done.3
  33.8 0.0 copy-start.4
  33.8 0.0 copy-start.5
  33.8 1.3 %shard_map.106 = (bf16[512,256]{1,0:T(8,128)(2,1)S(1)}, bf16[512,256]{1,0:T(8,128)(2,1)S(1)}, bf16[512,256]{1,0:T(8,128)(2,1)S(1)}, bf16[512,256]{1,0:T(8,128)(2,1)S(1)}) custom-call(s32[1]{0:T(128)} %bitcast.refs_0_, bf16[1,384,384]{2,1,0:T(8,128)(2,1)S(1)} %copy-done, bf16[384,128]{1,0:T(8,128)(2,1)S(1)} %collective-permute-done.refs_2_, ...), custom_call_target="tpu_custom_call" | custom-call | flops 1600000000 | bytes 2097152 | tf_op jit(solution)/shard_map/pallas_call | solution.py:238
  35.1 0.0 copy-done.4
  35.1 0.0 copy-done.5
  35.1 2.1 %shard_map.108 = (bf16[2,96,384]{2,1,0:T(8,128)(2,1)S(1)}, bf16[2,96,384]{2,1,0:T(8,128)(2,1)S(1)}) custom-call(bf16[512,256]{1,0:T(8,128)(2,1)S(1)} %get-tuple-element.21.first_ref, bf16[512,256]{1,0:T(8,128)(2,1)S(1)} %get-tuple-element.22.second_ref, bf16[8,512,256]{2,1,0:T(8,128)(2,1)S(1)} %shard_map.105.refs_7_.template_ref, ...), custom_call_target="tpu_custom_call" | custom-call | flops 2000000000 | bytes 2097152 | tf_op jit(solution)/shard_map/pallas_call | solution.py:249
  37.2 0.4 collective-permute-start.3
  37.6 4.7 %collective-permute-start.4 = (bf16[2,96,384]{2,1,0:T(8,128)(2,1)S(1)}, bf16[2,96,384]{2,1,0:T(8,128)(2,1)S(1)}, u32[]{:S(2)}, u32[]{:S(2)}) collective-permute-start(bf16[2,96,384]{2,1,0:T(8,128)(2,1)S(1)} %get-tuple-element.24), channel_id=1, source_target_pairs={{0,3},{1,2},{2,1},{3,0},{4,7},{5,6},{6,5},{7,4},{8,11},{9,10},{10,... | collective-permute-start | bytes 442376 | tf_op jit(solution)/shard_map/ppermute | solution.py:258
  42.3 2.1 %shard_map.107 = (bf16[2,96,384]{2,1,0:T(8,128)(2,1)S(1)}, f32[2,96,384]{2,1,0:T(8,128)S(1)}) custom-call(bf16[512,256]{1,0:T(8,128)(2,1)S(1)} %get-tuple-element.18.first_ref, bf16[512,256]{1,0:T(8,128)(2,1)S(1)} %get-tuple-element.19.second_ref, bf16[8,512,256]{2,1,0:T(8,128)(2,1)S(1)} %shard_map.105.refs_7_.template_ref, bf16[96,256]{1,0:T(8,128)(2,1)S(1)} %copy-done.5, ...), custom_call_target="tpu_custom_call" | custom-call | flops 2000000000 | bytes 2097152 | tf_op jit(solution)/shard_map/pallas_call | solution.py:249
  44.4 0.1 collective-permute-start.5
  44.5 0.0 collective-permute-done.3.a_ref
  44.5 3.8 %collective-permute-done.4.b_ref = bf16[2,96,384]{2,1,0:T(8,128)(2,1)S(1)} collective-permute-done((bf16[2,96,384]{2,1,0:T(8,128)(2,1)S(1)}, bf16[2,96,384]{2,1,0:T(8,128)(2,1)S(1)}, u32[]{:S(2)}, u32[]{:S(2)}) %collective-permute-start.4) | collective-permute-done | bytes 147488 | tf_op jit(solution)/shard_map/ppermute | solution.py:258
  48.3 0.0 collective-permute-done.5.c_ref
  48.3 0.7 %shard_map.109 = (f32[1,96,384]{2,1,0:T(8,128)}, f32[1,96,384]{2,1,0:T(8,128)}) custom-call(f32[2,96,384]{2,1,0:T(8,128)S(1)} %get-tuple-element.20.own_ref, bf16[2,96,384]{2,1,0:T(8,128)(2,1)S(1)} %collective-permute-done.3.a_ref, bf16[2,96,384]{2,1,0:T(8,128)(2,1)S(1)} %collective-permute-done.4.b_ref, bf16[2,96,384]{2,1,0:T(8,128)(2,1)S(1)} %collective-permute-done.5.c_ref), custom_call_target="tpu_custom_call" | custom-call | bytes 2097152 | tf_op jit(solution)/shard_map/pallas_call | solution.py:264
Async XLA Ops:
  0.6 0.7 %copy-start.1 = (s32[32]{0:T(128)S(1)}, s32[32]{0:T(128)}, u32[]{:S(2)}) copy-start(s32[32]{0:T(128)} %ids_ref.1) | copy-start | bytes 388
  3.6 30.1 %copy-start = (bf16[1,384,384]{2,1,0:T(8,128)(2,1)S(1)}, bf16[1,384,384]{2,1,0:T(8,128)(2,1)}, u32[]{:S(2)}) copy-start(bf16[1,384,384]{2,1,0:T(8,128)(2,1)} %refs_1_.1) | copy-start | bytes 884740
  3.6 30.1 %copy-start.2 = (bf16[512,512]{1,0:T(8,128)(2,1)S(1)}, bf16[512,512]{1,0:T(8,128)(2,1)}, u32[]{:S(2)}) copy-start(bf16[512,512]{1,0:T(8,128)(2,1)} %constant.18.clone.refs_5_) | copy-start | bytes 1572868
  3.6 30.1 %copy-start.3 = (bf16[512,448]{1,0:T(8,128)(2,1)S(1)}, bf16[512,448]{1,0:T(8,128)(2,1)}, u32[]{:S(2)}) copy-start(bf16[512,448]{1,0:T(8,128)(2,1)} %constant.19.clone.refs_6_) | copy-start | bytes 1376260
  3.6 27.4 %all-to-all-start = ((bf16[64,16,128]{2,1,0:T(8,128)(2,1)}), bf16[64,16,128]{2,1,0:T(8,128)(2,1)S(1)}, u32[]{:S(2)}, u32[]{:S(2)}) async-start(bf16[64,16,128]{2,1,0:T(8,128)(2,1)} %get-tuple-element.17), calls=%async_computation | async-start | bytes 524288 | tf_op jit(solution)/shard_map/all_to_all | solution.py:221
  18.9 14.8 %collective-permute-start = (bf16[384,128]{1,0:T(8,128)(2,1)S(1)}, bf16[384,128]{1,0:T(8,128)(2,1)S(1)}, u32[]{:S(2)}, u32[]{:S(2)}) collective-permute-start(bf16[384,128]{1,0:T(8,128)(2,1)S(1)} %get-tuple-element.14), channel_id=1, source_target_pairs={{6,0},{7,1},{4,2},{5,3},{10,4},{11,5},{8,6},{9,7},{14,8},{15,9},{1... | collective-permute-start | bytes 294920 | tf_op jit(solution)/shard_map/ppermute | solution.py:202
  20.2 13.5 %collective-permute-start.1 = (bf16[128,384]{1,0:T(8,128)(2,1)S(1)}, bf16[128,384]{1,0:T(8,128)(2,1)S(1)}, u32[]{:S(2)}, u32[]{:S(2)}) collective-permute-start(bf16[128,384]{1,0:T(8,128)(2,1)S(1)} %get-tuple-element.15), channel_id=1, source_target_pairs={{32,0},{33,1},{34,2},{35,3},{36,4},{37,5},{38,6},{39,7},{40,8},{41... | collective-permute-start | bytes 294920 | tf_op jit(solution)/shard_map/ppermute | solution.py:202
  21.5 12.2 %collective-permute-start.2 = (bf16[128,128]{1,0:T(8,128)(2,1)S(1)}, bf16[128,128]{1,0:T(8,128)(2,1)S(1)}, u32[]{:S(2)}, u32[]{:S(2)}) collective-permute-start(bf16[128,128]{1,0:T(8,128)(2,1)S(1)} %get-tuple-element.16), channel_id=1, source_target_pairs={{38,0},{39,1},{36,2},{37,3},{42,4},{43,5},{40,6},{41,7},{46,8},{47... | collective-permute-start | bytes 98312 | tf_op jit(solution)/shard_map/ppermute | solution.py:202
  33.8 1.3 %copy-start.4 = (bf16[512,384]{1,0:T(8,128)(2,1)S(1)}, bf16[512,384]{1,0:T(8,128)(2,1)}, u32[]{:S(2)}) copy-start(bf16[512,384]{1,0:T(8,128)(2,1)} %constant.21.clone.inv_col_ref) | copy-start | bytes 1179652
  33.8 1.3 %copy-start.5 = (bf16[96,256]{1,0:T(8,128)(2,1)S(1)}, bf16[96,256]{1,0:T(8,128)(2,1)}, u32[]{:S(2)}) copy-start(bf16[96,256]{1,0:T(8,128)(2,1)} %constant.20.clone.inv_row_ref) | copy-start | bytes 147460
  37.2 7.3 %collective-permute-start.3 = (bf16[2,96,384]{2,1,0:T(8,128)(2,1)S(1)}, bf16[2,96,384]{2,1,0:T(8,128)(2,1)S(1)}, u32[]{:S(2)}, u32[]{:S(2)}) collective-permute-start(bf16[2,96,384]{2,1,0:T(8,128)(2,1)S(1)} %get-tuple-element.23), channel_id=1, source_target_pairs={{0,2},{1,3},{2,0},{3,1},{4,6},{5,7},{6,4},{7,5},{8,10},{9,11},{10,... | collective-permute-start | bytes 442376 | tf_op jit(solution)/shard_map/ppermute | solution.py:258
  37.6 10.7 %collective-permute-start.4 = (bf16[2,96,384]{2,1,0:T(8,128)(2,1)S(1)}, bf16[2,96,384]{2,1,0:T(8,128)(2,1)S(1)}, u32[]{:S(2)}, u32[]{:S(2)}) collective-permute-start(bf16[2,96,384]{2,1,0:T(8,128)(2,1)S(1)} %get-tuple-element.24), channel_id=1, source_target_pairs={{0,3},{1,2},{2,1},{3,0},{4,7},{5,6},{6,5},{7,4},{8,11},{9,10},{10,... | collective-permute-start | bytes 442376 | tf_op jit(solution)/shard_map/ppermute | solution.py:258
  44.4 3.9 %collective-permute-start.5 = (bf16[2,96,384]{2,1,0:T(8,128)(2,1)S(1)}, bf16[2,96,384]{2,1,0:T(8,128)(2,1)S(1)}, u32[]{:S(2)}, u32[]{:S(2)}) collective-permute-start(bf16[2,96,384]{2,1,0:T(8,128)(2,1)S(1)} %get-tuple-element.25), channel_id=1, source_target_pairs={{0,1},{1,0},{2,3},{3,2},{4,5},{5,4},{6,7},{7,6},{8,9},{9,8},{10,11... | collective-permute-start | bytes 442376 | tf_op jit(solution)/shard_map/ppermute | solution.py:258

commit v4 on v3

--- a/solution.py
+++ b/solution.py
@@ -34,12 +34,16 @@
     return bf16(np.concatenate([np.cos(angle), -np.sin(angle)], 1))
 
 
-def row_table(rows):
+def row_table():
     j = np.arange(PAIRS)[:, None]
-    m = np.arange(rows)[None, :]
+    m = np.arange(ROWS_IN)[None, :]
     angle = (math.pi / LENGTH) * ((m * (2 * j + 1)) % (2 * LENGTH))
     c, s = np.cos(angle), np.sin(angle)
-    return bf16(np.block([[c, s], [-s, c], [c, -s], [s, c]]))
+    parts = []
+    for cut in (slice(0, TS), slice(TS, ROWS_IN)):
+        u, v = c[:, cut], s[:, cut]
+        parts.append(np.block([[u, v], [-v, u], [u, -v], [v, u]]))
+    return bf16(np.concatenate(parts, 1))
 
 
 def inverse_row_table():
@@ -61,15 +65,20 @@
     return jnp.dot(a, b, preferred_element_type=jnp.float32)
 
 
-def prepare_kernel(ids_ref, micro_hbm, stack_hbm, out_ref, right_ref, below_ref, corner_ref, micro_ref, stack_ref, sems):
-    load_stack = pltpu.make_async_copy(stack_hbm, stack_ref, sems.at[0])
-    load_micro = pltpu.make_async_copy(micro_hbm.at[0], micro_ref, sems.at[1])
+def prepare_kernel(
+    ids_hbm, micro_hbm, stack_hbm, out_hbm, right_ref, below_ref, corner_ref, ids_ref, micro_ref, stack_ref, out_ref, sems
+):
+    load_ids = pltpu.make_async_copy(ids_hbm, ids_ref, sems.at[0])
+    load_stack = pltpu.make_async_copy(stack_hbm, stack_ref, sems.at[1])
+    load_micro = pltpu.make_async_copy(micro_hbm.at[0], micro_ref, sems.at[2])
+    load_ids.start()
     load_stack.start()
     load_micro.start()
     row = lax.broadcasted_iota(jnp.int32, (2 * ORI_DEV, 256), 0)
     lane = lax.broadcasted_iota(jnp.int32, (2 * ORI_DEV, 256), 1)
     wanted = jnp.zeros((2 * ORI_DEV, 256), jnp.int32)
     first = lax.axis_index("orient") * ORI_DEV
+    load_ids.wait()
     for o in range(ORI_DEV):
         wanted = jnp.where(row % ORI_DEV == o, ids_ref[first + o], wanted)
     hot = jnp.where(lane == wanted, 1.0, 0.0).astype(jnp.bfloat16)
@@ -77,46 +86,57 @@
     picked = dot(hot, stack_ref[...])
     both = jnp.concatenate([picked[:ORI_DEV, :TS], picked[ORI_DEV:, TS:]], 0).astype(jnp.bfloat16)
     out_ref[...] = jnp.broadcast_to(both[None], out_ref.shape)
+    store = pltpu.make_async_copy(out_ref, out_hbm, sems.at[3])
+    store.start()
     load_micro.wait()
     right_ref[...] = micro_ref[:, :TS]
     below_ref[...] = micro_ref[:TS, :]
     corner_ref[...] = micro_ref[:TS, :TS]
-
-
-def image_spectra(member_ref, own_ref, right_ref, below_ref, corner_ref, col_ref, row_ref, out_refs, g_ref):
-    def columns(first, second, start, count):
-        g = dot(first, col_ref[:CORE]) + dot(second, col_ref[CORE:])
-        g_ref[0, start : start + count] = g[:, :HALF].astype(jnp.bfloat16)
-        g_ref[1, start : start + count] = g[:, HALF:].astype(jnp.bfloat16)
-
-    columns(own_ref[0], right_ref[...], 0, CORE)
-    columns(below_ref[...], corner_ref[...], CORE, TS)
-    for s, bits in enumerate(ORDER):
-        start = pl.multiple_of((member_ref[0] ^ bits) * ROWS, 32)
-        piece = jnp.concatenate([g_ref[0, pl.ds(start, ROWS_IN)], g_ref[1, pl.ds(start, ROWS_IN)]], 0)
-        out_refs[s][...] = dot(row_ref[...], piece).astype(jnp.bfloat16)
-
-
-def template_kernel(pixels_ref, col_hbm, row_hbm, out_ref, shape_ref, col_ref, row_ref, sems):
-    loads = [
-        pltpu.make_async_copy(col_hbm, col_ref, sems.at[0]),
-        pltpu.make_async_copy(row_hbm, row_ref, sems.at[1]),
-    ]
+    store.wait()
+
+
+def load_kernel(*refs):
+    sources, targets, sems = refs[:5], refs[6:11], refs[11]
+    loads = [pltpu.make_async_copy(a, b, sems.at[i]) for i, (a, b) in enumerate(zip(sources, targets))]
     for load in loads:
         load.start()
+    for load in loads:
+        load.wait()
+
+
+def template_kernel(pixels_ref, col_ref, row_ref, out_ref, shape_ref):
     values = pixels_ref[...].astype(jnp.float32).reshape(TS, ORI_DEV, TS)
     mean = jnp.sum(jnp.sum(values, 0), 1, keepdims=True) / (TS * TS)
     centered = values - mean[None]
     square = jnp.sum(jnp.sum(centered * centered, 0), 1, keepdims=True) / (TS * TS)
     spread = jnp.sqrt(square + 1e-06) * TS
     shape_ref[...] = (centered / spread[None]).reshape(TS * ORI_DEV, TS)
-    for load in loads:
-        load.wait()
-    for o in range(ORI_DEV):
-        shape = shape_ref[pl.ds(o, TS, stride=ORI_DEV), :].astype(jnp.bfloat16)
-        g = dot(shape, col_ref[...]).astype(jnp.bfloat16)
-        g = jnp.concatenate([g[:, :HALF], g[:, HALF:]], 0)
-        out_ref[o] = dot(row_ref[...], g).astype(jnp.bfloat16)
+    shapes = [shape_ref[pl.ds(o, TS, stride=ORI_DEV), :].astype(jnp.bfloat16) for o in range(ORI_DEV)]
+    half = ORI_DEV // 2
+    for start in (0, half):
+        together = jnp.concatenate(shapes[start : start + half], 0)
+        g = dot(together, col_ref[:TS]).astype(jnp.bfloat16)
+        for o in range(half):
+            mine = g[o * TS : (o + 1) * TS]
+            mine = jnp.concatenate([mine[:, :HALF], mine[:, HALF:]], 0)
+            out_ref[start + o] = dot(row_ref[:, : 2 * TS], mine).astype(jnp.bfloat16)
+
+
+def image_columns(own_ref, right_ref, below_ref, corner_ref, col_ref, g_ref):
+    def columns(first, second, start, count):
+        g = dot(first, col_ref[:CORE]) + dot(second, col_ref[CORE:])
+        g_ref[0, start : start + count] = g[:, :HALF].astype(jnp.bfloat16)
+        g_ref[1, start : start + count] = g[:, HALF:].astype(jnp.bfloat16)
+
+    columns(own_ref[0], right_ref[...], 0, CORE)
+    columns(below_ref[...], corner_ref[...], CORE, TS)
+
+
+def image_rows(member_ref, row_ref, g_ref, bits, out_ref):
+    start = pl.multiple_of((member_ref[0] ^ bits) * ROWS, 32)
+    cuts = [(start, TS), (pl.multiple_of(start + TS, 32), ROWS_IN - TS)]
+    piece = jnp.concatenate([g_ref[p, pl.ds(*cut)] for cut in cuts for p in range(2)], 0)
+    out_ref[...] = dot(row_ref[...], piece).astype(jnp.bfloat16)
 
 
 def block(image_ref, template_ref, inv_row_ref, inv_col_ref, out_ref, inner_ref):
@@ -145,8 +165,11 @@
     out_ref[1] = jnp.sum(corr, 0).astype(out_ref.dtype)
 
 
-def image_kernel(*refs):
-    image_spectra(*refs[:7], refs[8:12], refs[12])
+def image_kernel(member_ref, *refs):
+    own_ref, right_ref, below_ref, corner_ref, col_ref, row_ref, *out_refs, g_ref = refs
+    image_columns(own_ref, right_ref, below_ref, corner_ref, col_ref, g_ref)
+    for bits, out_ref in zip(ORDER, out_refs):
+        image_rows(member_ref, row_ref, g_ref, bits, out_ref)
 
 
 def pair_kernel(first_ref, second_ref, template_ref, inv_row_ref, inv_col_ref, out_a, out_b, inner_a, inner_b):
@@ -171,12 +194,12 @@
 LIMIT = 24 * 1024 * 1024
 
 
-def call(kernel, outs, specs, scratch=(), flops=0):
+def call(kernel, outs, specs, scratch=(), flops=0, out_specs=None):
     return pl.pallas_call(
         kernel,
         out_shape=outs,
         in_specs=specs,
-        out_specs=jax.tree.map(lambda _: VMEM, outs),
+        out_specs=out_specs or jax.tree.map(lambda _: VMEM, outs),
         scratch_shapes=list(scratch),
         compiler_params=pltpu.CompilerParams(vmem_limit_bytes=LIMIT),
         cost_estimate=pl.CostEstimate(flops=flops, bytes_accessed=2**21, transcendentals=0),
@@ -211,38 +234,43 @@
             shape_of((TS, CORE)),
             shape_of((TS, TS)),
         ),
-        [SMEM, HBM, HBM],
+        [HBM] * 3,
         [
+            pltpu.SMEM((MEMBERS * ORI_DEV,), jnp.int32),
             pltpu.VMEM((CORE, CORE), jnp.bfloat16),
             pltpu.VMEM((256, 256), jnp.bfloat16),
-            pltpu.SemaphoreType.DMA((2,)),
+            pltpu.VMEM((TILES, 2 * ORI_DEV, TS), jnp.bfloat16),
+            pltpu.SemaphoreType.DMA((4,)),
         ],
-    )(orient_list, pinned(micrograph), pinned(template_stack))
+        out_specs=(HBM, VMEM, VMEM, VMEM),
+    )(pinned(orient_list), pinned(micrograph), pinned(template_stack))
     pixels = lax.all_to_all(spread, "tile", 0, 0)
+    kept = [column_table(), row_table(), inverse_row_table(), inverse_column_table(), micrograph]
+    columns, rows, *tables, own_block = call(
+        load_kernel,
+        tuple(shape_of(array.shape) for array in kept),
+        [HBM] * 5 + [ANY],
+        [pltpu.SemaphoreType.DMA((5,))],
+        flops=1000000000,
+    )(*[pinned(array) for array in kept], corner)
     right = halo(right, 1)
     below = halo(below, GRID_W)
     corner = halo(corner, GRID_W + 1)
-    columns = column_table()
+    member = lax.axis_index("orient")[None]
     templates = call(
         template_kernel,
         shape_of((ORI_DEV, 4 * PAIRS, HALF)),
-        [VMEM, HBM, HBM],
-        [
-            pltpu.VMEM((TS * ORI_DEV, TS), jnp.float32),
-            pltpu.VMEM((TS, TILE), jnp.bfloat16),
-            pltpu.VMEM((4 * PAIRS, 2 * TS), jnp.bfloat16),
-            pltpu.SemaphoreType.DMA((2,)),
-        ],
+        [VMEM] * 3,
+        [pltpu.VMEM((TS * ORI_DEV, TS), jnp.float32)],
         flops=1000000000,
-    )(pixels, pinned(columns[:TS]), pinned(row_table(TS)))
+    )(pixels, columns, rows)
     image = call(
         image_kernel,
         (shape_of((4 * PAIRS, HALF)),) * MEMBERS,
-        [SMEM] + [VMEM] * 6 + [ANY],
+        [SMEM] + [VMEM] * 6,
         [pltpu.VMEM((2, TILE, HALF), jnp.bfloat16)],
         flops=1600000000,
-    )(lax.axis_index("orient")[None], micrograph, right, below, corner, columns, row_table(ROWS_IN), templates)
-    tables = inverse_row_table(), inverse_column_table()
+    )(member, own_block, right, below, corner, columns, rows)
     inner = pltpu.VMEM((ORI_DEV * ROWS, TILE), jnp.bfloat16)
 
     def pair(first, second, kind):

time: 49.3 us -> 45.8 us (0.929)
  waiting for transfers between devices: 12 us -> 10.3 us
  starting transfers between devices: 24.3 us -> 23.2 us
  local copies, waits for them, and re-layouts: 0.68 us -> 0 us
    all_to_all x1, waiting for transfers between devices: 8.22 us -> 0.01 us  [shards(): pixels = lax.all_to_all(spread, 'tile', 0, 0)]
    ppermute x3, waiting for transfers between devices: 0.01 us -> 6.48 us  [halo(): return lax.ppermute(block, ('tile', 'orient'), route)]
    ppermute x3, starting transfers between devices: 5.17 us -> 4.17 us  [sent(): lax.ppermute(piece, 'orient', [(i, i ^ bits) for i in range(MEMBERS)])]
    unnamed x12 -> x0, local copies, waits for them, and re-layouts: 0.68 us -> none
    pallas_call x1, Pallas kernels: 2.32 us -> 1.81 us  [shards(): call(prepare_kernel, (shape_of((TILES, 2 * ORI_DEV, TS)), shape_of((CORE,...]
    pallas_call x1 -> x2, Pallas kernels: 2.65 us -> 3.02 us  [the longest x1 1.56 us: shards(): call(template_kernel, shape_of((ORI_DEV, 4 * PAIRS, HALF)), [VMEM] * 3, [...]
where the time goes in v4:
time: 45.8 us; the launch traced here: 45.1 us
  starting transfers between devices  23.2 us (51%)
  Pallas kernels  10.9 us (24%)
  waiting for transfers between devices  10.3 us (22%)
  between operations  0.74 us (2%)
    all_to_all x1, starting transfers between devices, shards(): pixels = lax.all_to_all(spread, 'tile', 0, 0)  15.1 us
    ppermute x3, waiting for transfers between devices, halo(): return lax.ppermute(block, ('tile', 'orient'), route)  6.48 us
    ppermute x3, starting transfers between devices, sent(): lax.ppermute(piece, 'orient', [(i, i ^ bits) for i in range(MEMBERS)])  4.17 us
    pallas_call x2, Pallas kernels, pair(): call(pair_kernel, (shape_of((2, ROWS, CORE)), shape_of((2, ROWS, CORE), k...  4.01 us
    ppermute x3, starting transfers between devices, halo(): return lax.ppermute(block, ('tile', 'orient'), route)  3.88 us
    ppermute x3, waiting for transfers between devices, sent(): lax.ppermute(piece, 'orient', [(i, i ^ bits) for i in range(MEMBERS)])  3.86 us
    pallas_call x1, Pallas kernels, shards(): call(prepare_kernel, (shape_of((TILES, 2 * ORI_DEV, TS)), shape_of((CORE,...  1.81 us
    pallas_call x1, Pallas kernels, shards(): call(template_kernel, shape_of((ORI_DEV, 4 * PAIRS, HALF)), [VMEM] * 3, [...  1.56 us
  transfers between devices with their start and end apart: 7, of which 2 were waited for; matrix products, arithmetic and copies ran while one was open for 0% of the time, Pallas kernels for 10%

profile of v4, /device:TPU:1, one launch (start us, length us, event | category | flops | bytes accessed | tf_op | source)
XLA Modules:
  0.0 45.1 jit_solution(8526397302994517189)
XLA Ops:
  0.6 1.8 %shard_map.86 = (bf16[64,16,128]{2,1,0:T(8,128)(2,1)}, bf16[384,128]{1,0:T(8,128)(2,1)S(1)}, bf16[128,384]{1,0:T(8,128)(2,1)S(1)}, bf16[128,128]{1,0:T(8,128)(2,1)S(1)}) custom-call(s32[32]{0:T(128)} %ids_hbm.1, bf16[1,384,384]{2,1,0:T(8,128)(2,1)} %refs_4_.1, bf16[256,256]{1,0:T(8,128)(2,1)} %stack_hbm.1), custom_call_target="tpu_custom_call" | custom-call | bytes 2097152 | tf_op jit(solution)/shard_map/pallas_call | solution.py:229
  2.4 15.1 %all-to-all-start = ((bf16[64,16,128]{2,1,0:T(8,128)(2,1)}), bf16[64,16,128]{2,1,0:T(8,128)(2,1)S(1)}, u32[]{:S(2)}, u32[]{:S(2)}) async-start(bf16[64,16,128]{2,1,0:T(8,128)(2,1)} %get-tuple-element.27), calls=%async_computation | async-start | bytes 524288 | tf_op jit(solution)/shard_map/all_to_all | solution.py:247
  17.6 1.3 %collective-permute-start = (bf16[384,128]{1,0:T(8,128)(2,1)S(1)}, bf16[384,128]{1,0:T(8,128)(2,1)S(1)}, u32[]{:S(2)}, u32[]{:S(2)}) collective-permute-start(bf16[384,128]{1,0:T(8,128)(2,1)S(1)} %get-tuple-element.21), channel_id=1, source_target_pairs={{6,0},{7,1},{4,2},{5,3},{10,4},{11,5},{8,6},{9,7},{14,8},{15,9},{1... | collective-permute-start | bytes 294920 | tf_op jit(solution)/shard_map/ppermute | solution.py:225
  18.9 1.3 %collective-permute-start.1 = (bf16[128,384]{1,0:T(8,128)(2,1)S(1)}, bf16[128,384]{1,0:T(8,128)(2,1)S(1)}, u32[]{:S(2)}, u32[]{:S(2)}) collective-permute-start(bf16[128,384]{1,0:T(8,128)(2,1)S(1)} %get-tuple-element.22), channel_id=1, source_target_pairs={{32,0},{33,1},{34,2},{35,3},{36,4},{37,5},{38,6},{39,7},{40,8},{41... | collective-permute-start | bytes 294920 | tf_op jit(solution)/shard_map/ppermute | solution.py:225
  20.2 1.3 %collective-permute-start.2 = (bf16[128,128]{1,0:T(8,128)(2,1)S(1)}, bf16[128,128]{1,0:T(8,128)(2,1)S(1)}, u32[]{:S(2)}, u32[]{:S(2)}) collective-permute-start(bf16[128,128]{1,0:T(8,128)(2,1)S(1)} %get-tuple-element.19.refs_5_), channel_id=1, source_target_pairs={{38,0},{39,1},{36,2},{37,3},{42,4},{43,5},{40,6},{41,7},{46,8},{47... | collective-permute-start | bytes 98312 | tf_op jit(solution)/shard_map/ppermute | solution.py:225
  21.5 1.5 %shard_map.87 = (bf16[512,512]{1,0:T(8,128)(2,1)S(1)}, bf16[512,448]{1,0:T(8,128)(2,1)S(1)}, bf16[96,256]{1,0:T(8,128)(2,1)S(1)}, bf16[512,384]{1,0:T(8,128)(2,1)S(1)}, bf16[1,384,384]{2,1,0:T(8,128)(2,1)S(1)}) custom-call(bf16[512,512]{1,0:T(8,128)(2,1)} %constant.12.clone.refs_0_, bf16[512,448]{1,0:T(8,128)(2,1)} %constant.13.clone.refs_1_, ...), custom_call_target="tpu_custom_call" | custom-call | flops 1000000000 | bytes 2097152 | tf_op jit(solution)/shard_map/pallas_call | solution.py:249
  23.0 6.5 %collective-permute-done.2.refs_3_ = bf16[128,128]{1,0:T(8,128)(2,1)S(1)} collective-permute-done((bf16[128,128]{1,0:T(8,128)(2,1)S(1)}, bf16[128,128]{1,0:T(8,128)(2,1)S(1)}, u32[]{:S(2)}, u32[]{:S(2)}) %collective-permute-start.2) | collective-permute-done | bytes 32800 | tf_op jit(solution)/shard_map/ppermute | solution.py:225
  29.4 0.0 collective-permute-done.refs_1_
  29.4 0.0 collective-permute-done.1.refs_2_
  29.4 1.3 %shard_map.88 = (bf16[512,256]{1,0:T(8,128)(2,1)S(1)}, bf16[512,256]{1,0:T(8,128)(2,1)S(1)}, bf16[512,256]{1,0:T(8,128)(2,1)S(1)}, bf16[512,256]{1,0:T(8,128)(2,1)S(1)}) custom-call(s32[1]{0:T(128)} %bitcast.member_ref, bf16[1,384,384]{2,1,0:T(8,128)(2,1)S(1)} %get-tuple-element.20.refs_0_, bf16[384,128]{1,0:T(8,128)(2,1)S(1)} %collective-permute-done.refs_1_, ...), custom_call_target="tpu_custom_call" | custom-call | flops 1600000000 | bytes 2097152 | tf_op jit(solution)/shard_map/pallas_call | solution.py:267
  30.7 0.0 all-to-all-done.pixels_ref
  30.7 1.6 %shard_map.89.template_ref = bf16[8,512,256]{2,1,0:T(8,128)(2,1)S(1)} custom-call(bf16[64,16,128]{2,1,0:T(8,128)(2,1)S(1)} %all-to-all-done.pixels_ref, bf16[512,512]{1,0:T(8,128)(2,1)S(1)} %get-tuple-element.23.refs_4_.col_ref, bf16[512,448]{1,0:T(8,128)(2,1)S(1)} %get-tuple-element.24.refs_5_.row_ref), custom_call_target="tpu_custom_call" | custom-call | flops 1000000000 | bytes 2097152 | tf_op jit(solution)/shard_map/pallas_call | solution.py:260
  32.3 2.0 %shard_map.91 = (bf16[2,96,384]{2,1,0:T(8,128)(2,1)S(1)}, bf16[2,96,384]{2,1,0:T(8,128)(2,1)S(1)}) custom-call(bf16[512,256]{1,0:T(8,128)(2,1)S(1)} %get-tuple-element.31.first_ref, bf16[512,256]{1,0:T(8,128)(2,1)S(1)} %get-tuple-element.32.second_ref, bf16[8,512,256]{2,1,0:T(8,128)(2,1)S(1)} %shard_map.89.template_ref, ...), custom_call_target="tpu_custom_call" | custom-call | flops 2000000000 | bytes 2097152 | tf_op jit(solution)/shard_map/pallas_call | solution.py:277
  34.3 0.3 collective-permute-start.3
  34.6 3.7 %collective-permute-start.4 = (bf16[2,96,384]{2,1,0:T(8,128)(2,1)S(1)}, bf16[2,96,384]{2,1,0:T(8,128)(2,1)S(1)}, u32[]{:S(2)}, u32[]{:S(2)}) collective-permute-start(bf16[2,96,384]{2,1,0:T(8,128)(2,1)S(1)} %get-tuple-element.34), channel_id=1, source_target_pairs={{0,3},{1,2},{2,1},{3,0},{4,7},{5,6},{6,5},{7,4},{8,11},{9,10},{10,... | collective-permute-start | bytes 442376 | tf_op jit(solution)/shard_map/ppermute | solution.py:286
  38.4 2.0 %shard_map.90 = (bf16[2,96,384]{2,1,0:T(8,128)(2,1)S(1)}, f32[2,96,384]{2,1,0:T(8,128)S(1)}) custom-call(bf16[512,256]{1,0:T(8,128)(2,1)S(1)} %get-tuple-element.25.first_ref, bf16[512,256]{1,0:T(8,128)(2,1)S(1)} %get-tuple-element.26.second_ref, bf16[8,512,256]{2,1,0:T(8,128)(2,1)S(1)} %shard_map.89.template_ref, ...), custom_call_target="tpu_custom_call" | custom-call | flops 2000000000 | bytes 2097152 | tf_op jit(solution)/shard_map/pallas_call | solution.py:277
  40.4 0.1 collective-permute-start.5
  40.5 0.0 collective-permute-done.3.a_ref
  40.5 3.9 %collective-permute-done.4.b_ref = bf16[2,96,384]{2,1,0:T(8,128)(2,1)S(1)} collective-permute-done((bf16[2,96,384]{2,1,0:T(8,128)(2,1)S(1)}, bf16[2,96,384]{2,1,0:T(8,128)(2,1)S(1)}, u32[]{:S(2)}, u32[]{:S(2)}) %collective-permute-start.4) | collective-permute-done | bytes 147488 | tf_op jit(solution)/shard_map/ppermute | solution.py:286
  44.4 0.0 collective-permute-done.5.c_ref
  44.4 0.7 %shard_map.92 = (f32[1,96,384]{2,1,0:T(8,128)}, f32[1,96,384]{2,1,0:T(8,128)}) custom-call(f32[2,96,384]{2,1,0:T(8,128)S(1)} %get-tuple-element.30.own_ref, bf16[2,96,384]{2,1,0:T(8,128)(2,1)S(1)} %collective-permute-done.3.a_ref, bf16[2,96,384]{2,1,0:T(8,128)(2,1)S(1)} %collective-permute-done.4.b_ref, bf16[2,96,384]{2,1,0:T(8,128)(2,1)S(1)} %collective-permute-done.5.c_ref), custom_call_target="tpu_custom_call" | custom-call | bytes 2097152 | tf_op jit(solution)/shard_map/pallas_call | solution.py:292
Async XLA Ops:
  2.4 28.3 %all-to-all-start = ((bf16[64,16,128]{2,1,0:T(8,128)(2,1)}), bf16[64,16,128]{2,1,0:T(8,128)(2,1)S(1)}, u32[]{:S(2)}, u32[]{:S(2)}) async-start(bf16[64,16,128]{2,1,0:T(8,128)(2,1)} %get-tuple-element.27), calls=%async_computation | async-start | bytes 524288 | tf_op jit(solution)/shard_map/all_to_all | solution.py:247
  17.6 11.9 %collective-permute-start = (bf16[384,128]{1,0:T(8,128)(2,1)S(1)}, bf16[384,128]{1,0:T(8,128)(2,1)S(1)}, u32[]{:S(2)}, u32[]{:S(2)}) collective-permute-start(bf16[384,128]{1,0:T(8,128)(2,1)S(1)} %get-tuple-element.21), channel_id=1, source_target_pairs={{6,0},{7,1},{4,2},{5,3},{10,4},{11,5},{8,6},{9,7},{14,8},{15,9},{1... | collective-permute-start | bytes 294920 | tf_op jit(solution)/shard_map/ppermute | solution.py:225
  18.9 10.6 %collective-permute-start.1 = (bf16[128,384]{1,0:T(8,128)(2,1)S(1)}, bf16[128,384]{1,0:T(8,128)(2,1)S(1)}, u32[]{:S(2)}, u32[]{:S(2)}) collective-permute-start(bf16[128,384]{1,0:T(8,128)(2,1)S(1)} %get-tuple-element.22), channel_id=1, source_target_pairs={{32,0},{33,1},{34,2},{35,3},{36,4},{37,5},{38,6},{39,7},{40,8},{41... | collective-permute-start | bytes 294920 | tf_op jit(solution)/shard_map/ppermute | solution.py:225
  20.2 9.2 %collective-permute-start.2 = (bf16[128,128]{1,0:T(8,128)(2,1)S(1)}, bf16[128,128]{1,0:T(8,128)(2,1)S(1)}, u32[]{:S(2)}, u32[]{:S(2)}) collective-permute-start(bf16[128,128]{1,0:T(8,128)(2,1)S(1)} %get-tuple-element.19.refs_5_), channel_id=1, source_target_pairs={{38,0},{39,1},{36,2},{37,3},{42,4},{43,5},{40,6},{41,7},{46,8},{47... | collective-permute-start | bytes 98312 | tf_op jit(solution)/shard_map/ppermute | solution.py:225
  34.3 6.2 %collective-permute-start.3 = (bf16[2,96,384]{2,1,0:T(8,128)(2,1)S(1)}, bf16[2,96,384]{2,1,0:T(8,128)(2,1)S(1)}, u32[]{:S(2)}, u32[]{:S(2)}) collective-permute-start(bf16[2,96,384]{2,1,0:T(8,128)(2,1)S(1)} %get-tuple-element.33), channel_id=1, source_target_pairs={{0,2},{1,3},{2,0},{3,1},{4,6},{5,7},{6,4},{7,5},{8,10},{9,11},{10,... | collective-permute-start | bytes 442376 | tf_op jit(solution)/shard_map/ppermute | solution.py:286
  34.6 9.7 %collective-permute-start.4 = (bf16[2,96,384]{2,1,0:T(8,128)(2,1)S(1)}, bf16[2,96,384]{2,1,0:T(8,128)(2,1)S(1)}, u32[]{:S(2)}, u32[]{:S(2)}) collective-permute-start(bf16[2,96,384]{2,1,0:T(8,128)(2,1)S(1)} %get-tuple-element.34), channel_id=1, source_target_pairs={{0,3},{1,2},{2,1},{3,0},{4,7},{5,6},{6,5},{7,4},{8,11},{9,10},{10,... | collective-permute-start | bytes 442376 | tf_op jit(solution)/shard_map/ppermute | solution.py:286
  40.4 4.0 %collective-permute-start.5 = (bf16[2,96,384]{2,1,0:T(8,128)(2,1)S(1)}, bf16[2,96,384]{2,1,0:T(8,128)(2,1)S(1)}, u32[]{:S(2)}, u32[]{:S(2)}) collective-permute-start(bf16[2,96,384]{2,1,0:T(8,128)(2,1)S(1)} %get-tuple-element.35), channel_id=1, source_target_pairs={{0,1},{1,0},{2,3},{3,2},{4,5},{5,4},{6,7},{7,6},{8,9},{9,8},{10,11... | collective-permute-start | bytes 442376 | tf_op jit(solution)/shard_map/ppermute | solution.py:286

commit v5 on v4

--- a/solution.py
+++ b/solution.py
@@ -20,7 +20,7 @@
 LENGTH = 256
 PAIRS = LENGTH // 2
 HALF = TILE // 2
-ORDER = (2, 3, 1, 0)
+CORE_BIT, CHIP_BIT = 1, 2
 
 
 def bf16(table):
@@ -139,52 +139,53 @@
     out_ref[...] = dot(row_ref[...], piece).astype(jnp.bfloat16)
 
 
-def block(image_ref, template_ref, inv_row_ref, inv_col_ref, out_ref, inner_ref):
+def block(image_ref, template_refs, inv_row_ref, inv_col_ref, out_ref, inner_ref):
     def part(ref, p):
         return ref[p * PAIRS : (p + 1) * PAIRS]
 
-    for o in range(ORI_DEV):
-
-        def cross(p):
-            a, b = part(image_ref, 2 * p), part(image_ref, 2 * p + 1)
-            c, d = part(template_ref.at[o], 2 * p), part(template_ref.at[o], 2 * p + 1)
-            return a * c + b * d, b * c - a * d
-
-        plus_re, plus_im = cross(0)
-        minus_re, minus_im = cross(1)
-        mixed = jnp.concatenate(
-            [
-                jnp.concatenate([plus_re + minus_re, plus_im + minus_im], 1),
-                jnp.concatenate([minus_im - plus_im, plus_re - minus_re], 1),
-            ],
-            0,
-        )
-        inner_ref[o * ROWS : (o + 1) * ROWS] = dot(inv_row_ref[...], mixed).astype(jnp.bfloat16)
-    corr = dot(inner_ref[...], inv_col_ref[...]).reshape(ORI_DEV, ROWS, CORE)
-    out_ref[0] = jnp.max(corr, 0).astype(out_ref.dtype)
-    out_ref[1] = jnp.sum(corr, 0).astype(out_ref.dtype)
+    def corr(template_ref):
+        for o in range(ORI_DEV):
+
+            def cross(p):
+                a, b = part(image_ref, 2 * p), part(image_ref, 2 * p + 1)
+                c, d = part(template_ref.at[o], 2 * p), part(template_ref.at[o], 2 * p + 1)
+                return a * c + b * d, b * c - a * d
+
+            plus_re, plus_im = cross(0)
+            minus_re, minus_im = cross(1)
+            mixed = jnp.concatenate(
+                [
+                    jnp.concatenate([plus_re + minus_re, plus_im + minus_im], 1),
+                    jnp.concatenate([minus_im - plus_im, plus_re - minus_re], 1),
+                ],
+                0,
+            )
+            inner_ref[o * ROWS : (o + 1) * ROWS] = dot(inv_row_ref[...], mixed).astype(jnp.bfloat16)
+        out = dot(inner_ref[...], inv_col_ref[...]).reshape(ORI_DEV, ROWS, CORE)
+        return jnp.max(out, 0), jnp.sum(out, 0)
+
+    high_a, sum_a = corr(template_refs[0])
+    high_b, sum_b = corr(template_refs[1])
+    out_ref[0] = jnp.maximum(high_a, high_b).astype(out_ref.dtype)
+    out_ref[1] = (sum_a + sum_b).astype(out_ref.dtype)
 
 
 def image_kernel(member_ref, *refs):
-    own_ref, right_ref, below_ref, corner_ref, col_ref, row_ref, *out_refs, g_ref = refs
+    own_ref, right_ref, below_ref, corner_ref, col_ref, row_ref, far_ref, near_ref, g_ref = refs
     image_columns(own_ref, right_ref, below_ref, corner_ref, col_ref, g_ref)
-    for bits, out_ref in zip(ORDER, out_refs):
-        image_rows(member_ref, row_ref, g_ref, bits, out_ref)
-
-
-def pair_kernel(first_ref, second_ref, template_ref, inv_row_ref, inv_col_ref, out_a, out_b, inner_a, inner_b):
-    block(first_ref, template_ref, inv_row_ref, inv_col_ref, out_a, inner_a)
-    block(second_ref, template_ref, inv_row_ref, inv_col_ref, out_b, inner_b)
-
-
-def finish_kernel(own_ref, a_ref, b_ref, c_ref, peak_ref, excess_ref):
-    others = [ref[...].astype(jnp.float32) for ref in (a_ref, b_ref, c_ref)]
-    peak, total = own_ref[0], own_ref[1]
-    for other in others:
-        peak = jnp.maximum(peak, other[0])
-        total = total + other[1]
+    image_rows(member_ref, row_ref, g_ref, CHIP_BIT, far_ref)
+    image_rows(member_ref, row_ref, g_ref, 0, near_ref)
+
+
+def block_kernel(image_ref, mine_ref, other_ref, inv_row_ref, inv_col_ref, out_ref, inner_ref):
+    block(image_ref, (mine_ref, other_ref), inv_row_ref, inv_col_ref, out_ref, inner_ref)
+
+
+def finish_kernel(own_ref, far_ref, peak_ref, excess_ref):
+    far = far_ref[...].astype(jnp.float32)
+    peak = jnp.maximum(own_ref[0], far[0])
     peak_ref[0] = peak
-    excess_ref[0] = peak - total / (MEMBERS * ORI_DEV)
+    excess_ref[0] = peak - (own_ref[1] + far[1]) / (MEMBERS * ORI_DEV)
 
 
 VMEM = pl.BlockSpec(memory_space=pltpu.VMEM)
@@ -257,39 +258,40 @@
     below = halo(below, GRID_W)
     corner = halo(corner, GRID_W + 1)
     member = lax.axis_index("orient")[None]
-    templates = call(
-        template_kernel,
-        shape_of((ORI_DEV, 4 * PAIRS, HALF)),
-        [VMEM] * 3,
-        [pltpu.VMEM((TS * ORI_DEV, TS), jnp.float32)],
-        flops=1000000000,
-    )(pixels, columns, rows)
+
+    def sent(piece, bits):
+        return lax.ppermute(piece, "orient", [(i, i ^ bits) for i in range(MEMBERS)])
+
+    templates = [
+        call(
+            template_kernel,
+            shape_of((ORI_DEV, 4 * PAIRS, HALF)),
+            [VMEM] * 3,
+            [pltpu.VMEM((TS * ORI_DEV, TS), jnp.float32)],
+            flops=10000000000,
+        )(group, columns, rows)
+        for group in (pixels, sent(pixels, CORE_BIT))
+    ]
+    spectra = shape_of((4 * PAIRS, HALF))
     image = call(
         image_kernel,
-        (shape_of((4 * PAIRS, HALF)),) * MEMBERS,
+        (spectra, spectra),
         [SMEM] + [VMEM] * 6,
         [pltpu.VMEM((2, TILE, HALF), jnp.bfloat16)],
         flops=1600000000,
     )(member, own_block, right, below, corner, columns, rows)
-    inner = pltpu.VMEM((ORI_DEV * ROWS, TILE), jnp.bfloat16)
-
-    def pair(first, second, kind):
-        return call(
-            pair_kernel,
-            (shape_of((2, ROWS, CORE)), shape_of((2, ROWS, CORE), kind)),
+    far, own = [
+        call(
+            block_kernel,
+            shape_of((2, ROWS, CORE), kind),
             [VMEM] * 5,
-            [inner, inner],
+            [pltpu.VMEM((ORI_DEV * ROWS, TILE), jnp.bfloat16)],
             flops=2000000000,
-        )(image[first], image[second], templates, *tables)
-
-    def sent(piece, bits):
-        return lax.ppermute(piece, "orient", [(i, i ^ bits) for i in range(MEMBERS)])
-
-    far = pair(0, 1, jnp.bfloat16)
-    near = pair(2, 3, jnp.float32)
-    others = [sent(far[0], ORDER[0]), sent(far[1], ORDER[1]), sent(near[0], ORDER[2])]
+        )(spectrum, *templates, *tables)
+        for spectrum, kind in zip(image, (jnp.bfloat16, jnp.float32))
+    ]
     out = shape_of((1, ROWS, CORE), jnp.float32)
-    return call(finish_kernel, (out, out), [VMEM] * 4)(near[1], *others)
+    return call(finish_kernel, (out, out), [VMEM] * 2)(own, sent(far, CHIP_BIT))
 
 
 def solution(mesh):

time: 45.8 us -> 45.6 us (level)
  the two profiles are of different devices: /device:TPU:1 before, /device:TPU:120 now
where the time goes in v5:
time: 45.6 us; the launch traced here: 45.3 us
  starting transfers between devices  23 us (50%)
  Pallas kernels  12.1 us (27%)
  waiting for transfers between devices  9.45 us (21%)
  between operations  0.75 us (2%)
    all_to_all x1, starting transfers between devices, shards(): pixels = lax.all_to_all(spread, 'tile', 0, 0)  13.1 us
    ppermute x3, starting transfers between devices, halo(): return lax.ppermute(block, ('tile', 'orient'), route)  9.74 us
    ppermute x3, waiting for transfers between devices, halo(): return lax.ppermute(block, ('tile', 'orient'), route)  5.23 us
    ppermute x2, waiting for transfers between devices, sent(): lax.ppermute(piece, 'orient', [(i, i ^ bits) for i in range(MEMBERS)])  4.21 us
    pallas_call x2, Pallas kernels, shards(): call(block_kernel, shape_of((2, ROWS, CORE), kind), [VMEM] * 5, [pltpu.VM...  4.02 us
    pallas_call x2, Pallas kernels, shards(): call(template_kernel, shape_of((ORI_DEV, 4 * PAIRS, HALF)), [VMEM] * 3, [...  3.12 us
    pallas_call x1, Pallas kernels, shards(): call(prepare_kernel, (shape_of((TILES, 2 * ORI_DEV, TS)), shape_of((CORE,...  1.81 us
    pallas_call x1, Pallas kernels, shards(): call(load_kernel, tuple((shape_of(array.shape) for array in kept)), [HBM]...  1.46 us
  transfers between devices with their start and end apart: 6, of which 2 were waited for; matrix products, arithmetic and copies ran while one was open for 0% of the time, Pallas kernels for 13%

profile of v5, /device:TPU:120, one launch (start us, length us, event | category | flops | bytes accessed | tf_op | source)
XLA Modules:
  0.0 45.3 jit_solution(15565588521218519908)
XLA Ops:
  0.6 1.8 %shard_map.86 = (bf16[64,16,128]{2,1,0:T(8,128)(2,1)}, bf16[384,128]{1,0:T(8,128)(2,1)S(1)}, bf16[128,384]{1,0:T(8,128)(2,1)S(1)}, bf16[128,128]{1,0:T(8,128)(2,1)S(1)}) custom-call(s32[32]{0:T(128)} %ids_hbm.1, bf16[1,384,384]{2,1,0:T(8,128)(2,1)} %refs_4_.1, bf16[256,256]{1,0:T(8,128)(2,1)} %stack_hbm.1), custom_call_target="tpu_custom_call" | custom-call | bytes 2097152 | tf_op jit(solution)/shard_map/pallas_call | solution.py:230
  2.4 13.1 %all-to-all-start = ((bf16[64,16,128]{2,1,0:T(8,128)(2,1)}), bf16[64,16,128]{2,1,0:T(8,128)(2,1)S(1)}, u32[]{:S(2)}, u32[]{:S(2)}) async-start(bf16[64,16,128]{2,1,0:T(8,128)(2,1)} %get-tuple-element.20), calls=%async_computation | async-start | bytes 524288 | tf_op jit(solution)/shard_map/all_to_all | solution.py:248
  15.5 4.9 %collective-permute-start = (bf16[384,128]{1,0:T(8,128)(2,1)S(1)}, bf16[384,128]{1,0:T(8,128)(2,1)S(1)}, u32[]{:S(2)}, u32[]{:S(2)}) collective-permute-start(bf16[384,128]{1,0:T(8,128)(2,1)S(1)} %get-tuple-element.15), channel_id=1, source_target_pairs={{6,0},{7,1},{4,2},{5,3},{10,4},{11,5},{8,6},{9,7},{14,8},{15,9},{1... | collective-permute-start | bytes 294920 | tf_op jit(solution)/shard_map/ppermute | solution.py:226
  20.4 2.4 %collective-permute-start.1 = (bf16[128,384]{1,0:T(8,128)(2,1)S(1)}, bf16[128,384]{1,0:T(8,128)(2,1)S(1)}, u32[]{:S(2)}, u32[]{:S(2)}) collective-permute-start(bf16[128,384]{1,0:T(8,128)(2,1)S(1)} %get-tuple-element.16), channel_id=1, source_target_pairs={{32,0},{33,1},{34,2},{35,3},{36,4},{37,5},{38,6},{39,7},{40,8},{41... | collective-permute-start | bytes 294920 | tf_op jit(solution)/shard_map/ppermute | solution.py:226
  22.8 2.4 %collective-permute-start.2 = (bf16[128,128]{1,0:T(8,128)(2,1)S(1)}, bf16[128,128]{1,0:T(8,128)(2,1)S(1)}, u32[]{:S(2)}, u32[]{:S(2)}) collective-permute-start(bf16[128,128]{1,0:T(8,128)(2,1)S(1)} %get-tuple-element.13.refs_5_), channel_id=1, source_target_pairs={{38,0},{39,1},{36,2},{37,3},{42,4},{43,5},{40,6},{41,7},{46,8},{47... | collective-permute-start | bytes 98312 | tf_op jit(solution)/shard_map/ppermute | solution.py:226
  25.3 1.5 %shard_map.87 = (bf16[512,512]{1,0:T(8,128)(2,1)S(1)}, bf16[512,448]{1,0:T(8,128)(2,1)S(1)}, bf16[96,256]{1,0:T(8,128)(2,1)S(1)}, bf16[512,384]{1,0:T(8,128)(2,1)S(1)}, bf16[1,384,384]{2,1,0:T(8,128)(2,1)S(1)}) custom-call(bf16[512,512]{1,0:T(8,128)(2,1)} %constant.12.clone.refs_0_, bf16[512,448]{1,0:T(8,128)(2,1)} %constant.13.clone.refs_1_, ...), custom_call_target="tpu_custom_call" | custom-call | flops 1000000000 | bytes 2097152 | tf_op jit(solution)/shard_map/pallas_call | solution.py:250
  26.8 5.2 %collective-permute-done.2.refs_3_ = bf16[128,128]{1,0:T(8,128)(2,1)S(1)} collective-permute-done((bf16[128,128]{1,0:T(8,128)(2,1)S(1)}, bf16[128,128]{1,0:T(8,128)(2,1)S(1)}, u32[]{:S(2)}, u32[]{:S(2)}) %collective-permute-start.2) | collective-permute-done | bytes 32800 | tf_op jit(solution)/shard_map/ppermute | solution.py:226
  32.0 0.0 collective-permute-done.refs_1_
  32.0 0.0 collective-permute-done.1.refs_2_
  32.0 1.0 %shard_map.88 = (bf16[512,256]{1,0:T(8,128)(2,1)S(1)}, bf16[512,256]{1,0:T(8,128)(2,1)S(1)}) custom-call(s32[1]{0:T(128)} %bitcast.member_ref, bf16[1,384,384]{2,1,0:T(8,128)(2,1)S(1)} %get-tuple-element.14.refs_0_, bf16[384,128]{1,0:T(8,128)(2,1)S(1)} %collective-permute-done.refs_1_, bf16[128,384]{1,0:T(8,128)(2,1)S(1)} %collective-permute-done.1.refs_2_, ...), custom_call_target="tpu_custom_call" | custom-call | flops 1600000000 | bytes 2097152 | tf_op jit(solution)/shard_map/pallas_call | solution.py:276
  33.0 0.0 all-to-all-done.pixels_ref
  33.0 0.1 collective-permute-start.3
  33.1 1.6 %shard_map.89.mine_ref = bf16[8,512,256]{2,1,0:T(8,128)(2,1)S(1)} custom-call(bf16[64,16,128]{2,1,0:T(8,128)(2,1)S(1)} %all-to-all-done.pixels_ref, bf16[512,512]{1,0:T(8,128)(2,1)S(1)} %get-tuple-element.17.refs_4_.col_ref, bf16[512,448]{1,0:T(8,128)(2,1)S(1)} %get-tuple-element.18.refs_5_.row_ref), custom_call_target="tpu_custom_call" | custom-call | flops 10000000000 | bytes 2097152 | tf_op jit(solution)/shard_map/pallas_call | solution.py:266
  34.7 0.0 collective-permute-done.3.pixels_ref
  34.7 1.6 %shard_map.90.other_ref = bf16[8,512,256]{2,1,0:T(8,128)(2,1)S(1)} custom-call(bf16[64,16,128]{2,1,0:T(8,128)(2,1)S(1)} %collective-permute-done.3.pixels_ref, bf16[512,512]{1,0:T(8,128)(2,1)S(1)} %get-tuple-element.17.refs_4_.col_ref, bf16[512,448]{1,0:T(8,128)(2,1)S(1)} %get-tuple-element.18.refs_5_.row_ref), custom_call_target="tpu_custom_call" | custom-call | flops 10000000000 | bytes 2097152 | tf_op jit(solution)/shard_map/pallas_call | solution.py:266
  36.2 2.0 %shard_map.92 = bf16[2,96,384]{2,1,0:T(8,128)(2,1)S(1)} custom-call(bf16[512,256]{1,0:T(8,128)(2,1)S(1)} %get-tuple-element.23.image_ref, bf16[8,512,256]{2,1,0:T(8,128)(2,1)S(1)} %shard_map.89.mine_ref, bf16[8,512,256]{2,1,0:T(8,128)(2,1)S(1)} %shard_map.90.other_ref, bf16[96,256]{1,0:T(8,128)(2,1)S(1)} %get-tuple-element.21.inv_row_ref, ...), custom_call_target="tpu_custom_call" | custom-call | flops 2000000000 | bytes 2097152 | tf_op jit(solution)/shard_map/pallas_call | solution.py:284
  38.3 0.1 collective-permute-start.4
  38.4 2.0 %shard_map.91.own_ref = f32[2,96,384]{2,1,0:T(8,128)S(1)} custom-call(bf16[512,256]{1,0:T(8,128)(2,1)S(1)} %get-tuple-element.19.image_ref, bf16[8,512,256]{2,1,0:T(8,128)(2,1)S(1)} %shard_map.89.mine_ref, bf16[8,512,256]{2,1,0:T(8,128)(2,1)S(1)} %shard_map.90.other_ref, bf16[96,256]{1,0:T(8,128)(2,1)S(1)} %get-tuple-element.21.inv_row_ref, ...), custom_call_target="tpu_custom_call" | custom-call | flops 2000000000 | bytes 2097152 | tf_op jit(solution)/shard_map/pallas_call | solution.py:284
  40.4 4.2 %collective-permute-done.4.far_ref = bf16[2,96,384]{2,1,0:T(8,128)(2,1)S(1)} collective-permute-done((bf16[2,96,384]{2,1,0:T(8,128)(2,1)S(1)}, bf16[2,96,384]{2,1,0:T(8,128)(2,1)S(1)}, u32[]{:S(2)}, u32[]{:S(2)}) %collective-permute-start.4) | collective-permute-done | bytes 147488 | tf_op jit(solution)/shard_map/ppermute | solution.py:263
  44.6 0.7 %shard_map.93 = (f32[1,96,384]{2,1,0:T(8,128)}, f32[1,96,384]{2,1,0:T(8,128)}) custom-call(f32[2,96,384]{2,1,0:T(8,128)S(1)} %shard_map.91.own_ref, bf16[2,96,384]{2,1,0:T(8,128)(2,1)S(1)} %collective-permute-done.4.far_ref), custom_call_target="tpu_custom_call" | custom-call | bytes 2097152 | tf_op jit(solution)/shard_map/pallas_call | solution.py:294
Async XLA Ops:
  2.4 30.5 %all-to-all-start = ((bf16[64,16,128]{2,1,0:T(8,128)(2,1)}), bf16[64,16,128]{2,1,0:T(8,128)(2,1)S(1)}, u32[]{:S(2)}, u32[]{:S(2)}) async-start(bf16[64,16,128]{2,1,0:T(8,128)(2,1)} %get-tuple-element.20), calls=%async_computation | async-start | bytes 524288 | tf_op jit(solution)/shard_map/all_to_all | solution.py:248
  15.5 16.5 %collective-permute-start = (bf16[384,128]{1,0:T(8,128)(2,1)S(1)}, bf16[384,128]{1,0:T(8,128)(2,1)S(1)}, u32[]{:S(2)}, u32[]{:S(2)}) collective-permute-start(bf16[384,128]{1,0:T(8,128)(2,1)S(1)} %get-tuple-element.15), channel_id=1, source_target_pairs={{6,0},{7,1},{4,2},{5,3},{10,4},{11,5},{8,6},{9,7},{14,8},{15,9},{1... | collective-permute-start | bytes 294920 | tf_op jit(solution)/shard_map/ppermute | solution.py:226
  20.4 11.6 %collective-permute-start.1 = (bf16[128,384]{1,0:T(8,128)(2,1)S(1)}, bf16[128,384]{1,0:T(8,128)(2,1)S(1)}, u32[]{:S(2)}, u32[]{:S(2)}) collective-permute-start(bf16[128,384]{1,0:T(8,128)(2,1)S(1)} %get-tuple-element.16), channel_id=1, source_target_pairs={{32,0},{33,1},{34,2},{35,3},{36,4},{37,5},{38,6},{39,7},{40,8},{41... | collective-permute-start | bytes 294920 | tf_op jit(solution)/shard_map/ppermute | solution.py:226
  22.8 9.1 %collective-permute-start.2 = (bf16[128,128]{1,0:T(8,128)(2,1)S(1)}, bf16[128,128]{1,0:T(8,128)(2,1)S(1)}, u32[]{:S(2)}, u32[]{:S(2)}) collective-permute-start(bf16[128,128]{1,0:T(8,128)(2,1)S(1)} %get-tuple-element.13.refs_5_), channel_id=1, source_target_pairs={{38,0},{39,1},{36,2},{37,3},{42,4},{43,5},{40,6},{41,7},{46,8},{47... | collective-permute-start | bytes 98312 | tf_op jit(solution)/shard_map/ppermute | solution.py:226
  33.0 1.7 %collective-permute-start.3 = (bf16[64,16,128]{2,1,0:T(8,128)(2,1)S(1)}, bf16[64,16,128]{2,1,0:T(8,128)(2,1)S(1)}, u32[]{:S(2)}, u32[]{:S(2)}) collective-permute-start(bf16[64,16,128]{2,1,0:T(8,128)(2,1)S(1)} %all-to-all-done.pixels_ref), channel_id=1, source_target_pairs={{0,1},{1,0},{2,3},{3,2},{4,5},{5,4},{6,7},{7,6},{8,9},{9,8},{10,11... | collective-permute-start | bytes 786440 | tf_op jit(solution)/shard_map/ppermute | solution.py:263
  38.3 6.3 %collective-permute-start.4 = (bf16[2,96,384]{2,1,0:T(8,128)(2,1)S(1)}, bf16[2,96,384]{2,1,0:T(8,128)(2,1)S(1)}, u32[]{:S(2)}, u32[]{:S(2)}) collective-permute-start(bf16[2,96,384]{2,1,0:T(8,128)(2,1)S(1)} %shard_map.92), channel_id=1, source_target_pairs={{0,2},{1,3},{2,0},{3,1},{4,6},{5,7},{6,4},{7,5},{8,10},{9,11},{10,... | collective-permute-start | bytes 442376 | tf_op jit(solution)/shard_map/ppermute | solution.py:263

commit v6 on v5

--- a/solution.py
+++ b/solution.py
@@ -171,7 +171,7 @@
 
 
 def image_kernel(member_ref, *refs):
-    own_ref, right_ref, below_ref, corner_ref, col_ref, row_ref, far_ref, near_ref, g_ref = refs
+    own_ref, right_ref, below_ref, corner_ref, col_ref, row_ref, _, far_ref, near_ref, g_ref = refs
     image_columns(own_ref, right_ref, below_ref, corner_ref, col_ref, g_ref)
     image_rows(member_ref, row_ref, g_ref, CHIP_BIT, far_ref)
     image_rows(member_ref, row_ref, g_ref, 0, near_ref)
@@ -276,10 +276,10 @@
     image = call(
         image_kernel,
         (spectra, spectra),
-        [SMEM] + [VMEM] * 6,
+        [SMEM] + [VMEM] * 6 + [ANY],
         [pltpu.VMEM((2, TILE, HALF), jnp.bfloat16)],
         flops=1600000000,
-    )(member, own_block, right, below, corner, columns, rows)
+    )(member, own_block, right, below, corner, columns, rows, templates[0])
     far, own = [
         call(
             block_kernel,

time: 45.6 us -> 46 us (level)
  the two profiles are of different devices: /device:TPU:120 before, /device:TPU:1 now
where the time goes in v6:
time: 46 us; the launch traced here: 45.7 us
  starting transfers between devices  22.8 us (50%)
  Pallas kernels  12.4 us (27%)
  waiting for transfers between devices  9.78 us (21%)
  between operations  0.75 us (2%)
    all_to_all x1, starting transfers between devices, shards(): pixels = lax.all_to_all(spread, 'tile', 0, 0)  15.1 us
    all_to_all x1, waiting for transfers between devices, shards(): pixels = lax.all_to_all(spread, 'tile', 0, 0)  6.76 us
    pallas_call x2, Pallas kernels, shards(): call(block_kernel, shape_of((2, ROWS, CORE), kind), [VMEM] * 5, [pltpu.VM...  4.28 us
    ppermute x3, starting transfers between devices, halo(): return lax.ppermute(block, ('tile', 'orient'), route)  3.88 us
    ppermute x2, starting transfers between devices, sent(): lax.ppermute(piece, 'orient', [(i, i ^ bits) for i in range(MEMBERS)])  3.77 us
    pallas_call x2, Pallas kernels, shards(): call(template_kernel, shape_of((ORI_DEV, 4 * PAIRS, HALF)), [VMEM] * 3, [...  3.12 us
    ppermute x2, waiting for transfers between devices, sent(): lax.ppermute(piece, 'orient', [(i, i ^ bits) for i in range(MEMBERS)])  3.01 us
    pallas_call x1, Pallas kernels, shards(): call(prepare_kernel, (shape_of((TILES, 2 * ORI_DEV, TS)), shape_of((CORE,...  1.81 us
  transfers between devices with their start and end apart: 6, of which 2 were waited for; matrix products, arithmetic and copies ran while one was open for 0% of the time, Pallas kernels for 13%

profile of v6, /device:TPU:1, one launch (start us, length us, event | category | flops | bytes accessed | tf_op | source)
XLA Modules:
  0.0 45.7 jit_solution(15999351371601848944)
XLA Ops:
  0.6 1.8 %shard_map.86 = (bf16[64,16,128]{2,1,0:T(8,128)(2,1)}, bf16[384,128]{1,0:T(8,128)(2,1)S(1)}, bf16[128,384]{1,0:T(8,128)(2,1)S(1)}, bf16[128,128]{1,0:T(8,128)(2,1)S(1)}) custom-call(s32[32]{0:T(128)} %ids_hbm.1, bf16[1,384,384]{2,1,0:T(8,128)(2,1)} %refs_4_.1, bf16[256,256]{1,0:T(8,128)(2,1)} %stack_hbm.1), custom_call_target="tpu_custom_call" | custom-call | bytes 2097152 | tf_op jit(solution)/shard_map/pallas_call | solution.py:230
  2.4 15.1 %all-to-all-start = ((bf16[64,16,128]{2,1,0:T(8,128)(2,1)}), bf16[64,16,128]{2,1,0:T(8,128)(2,1)S(1)}, u32[]{:S(2)}, u32[]{:S(2)}) async-start(bf16[64,16,128]{2,1,0:T(8,128)(2,1)} %get-tuple-element.19), calls=%async_computation | async-start | bytes 524288 | tf_op jit(solution)/shard_map/all_to_all | solution.py:248
  17.6 1.3 %collective-permute-start.2 = (bf16[128,128]{1,0:T(8,128)(2,1)S(1)}, bf16[128,128]{1,0:T(8,128)(2,1)S(1)}, u32[]{:S(2)}, u32[]{:S(2)}) collective-permute-start(bf16[128,128]{1,0:T(8,128)(2,1)S(1)} %get-tuple-element.13.refs_5_), channel_id=1, source_target_pairs={{38,0},{39,1},{36,2},{37,3},{42,4},{43,5},{40,6},{41,7},{46,8},{47... | collective-permute-start | bytes 98312 | tf_op jit(solution)/shard_map/ppermute | solution.py:226
  18.9 1.3 %collective-permute-start = (bf16[384,128]{1,0:T(8,128)(2,1)S(1)}, bf16[384,128]{1,0:T(8,128)(2,1)S(1)}, u32[]{:S(2)}, u32[]{:S(2)}) collective-permute-start(bf16[384,128]{1,0:T(8,128)(2,1)S(1)} %get-tuple-element.15), channel_id=1, source_target_pairs={{6,0},{7,1},{4,2},{5,3},{10,4},{11,5},{8,6},{9,7},{14,8},{15,9},{1... | collective-permute-start | bytes 294920 | tf_op jit(solution)/shard_map/ppermute | solution.py:226
  20.2 1.3 %collective-permute-start.1 = (bf16[128,384]{1,0:T(8,128)(2,1)S(1)}, bf16[128,384]{1,0:T(8,128)(2,1)S(1)}, u32[]{:S(2)}, u32[]{:S(2)}) collective-permute-start(bf16[128,384]{1,0:T(8,128)(2,1)S(1)} %get-tuple-element.16), channel_id=1, source_target_pairs={{32,0},{33,1},{34,2},{35,3},{36,4},{37,5},{38,6},{39,7},{40,8},{41... | collective-permute-start | bytes 294920 | tf_op jit(solution)/shard_map/ppermute | solution.py:226
  21.5 1.5 %shard_map.87 = (bf16[512,512]{1,0:T(8,128)(2,1)S(1)}, bf16[512,448]{1,0:T(8,128)(2,1)S(1)}, bf16[96,256]{1,0:T(8,128)(2,1)S(1)}, bf16[512,384]{1,0:T(8,128)(2,1)S(1)}, bf16[1,384,384]{2,1,0:T(8,128)(2,1)S(1)}) custom-call(bf16[512,512]{1,0:T(8,128)(2,1)} %constant.12.clone.refs_0_, bf16[512,448]{1,0:T(8,128)(2,1)} %constant.13.clone.refs_1_, ...), custom_call_target="tpu_custom_call" | custom-call | flops 1000000000 | bytes 2097152 | tf_op jit(solution)/shard_map/pallas_call | solution.py:250
  22.9 6.8 %all-to-all-done.pixels_ref = bf16[64,16,128]{2,1,0:T(8,128)(2,1)S(1)} async-done(((bf16[64,16,128]{2,1,0:T(8,128)(2,1)}), bf16[64,16,128]{2,1,0:T(8,128)(2,1)S(1)}, u32[]{:S(2)}, u32[]{:S(2)}) %all-to-all-start) | async-done | bytes 262176 | tf_op jit(solution)/shard_map/all_to_all | solution.py:248
  29.7 3.4 %collective-permute-start.3 = (bf16[64,16,128]{2,1,0:T(8,128)(2,1)S(1)}, bf16[64,16,128]{2,1,0:T(8,128)(2,1)S(1)}, u32[]{:S(2)}, u32[]{:S(2)}) collective-permute-start(bf16[64,16,128]{2,1,0:T(8,128)(2,1)S(1)} %all-to-all-done.pixels_ref), channel_id=1, source_target_pairs={{0,1},{1,0},{2,3},{3,2},{4,5},{5,4},{6,7},{7,6},{8,9},{9,8},{10,11... | collective-permute-start | bytes 786440 | tf_op jit(solution)/shard_map/ppermute | solution.py:263
  33.1 1.6 %shard_map.88.refs_6_.mine_ref = bf16[8,512,256]{2,1,0:T(8,128)(2,1)S(1)} custom-call(bf16[64,16,128]{2,1,0:T(8,128)(2,1)S(1)} %all-to-all-done.pixels_ref, bf16[512,512]{1,0:T(8,128)(2,1)S(1)} %get-tuple-element.17.col_ref.refs_4_, bf16[512,448]{1,0:T(8,128)(2,1)S(1)} %get-tuple-element.18.row_ref.refs_5_), custom_call_target="tpu_custom_call" | custom-call | flops 10000000000 | bytes 2097152 | tf_op jit(solution)/shard_map/pallas_call | solution.py:266
  34.6 0.0 collective-permute-done.2.refs_3_
  34.6 0.0 collective-permute-done.refs_1_
  34.7 0.0 collective-permute-done.1.refs_2_
  34.7 1.0 %shard_map.89 = (bf16[512,256]{1,0:T(8,128)(2,1)S(1)}, bf16[512,256]{1,0:T(8,128)(2,1)S(1)}) custom-call(s32[1]{0:T(128)} %bitcast.member_ref, bf16[1,384,384]{2,1,0:T(8,128)(2,1)S(1)} %get-tuple-element.14.refs_0_, bf16[384,128]{1,0:T(8,128)(2,1)S(1)} %collective-permute-done.refs_1_, bf16[128,384]{1,0:T(8,128)(2,1)S(1)} %collective-permute-done.1.refs_2_, ...), custom_call_target="tpu_custom_call" | custom-call | flops 1600000000 | bytes 2097152 | tf_op jit(solution)/shard_map/pallas_call | solution.py:276
  35.7 0.0 collective-permute-done.3.pixels_ref
  35.7 1.6 %shard_map.90.other_ref = bf16[8,512,256]{2,1,0:T(8,128)(2,1)S(1)} custom-call(bf16[64,16,128]{2,1,0:T(8,128)(2,1)S(1)} %collective-permute-done.3.pixels_ref, bf16[512,512]{1,0:T(8,128)(2,1)S(1)} %get-tuple-element.17.col_ref.refs_4_, bf16[512,448]{1,0:T(8,128)(2,1)S(1)} %get-tuple-element.18.row_ref.refs_5_), custom_call_target="tpu_custom_call" | custom-call | flops 10000000000 | bytes 2097152 | tf_op jit(solution)/shard_map/pallas_call | solution.py:266
  37.2 2.1 %shard_map.92 = bf16[2,96,384]{2,1,0:T(8,128)(2,1)S(1)} custom-call(bf16[512,256]{1,0:T(8,128)(2,1)S(1)} %get-tuple-element.23.image_ref, bf16[8,512,256]{2,1,0:T(8,128)(2,1)S(1)} %shard_map.88.refs_6_.mine_ref, bf16[8,512,256]{2,1,0:T(8,128)(2,1)S(1)} %shard_map.90.other_ref, bf16[96,256]{1,0:T(8,128)(2,1)S(1)} %get-tuple-element.21.inv_row_ref, ...), custom_call_target="tpu_custom_call" | custom-call | flops 2000000000 | bytes 2097152 | tf_op jit(solution)/shard_map/pallas_call | solution.py:284
  39.4 0.4 collective-permute-start.4
  39.8 2.1 %shard_map.91.own_ref = f32[2,96,384]{2,1,0:T(8,128)S(1)} custom-call(bf16[512,256]{1,0:T(8,128)(2,1)S(1)} %get-tuple-element.20.image_ref, bf16[8,512,256]{2,1,0:T(8,128)(2,1)S(1)} %shard_map.88.refs_6_.mine_ref, bf16[8,512,256]{2,1,0:T(8,128)(2,1)S(1)} %shard_map.90.other_ref, bf16[96,256]{1,0:T(8,128)(2,1)S(1)} %get-tuple-element.21.inv_row_ref, ...), custom_call_target="tpu_custom_call" | custom-call | flops 2000000000 | bytes 2097152 | tf_op jit(solution)/shard_map/pallas_call | solution.py:284
  41.9 3.0 %collective-permute-done.4.far_ref = bf16[2,96,384]{2,1,0:T(8,128)(2,1)S(1)} collective-permute-done((bf16[2,96,384]{2,1,0:T(8,128)(2,1)S(1)}, bf16[2,96,384]{2,1,0:T(8,128)(2,1)S(1)}, u32[]{:S(2)}, u32[]{:S(2)}) %collective-permute-start.4) | collective-permute-done | bytes 147488 | tf_op jit(solution)/shard_map/ppermute | solution.py:263
  45.0 0.7 %shard_map.93 = (f32[1,96,384]{2,1,0:T(8,128)}, f32[1,96,384]{2,1,0:T(8,128)}) custom-call(f32[2,96,384]{2,1,0:T(8,128)S(1)} %shard_map.91.own_ref, bf16[2,96,384]{2,1,0:T(8,128)(2,1)S(1)} %collective-permute-done.4.far_ref), custom_call_target="tpu_custom_call" | custom-call | bytes 2097152 | tf_op jit(solution)/shard_map/pallas_call | solution.py:294
Async XLA Ops:
  2.4 27.3 %all-to-all-start = ((bf16[64,16,128]{2,1,0:T(8,128)(2,1)}), bf16[64,16,128]{2,1,0:T(8,128)(2,1)S(1)}, u32[]{:S(2)}, u32[]{:S(2)}) async-start(bf16[64,16,128]{2,1,0:T(8,128)(2,1)} %get-tuple-element.19), calls=%async_computation | async-start | bytes 524288 | tf_op jit(solution)/shard_map/all_to_all | solution.py:248
  17.6 17.1 %collective-permute-start.2 = (bf16[128,128]{1,0:T(8,128)(2,1)S(1)}, bf16[128,128]{1,0:T(8,128)(2,1)S(1)}, u32[]{:S(2)}, u32[]{:S(2)}) collective-permute-start(bf16[128,128]{1,0:T(8,128)(2,1)S(1)} %get-tuple-element.13.refs_5_), channel_id=1, source_target_pairs={{38,0},{39,1},{36,2},{37,3},{42,4},{43,5},{40,6},{41,7},{46,8},{47... | collective-permute-start | bytes 98312 | tf_op jit(solution)/shard_map/ppermute | solution.py:226
  18.9 15.8 %collective-permute-start = (bf16[384,128]{1,0:T(8,128)(2,1)S(1)}, bf16[384,128]{1,0:T(8,128)(2,1)S(1)}, u32[]{:S(2)}, u32[]{:S(2)}) collective-permute-start(bf16[384,128]{1,0:T(8,128)(2,1)S(1)} %get-tuple-element.15), channel_id=1, source_target_pairs={{6,0},{7,1},{4,2},{5,3},{10,4},{11,5},{8,6},{9,7},{14,8},{15,9},{1... | collective-permute-start | bytes 294920 | tf_op jit(solution)/shard_map/ppermute | solution.py:226
  20.2 14.5 %collective-permute-start.1 = (bf16[128,384]{1,0:T(8,128)(2,1)S(1)}, bf16[128,384]{1,0:T(8,128)(2,1)S(1)}, u32[]{:S(2)}, u32[]{:S(2)}) collective-permute-start(bf16[128,384]{1,0:T(8,128)(2,1)S(1)} %get-tuple-element.16), channel_id=1, source_target_pairs={{32,0},{33,1},{34,2},{35,3},{36,4},{37,5},{38,6},{39,7},{40,8},{41... | collective-permute-start | bytes 294920 | tf_op jit(solution)/shard_map/ppermute | solution.py:226
  29.7 6.0 %collective-permute-start.3 = (bf16[64,16,128]{2,1,0:T(8,128)(2,1)S(1)}, bf16[64,16,128]{2,1,0:T(8,128)(2,1)S(1)}, u32[]{:S(2)}, u32[]{:S(2)}) collective-permute-start(bf16[64,16,128]{2,1,0:T(8,128)(2,1)S(1)} %all-to-all-done.pixels_ref), channel_id=1, source_target_pairs={{0,1},{1,0},{2,3},{3,2},{4,5},{5,4},{6,7},{7,6},{8,9},{9,8},{10,11... | collective-permute-start | bytes 786440 | tf_op jit(solution)/shard_map/ppermute | solution.py:263
  39.4 5.6 %collective-permute-start.4 = (bf16[2,96,384]{2,1,0:T(8,128)(2,1)S(1)}, bf16[2,96,384]{2,1,0:T(8,128)(2,1)S(1)}, u32[]{:S(2)}, u32[]{:S(2)}) collective-permute-start(bf16[2,96,384]{2,1,0:T(8,128)(2,1)S(1)} %shard_map.92), channel_id=1, source_target_pairs={{0,2},{1,3},{2,0},{3,1},{4,6},{5,7},{6,4},{7,5},{8,10},{9,11},{10,... | collective-permute-start | bytes 442376 | tf_op jit(solution)/shard_map/ppermute | solution.py:263

commit v7 on v6

--- a/solution.py
+++ b/solution.py
@@ -104,17 +104,21 @@
         load.wait()
 
 
-def template_kernel(pixels_ref, col_ref, row_ref, out_ref, shape_ref):
+def normalize_kernel(pixels_ref, out_ref, shape_ref):
     values = pixels_ref[...].astype(jnp.float32).reshape(TS, ORI_DEV, TS)
     mean = jnp.sum(jnp.sum(values, 0), 1, keepdims=True) / (TS * TS)
     centered = values - mean[None]
     square = jnp.sum(jnp.sum(centered * centered, 0), 1, keepdims=True) / (TS * TS)
     spread = jnp.sqrt(square + 1e-06) * TS
     shape_ref[...] = (centered / spread[None]).reshape(TS * ORI_DEV, TS)
-    shapes = [shape_ref[pl.ds(o, TS, stride=ORI_DEV), :].astype(jnp.bfloat16) for o in range(ORI_DEV)]
+    for o in range(ORI_DEV):
+        out_ref[o * TS : (o + 1) * TS] = shape_ref[pl.ds(o, TS, stride=ORI_DEV), :].astype(jnp.bfloat16)
+
+
+def template_kernel(shapes_ref, col_ref, row_ref, out_ref):
     half = ORI_DEV // 2
     for start in (0, half):
-        together = jnp.concatenate(shapes[start : start + half], 0)
+        together = shapes_ref[start * TS : (start + half) * TS]
         g = dot(together, col_ref[:TS]).astype(jnp.bfloat16)
         for o in range(half):
             mine = g[o * TS : (o + 1) * TS]
@@ -171,13 +175,17 @@
 
 
 def image_kernel(member_ref, *refs):
-    own_ref, right_ref, below_ref, corner_ref, col_ref, row_ref, _, far_ref, near_ref, g_ref = refs
+    own_ref, right_ref, below_ref, corner_ref, col_ref, row_ref, _, far_ref, g_ref = refs
     image_columns(own_ref, right_ref, below_ref, corner_ref, col_ref, g_ref)
     image_rows(member_ref, row_ref, g_ref, CHIP_BIT, far_ref)
-    image_rows(member_ref, row_ref, g_ref, 0, near_ref)
-
-
-def block_kernel(image_ref, mine_ref, other_ref, inv_row_ref, inv_col_ref, out_ref, inner_ref):
+
+
+def far_kernel(image_ref, mine_ref, other_ref, inv_row_ref, inv_col_ref, out_ref, inner_ref):
+    block(image_ref, (mine_ref, other_ref), inv_row_ref, inv_col_ref, out_ref, inner_ref)
+
+
+def own_kernel(member_ref, row_ref, g_ref, mine_ref, other_ref, inv_row_ref, inv_col_ref, out_ref, image_ref, inner_ref):
+    image_rows(member_ref, row_ref, g_ref, 0, image_ref)
     block(image_ref, (mine_ref, other_ref), inv_row_ref, inv_col_ref, out_ref, inner_ref)
 
 
@@ -262,34 +270,44 @@
     def sent(piece, bits):
         return lax.ppermute(piece, "orient", [(i, i ^ bits) for i in range(MEMBERS)])
 
+    shapes = call(
+        normalize_kernel,
+        shape_of((ORI_DEV * TS, TS)),
+        [VMEM],
+        [pltpu.VMEM((TS * ORI_DEV, TS), jnp.float32)],
+        flops=100000000,
+    )(pixels)
     templates = [
         call(
             template_kernel,
             shape_of((ORI_DEV, 4 * PAIRS, HALF)),
             [VMEM] * 3,
-            [pltpu.VMEM((TS * ORI_DEV, TS), jnp.float32)],
             flops=10000000000,
         )(group, columns, rows)
-        for group in (pixels, sent(pixels, CORE_BIT))
+        for group in (shapes, sent(shapes, CORE_BIT))
     ]
-    spectra = shape_of((4 * PAIRS, HALF))
-    image = call(
+    spectrum = shape_of((4 * PAIRS, HALF))
+    image, g = call(
         image_kernel,
-        (spectra, spectra),
+        (spectrum, shape_of((2, TILE, HALF))),
         [SMEM] + [VMEM] * 6 + [ANY],
-        [pltpu.VMEM((2, TILE, HALF), jnp.bfloat16)],
         flops=1600000000,
     )(member, own_block, right, below, corner, columns, rows, templates[0])
-    far, own = [
-        call(
-            block_kernel,
-            shape_of((2, ROWS, CORE), kind),
-            [VMEM] * 5,
-            [pltpu.VMEM((ORI_DEV * ROWS, TILE), jnp.bfloat16)],
-            flops=2000000000,
-        )(spectrum, *templates, *tables)
-        for spectrum, kind in zip(image, (jnp.bfloat16, jnp.float32))
-    ]
+    inner = pltpu.VMEM((ORI_DEV * ROWS, TILE), jnp.bfloat16)
+    far = call(
+        far_kernel,
+        shape_of((2, ROWS, CORE)),
+        [VMEM] * 5,
+        [inner],
+        flops=2000000000,
+    )(image, *templates, *tables)
+    own = call(
+        own_kernel,
+        shape_of((2, ROWS, CORE), jnp.float32),
+        [SMEM] + [VMEM] * 6,
+        [pltpu.VMEM((4 * PAIRS, HALF), jnp.bfloat16), inner],
+        flops=2000000000,
+    )(member, rows, g, *templates, *tables)
     out = shape_of((1, ROWS, CORE), jnp.float32)
     return call(finish_kernel, (out, out), [VMEM] * 2)(own, sent(far, CHIP_BIT))
 

time: 46 us -> 45.5 us (0.989)
  waiting for transfers between devices: 9.78 us -> 9.25 us
    ppermute x2, waiting for transfers between devices: 3.01 us -> 2.48 us  [sent(): lax.ppermute(piece, 'orient', [(i, i ^ bits) for i in range(MEMBERS)])]
    pallas_call x5 -> x6, Pallas kernels: 8.39 us -> 8.4 us  [the longest x1 2.69 us: shards(): call(own_kernel, shape_of((2, ROWS, CORE), jnp.float32), [SMEM] + [VMEM]...]
  transfers between devices with their start and end apart: 6 -> 6, of which waited for: 2 -> 2; matrix products, arithmetic and copies ran while one was open for 0% -> 0% of each run, Pallas kernels for 13% -> 15%
where the time goes in v7:
time: 45.5 us; the launch traced here: 45.3 us
  starting transfers between devices  22.9 us (50%)
  Pallas kernels  12.4 us (27%)
  waiting for transfers between devices  9.25 us (20%)
  between operations  0.76 us (2%)
    all_to_all x1, starting transfers between devices, shards(): pixels = lax.all_to_all(spread, 'tile', 0, 0)  15.1 us
    all_to_all x1, waiting for transfers between devices, shards(): pixels = lax.all_to_all(spread, 'tile', 0, 0)  6.76 us
    ppermute x3, starting transfers between devices, halo(): return lax.ppermute(block, ('tile', 'orient'), route)  3.88 us
    ppermute x2, starting transfers between devices, sent(): lax.ppermute(piece, 'orient', [(i, i ^ bits) for i in range(MEMBERS)])  3.86 us
    pallas_call x1, Pallas kernels, shards(): call(own_kernel, shape_of((2, ROWS, CORE), jnp.float32), [SMEM] + [VMEM]...  2.69 us
    ppermute x2, waiting for transfers between devices, sent(): lax.ppermute(piece, 'orient', [(i, i ^ bits) for i in range(MEMBERS)])  2.48 us
    pallas_call x2, Pallas kernels, shards(): call(template_kernel, shape_of((ORI_DEV, 4 * PAIRS, HALF)), [VMEM] * 3, f...  2.21 us
    pallas_call x1, Pallas kernels, shards(): call(far_kernel, shape_of((2, ROWS, CORE)), [VMEM] * 5, [inner], flops=20...  2.1 us
  transfers between devices with their start and end apart: 6, of which 2 were waited for; matrix products, arithmetic and copies ran while one was open for 0% of the time, Pallas kernels for 15%

profile of v7, /device:TPU:1, one launch (start us, length us, event | category | flops | bytes accessed | tf_op | source)
XLA Modules:
  0.0 45.3 jit_solution(2454581233441300145)
XLA Ops:
  0.6 1.8 %shard_map.86 = (bf16[64,16,128]{2,1,0:T(8,128)(2,1)}, bf16[384,128]{1,0:T(8,128)(2,1)S(1)}, bf16[128,384]{1,0:T(8,128)(2,1)S(1)}, bf16[128,128]{1,0:T(8,128)(2,1)S(1)}) custom-call(s32[32]{0:T(128)} %ids_hbm.1, bf16[1,384,384]{2,1,0:T(8,128)(2,1)} %refs_4_.1, bf16[256,256]{1,0:T(8,128)(2,1)} %stack_hbm.1), custom_call_target="tpu_custom_call" | custom-call | bytes 2097152 | tf_op jit(solution)/shard_map/pallas_call | solution.py:238
  2.4 15.1 %all-to-all-start = ((bf16[64,16,128]{2,1,0:T(8,128)(2,1)}), bf16[64,16,128]{2,1,0:T(8,128)(2,1)S(1)}, u32[]{:S(2)}, u32[]{:S(2)}) async-start(bf16[64,16,128]{2,1,0:T(8,128)(2,1)} %get-tuple-element.19), calls=%async_computation | async-start | bytes 524288 | tf_op jit(solution)/shard_map/all_to_all | solution.py:256
  17.6 1.3 %collective-permute-start.2 = (bf16[128,128]{1,0:T(8,128)(2,1)S(1)}, bf16[128,128]{1,0:T(8,128)(2,1)S(1)}, u32[]{:S(2)}, u32[]{:S(2)}) collective-permute-start(bf16[128,128]{1,0:T(8,128)(2,1)S(1)} %get-tuple-element.13.refs_5_), channel_id=1, source_target_pairs={{38,0},{39,1},{36,2},{37,3},{42,4},{43,5},{40,6},{41,7},{46,8},{47... | collective-permute-start | bytes 98312 | tf_op jit(solution)/shard_map/ppermute | solution.py:234
  18.9 1.3 %collective-permute-start = (bf16[384,128]{1,0:T(8,128)(2,1)S(1)}, bf16[384,128]{1,0:T(8,128)(2,1)S(1)}, u32[]{:S(2)}, u32[]{:S(2)}) collective-permute-start(bf16[384,128]{1,0:T(8,128)(2,1)S(1)} %get-tuple-element.16), channel_id=1, source_target_pairs={{6,0},{7,1},{4,2},{5,3},{10,4},{11,5},{8,6},{9,7},{14,8},{15,9},{1... | collective-permute-start | bytes 294920 | tf_op jit(solution)/shard_map/ppermute | solution.py:234
  20.2 1.3 %collective-permute-start.1 = (bf16[128,384]{1,0:T(8,128)(2,1)S(1)}, bf16[128,384]{1,0:T(8,128)(2,1)S(1)}, u32[]{:S(2)}, u32[]{:S(2)}) collective-permute-start(bf16[128,384]{1,0:T(8,128)(2,1)S(1)} %get-tuple-element.17), channel_id=1, source_target_pairs={{32,0},{33,1},{34,2},{35,3},{36,4},{37,5},{38,6},{39,7},{40,8},{41... | collective-permute-start | bytes 294920 | tf_op jit(solution)/shard_map/ppermute | solution.py:234
  21.5 1.5 %shard_map.87 = (bf16[512,512]{1,0:T(8,128)(2,1)S(1)}, bf16[512,448]{1,0:T(8,128)(2,1)S(1)}, bf16[96,256]{1,0:T(8,128)(2,1)S(1)}, bf16[512,384]{1,0:T(8,128)(2,1)S(1)}, bf16[1,384,384]{2,1,0:T(8,128)(2,1)S(1)}) custom-call(bf16[512,512]{1,0:T(8,128)(2,1)} %constant.12.clone.refs_0_, bf16[512,448]{1,0:T(8,128)(2,1)} %constant.13.clone.refs_1_, ...), custom_call_target="tpu_custom_call" | custom-call | flops 1000000000 | bytes 2097152 | tf_op jit(solution)/shard_map/pallas_call | solution.py:258
  22.9 6.8 %all-to-all-done.pixels_ref = bf16[64,16,128]{2,1,0:T(8,128)(2,1)S(1)} async-done(((bf16[64,16,128]{2,1,0:T(8,128)(2,1)}), bf16[64,16,128]{2,1,0:T(8,128)(2,1)S(1)}, u32[]{:S(2)}, u32[]{:S(2)}) %all-to-all-start) | async-done | bytes 262176 | tf_op jit(solution)/shard_map/all_to_all | solution.py:256
  29.7 0.5 %shard_map.88.shapes_ref = bf16[1024,128]{1,0:T(8,128)(2,1)S(1)} custom-call(bf16[64,16,128]{2,1,0:T(8,128)(2,1)S(1)} %all-to-all-done.pixels_ref), custom_call_target="tpu_custom_call" | custom-call | flops 100000000 | bytes 2097152 | tf_op jit(solution)/shard_map/pallas_call | solution.py:273
  30.3 3.5 %collective-permute-start.3 = (bf16[1024,128]{1,0:T(8,128)(2,1)S(1)}, bf16[1024,128]{1,0:T(8,128)(2,1)S(1)}, u32[]{:S(2)}, u32[]{:S(2)}) collective-permute-start(bf16[1024,128]{1,0:T(8,128)(2,1)S(1)} %shard_map.88.shapes_ref), channel_id=1, source_target_pairs={{0,1},{1,0},{2,3},{3,2},{4,5},{5,4},{6,7},{7,6},{8,9},{9,8},{10,11... | collective-permute-start | bytes 786440 | tf_op jit(solution)/shard_map/ppermute | solution.py:271
  33.7 1.1 %shard_map.89.refs_6_.mine_ref = bf16[8,512,256]{2,1,0:T(8,128)(2,1)S(1)} custom-call(bf16[1024,128]{1,0:T(8,128)(2,1)S(1)} %shard_map.88.shapes_ref, bf16[512,512]{1,0:T(8,128)(2,1)S(1)} %get-tuple-element.18.col_ref.refs_4_, bf16[512,448]{1,0:T(8,128)(2,1)S(1)} %get-tuple-element.14.row_ref.refs_5_), custom_call_target="tpu_custom_call" | custom-call | flops 10000000000 | bytes 2097152 | tf_op jit(solution)/shard_map/pallas_call | solution.py:281
  34.8 0.0 collective-permute-done.2.refs_3_
  34.8 0.0 collective-permute-done.refs_1_
  34.8 0.0 collective-permute-done.1.refs_2_
  34.8 0.9 %shard_map.90 = (bf16[512,256]{1,0:T(8,128)(2,1)S(1)}, bf16[2,512,256]{2,1,0:T(8,128)(2,1)S(1)}) custom-call(s32[1]{0:T(128)} %bitcast.member_ref, bf16[1,384,384]{2,1,0:T(8,128)(2,1)S(1)} %get-tuple-element.15.refs_0_, bf16[384,128]{1,0:T(8,128)(2,1)S(1)} %collective-permute-done.refs_1_, bf16[128,384]{1,0:T(8,128)(2,1)S(1)} %collective-permute-done.1.refs_2_, ...), custom_call_target="tpu_custom_call" | custom-call | flops 1600000000 | bytes 2097152 | tf_op jit(solution)/shard_map/pallas_call | solution.py:290
  35.7 0.0 collective-permute-done.3.shapes_ref
  35.7 1.1 %shard_map.91.other_ref = bf16[8,512,256]{2,1,0:T(8,128)(2,1)S(1)} custom-call(bf16[1024,128]{1,0:T(8,128)(2,1)S(1)} %collective-permute-done.3.shapes_ref, bf16[512,512]{1,0:T(8,128)(2,1)S(1)} %get-tuple-element.18.col_ref.refs_4_, bf16[512,448]{1,0:T(8,128)(2,1)S(1)} %get-tuple-element.14.row_ref.refs_5_), custom_call_target="tpu_custom_call" | custom-call | flops 10000000000 | bytes 2097152 | tf_op jit(solution)/shard_map/pallas_call | solution.py:281
  36.8 2.1 %shard_map.93 = bf16[2,96,384]{2,1,0:T(8,128)(2,1)S(1)} custom-call(bf16[512,256]{1,0:T(8,128)(2,1)S(1)} %get-tuple-element.23.image_ref, bf16[8,512,256]{2,1,0:T(8,128)(2,1)S(1)} %shard_map.89.refs_6_.mine_ref, bf16[8,512,256]{2,1,0:T(8,128)(2,1)S(1)} %shard_map.91.other_ref, bf16[96,256]{1,0:T(8,128)(2,1)S(1)} %get-tuple-element.21.inv_row_ref, ...), custom_call_target="tpu_custom_call" | custom-call | flops 2000000000 | bytes 2097152 | tf_op jit(solution)/shard_map/pallas_call | solution.py:297
  39.0 0.4 collective-permute-start.4
  39.4 2.7 %shard_map.92.own_ref = f32[2,96,384]{2,1,0:T(8,128)S(1)} custom-call(s32[1]{0:T(128)} %bitcast.member_ref, bf16[512,448]{1,0:T(8,128)(2,1)S(1)} %get-tuple-element.14.row_ref.refs_5_, bf16[2,512,256]{2,1,0:T(8,128)(2,1)S(1)} %get-tuple-element.20.g_ref, bf16[8,512,256]{2,1,0:T(8,128)(2,1)S(1)} %shard_map.89.refs_6_.mine_ref, ...), custom_call_target="tpu_custom_call" | custom-call | flops 2000000000 | bytes 2097152 | tf_op jit(solution)/shard_map/pallas_call | solution.py:304
  42.0 2.5 %collective-permute-done.4.far_ref = bf16[2,96,384]{2,1,0:T(8,128)(2,1)S(1)} collective-permute-done((bf16[2,96,384]{2,1,0:T(8,128)(2,1)S(1)}, bf16[2,96,384]{2,1,0:T(8,128)(2,1)S(1)}, u32[]{:S(2)}, u32[]{:S(2)}) %collective-permute-start.4) | collective-permute-done | bytes 147488 | tf_op jit(solution)/shard_map/ppermute | solution.py:271
  44.5 0.7 %shard_map.94 = (f32[1,96,384]{2,1,0:T(8,128)}, f32[1,96,384]{2,1,0:T(8,128)}) custom-call(f32[2,96,384]{2,1,0:T(8,128)S(1)} %shard_map.92.own_ref, bf16[2,96,384]{2,1,0:T(8,128)(2,1)S(1)} %collective-permute-done.4.far_ref), custom_call_target="tpu_custom_call" | custom-call | bytes 2097152 | tf_op jit(solution)/shard_map/pallas_call | solution.py:312
Async XLA Ops:
  2.4 27.3 %all-to-all-start = ((bf16[64,16,128]{2,1,0:T(8,128)(2,1)}), bf16[64,16,128]{2,1,0:T(8,128)(2,1)S(1)}, u32[]{:S(2)}, u32[]{:S(2)}) async-start(bf16[64,16,128]{2,1,0:T(8,128)(2,1)} %get-tuple-element.19), calls=%async_computation | async-start | bytes 524288 | tf_op jit(solution)/shard_map/all_to_all | solution.py:256
  17.6 17.2 %collective-permute-start.2 = (bf16[128,128]{1,0:T(8,128)(2,1)S(1)}, bf16[128,128]{1,0:T(8,128)(2,1)S(1)}, u32[]{:S(2)}, u32[]{:S(2)}) collective-permute-start(bf16[128,128]{1,0:T(8,128)(2,1)S(1)} %get-tuple-element.13.refs_5_), channel_id=1, source_target_pairs={{38,0},{39,1},{36,2},{37,3},{42,4},{43,5},{40,6},{41,7},{46,8},{47... | collective-permute-start | bytes 98312 | tf_op jit(solution)/shard_map/ppermute | solution.py:234
  18.9 16.0 %collective-permute-start = (bf16[384,128]{1,0:T(8,128)(2,1)S(1)}, bf16[384,128]{1,0:T(8,128)(2,1)S(1)}, u32[]{:S(2)}, u32[]{:S(2)}) collective-permute-start(bf16[384,128]{1,0:T(8,128)(2,1)S(1)} %get-tuple-element.16), channel_id=1, source_target_pairs={{6,0},{7,1},{4,2},{5,3},{10,4},{11,5},{8,6},{9,7},{14,8},{15,9},{1... | collective-permute-start | bytes 294920 | tf_op jit(solution)/shard_map/ppermute | solution.py:234
  20.2 14.7 %collective-permute-start.1 = (bf16[128,384]{1,0:T(8,128)(2,1)S(1)}, bf16[128,384]{1,0:T(8,128)(2,1)S(1)}, u32[]{:S(2)}, u32[]{:S(2)}) collective-permute-start(bf16[128,384]{1,0:T(8,128)(2,1)S(1)} %get-tuple-element.17), channel_id=1, source_target_pairs={{32,0},{33,1},{34,2},{35,3},{36,4},{37,5},{38,6},{39,7},{40,8},{41... | collective-permute-start | bytes 294920 | tf_op jit(solution)/shard_map/ppermute | solution.py:234
  30.3 5.4 %collective-permute-start.3 = (bf16[1024,128]{1,0:T(8,128)(2,1)S(1)}, bf16[1024,128]{1,0:T(8,128)(2,1)S(1)}, u32[]{:S(2)}, u32[]{:S(2)}) collective-permute-start(bf16[1024,128]{1,0:T(8,128)(2,1)S(1)} %shard_map.88.shapes_ref), channel_id=1, source_target_pairs={{0,1},{1,0},{2,3},{3,2},{4,5},{5,4},{6,7},{7,6},{8,9},{9,8},{10,11... | collective-permute-start | bytes 786440 | tf_op jit(solution)/shard_map/ppermute | solution.py:271
  39.0 5.6 %collective-permute-start.4 = (bf16[2,96,384]{2,1,0:T(8,128)(2,1)S(1)}, bf16[2,96,384]{2,1,0:T(8,128)(2,1)S(1)}, u32[]{:S(2)}, u32[]{:S(2)}) collective-permute-start(bf16[2,96,384]{2,1,0:T(8,128)(2,1)S(1)} %shard_map.93), channel_id=1, source_target_pairs={{0,2},{1,3},{2,0},{3,1},{4,6},{5,7},{6,4},{7,5},{8,10},{9,11},{10,... | collective-permute-start | bytes 442376 | tf_op jit(solution)/shard_map/ppermute | solution.py:271

commit v8 on v7

--- a/solution.py
+++ b/solution.py
@@ -104,21 +104,17 @@
         load.wait()
 
 
-def normalize_kernel(pixels_ref, out_ref, shape_ref):
+def template_kernel(pixels_ref, col_ref, row_ref, out_ref, shape_ref):
     values = pixels_ref[...].astype(jnp.float32).reshape(TS, ORI_DEV, TS)
     mean = jnp.sum(jnp.sum(values, 0), 1, keepdims=True) / (TS * TS)
     centered = values - mean[None]
     square = jnp.sum(jnp.sum(centered * centered, 0), 1, keepdims=True) / (TS * TS)
     spread = jnp.sqrt(square + 1e-06) * TS
     shape_ref[...] = (centered / spread[None]).reshape(TS * ORI_DEV, TS)
-    for o in range(ORI_DEV):
-        out_ref[o * TS : (o + 1) * TS] = shape_ref[pl.ds(o, TS, stride=ORI_DEV), :].astype(jnp.bfloat16)
-
-
-def template_kernel(shapes_ref, col_ref, row_ref, out_ref):
+    shapes = [shape_ref[pl.ds(o, TS, stride=ORI_DEV), :].astype(jnp.bfloat16) for o in range(ORI_DEV)]
     half = ORI_DEV // 2
     for start in (0, half):
-        together = shapes_ref[start * TS : (start + half) * TS]
+        together = jnp.concatenate(shapes[start : start + half], 0)
         g = dot(together, col_ref[:TS]).astype(jnp.bfloat16)
         for o in range(half):
             mine = g[o * TS : (o + 1) * TS]
@@ -175,7 +171,7 @@
 
 
 def image_kernel(member_ref, *refs):
-    own_ref, right_ref, below_ref, corner_ref, col_ref, row_ref, _, far_ref, g_ref = refs
+    corner_ref, right_ref, below_ref, own_ref, col_ref, row_ref, far_ref, g_ref = refs
     image_columns(own_ref, right_ref, below_ref, corner_ref, col_ref, g_ref)
     image_rows(member_ref, row_ref, g_ref, CHIP_BIT, far_ref)
 
@@ -260,39 +256,33 @@
         tuple(shape_of(array.shape) for array in kept),
         [HBM] * 5 + [ANY],
         [pltpu.SemaphoreType.DMA((5,))],
-        flops=1000000000,
+        flops=10000000000,
     )(*[pinned(array) for array in kept], corner)
+    corner = halo(corner, GRID_W + 1)
     right = halo(right, 1)
     below = halo(below, GRID_W)
-    corner = halo(corner, GRID_W + 1)
     member = lax.axis_index("orient")[None]
 
     def sent(piece, bits):
         return lax.ppermute(piece, "orient", [(i, i ^ bits) for i in range(MEMBERS)])
 
-    shapes = call(
-        normalize_kernel,
-        shape_of((ORI_DEV * TS, TS)),
-        [VMEM],
-        [pltpu.VMEM((TS * ORI_DEV, TS), jnp.float32)],
-        flops=100000000,
-    )(pixels)
     templates = [
         call(
             template_kernel,
             shape_of((ORI_DEV, 4 * PAIRS, HALF)),
             [VMEM] * 3,
+            [pltpu.VMEM((TS * ORI_DEV, TS), jnp.float32)],
             flops=10000000000,
         )(group, columns, rows)
-        for group in (shapes, sent(shapes, CORE_BIT))
+        for group in (pixels, sent(pixels, CORE_BIT))
     ]
     spectrum = shape_of((4 * PAIRS, HALF))
     image, g = call(
         image_kernel,
         (spectrum, shape_of((2, TILE, HALF))),
-        [SMEM] + [VMEM] * 6 + [ANY],
+        [SMEM] + [VMEM] * 6,
         flops=1600000000,
-    )(member, own_block, right, below, corner, columns, rows, templates[0])
+    )(member, corner, right, below, own_block, columns, rows)
     inner = pltpu.VMEM((ORI_DEV * ROWS, TILE), jnp.bfloat16)
     far = call(
         far_kernel,

time: 45.5 us -> 44.9 us (0.987)
  waiting for transfers between devices: 9.25 us -> 8.36 us
    all_to_all x1, waiting for transfers between devices: 6.76 us -> 0.3 us  [shards(): pixels = lax.all_to_all(spread, 'tile', 0, 0)]
    ppermute x3, waiting for transfers between devices: 0.01 us -> 5.6 us  [halo(): return lax.ppermute(block, ('tile', 'orient'), route)]
    pallas_call x3 -> x2, Pallas kernels: 2.75 us -> 3.11 us  [shards(): call(template_kernel, shape_of((ORI_DEV, 4 * PAIRS, HALF)), [VMEM] * 3, [...]
  transfers between devices with their start and end apart: 6 -> 6, of which waited for: 2 -> 4; matrix products, arithmetic and copies ran while one was open for 0% -> 0% of each run, Pallas kernels for 15% -> 15%
where the time goes in v8:
time: 44.9 us; the launch traced here: 44.7 us
  starting transfers between devices  22.8 us (51%)
  Pallas kernels  12.8 us (29%)
  waiting for transfers between devices  8.36 us (19%)
  between operations  0.73 us (2%)
    all_to_all x1, starting transfers between devices, shards(): pixels = lax.all_to_all(spread, 'tile', 0, 0)  15.1 us
    ppermute x3, waiting for transfers between devices, halo(): return lax.ppermute(block, ('tile', 'orient'), route)  5.6 us
    ppermute x3, starting transfers between devices, halo(): return lax.ppermute(block, ('tile', 'orient'), route)  3.88 us
    ppermute x2, starting transfers between devices, sent(): lax.ppermute(piece, 'orient', [(i, i ^ bits) for i in range(MEMBERS)])  3.77 us
    pallas_call x2, Pallas kernels, shards(): call(template_kernel, shape_of((ORI_DEV, 4 * PAIRS, HALF)), [VMEM] * 3, [...  3.11 us
    pallas_call x1, Pallas kernels, shards(): call(own_kernel, shape_of((2, ROWS, CORE), jnp.float32), [SMEM] + [VMEM]...  2.69 us
    ppermute x2, waiting for transfers between devices, sent(): lax.ppermute(piece, 'orient', [(i, i ^ bits) for i in range(MEMBERS)])  2.46 us
    pallas_call x1, Pallas kernels, shards(): call(far_kernel, shape_of((2, ROWS, CORE)), [VMEM] * 5, [inner], flops=20...  2.15 us
  transfers between devices with their start and end apart: 6, of which 4 were waited for; matrix products, arithmetic and copies ran while one was open for 0% of the time, Pallas kernels for 15%

profile of v8, /device:TPU:1, one launch (start us, length us, event | category | flops | bytes accessed | tf_op | source)
XLA Modules:
  0.0 44.7 jit_solution(14891605555070868887)
XLA Ops:
  0.6 1.8 %shard_map.86 = (bf16[64,16,128]{2,1,0:T(8,128)(2,1)}, bf16[384,128]{1,0:T(8,128)(2,1)S(1)}, bf16[128,384]{1,0:T(8,128)(2,1)S(1)}, bf16[128,128]{1,0:T(8,128)(2,1)S(1)}) custom-call(s32[32]{0:T(128)} %ids_hbm.1, bf16[1,384,384]{2,1,0:T(8,128)(2,1)} %refs_4_.1, bf16[256,256]{1,0:T(8,128)(2,1)} %stack_hbm.1), custom_call_target="tpu_custom_call" | custom-call | bytes 2097152 | tf_op jit(solution)/shard_map/pallas_call | solution.py:234
  2.4 15.1 %all-to-all-start = ((bf16[64,16,128]{2,1,0:T(8,128)(2,1)}), bf16[64,16,128]{2,1,0:T(8,128)(2,1)S(1)}, u32[]{:S(2)}, u32[]{:S(2)}) async-start(bf16[64,16,128]{2,1,0:T(8,128)(2,1)} %get-tuple-element.20), calls=%async_computation | async-start | bytes 524288 | tf_op jit(solution)/shard_map/all_to_all | solution.py:252
  17.6 1.3 %collective-permute-start = (bf16[128,128]{1,0:T(8,128)(2,1)S(1)}, bf16[128,128]{1,0:T(8,128)(2,1)S(1)}, u32[]{:S(2)}, u32[]{:S(2)}) collective-permute-start(bf16[128,128]{1,0:T(8,128)(2,1)S(1)} %get-tuple-element.13.refs_5_), channel_id=1, source_target_pairs={{38,0},{39,1},{36,2},{37,3},{42,4},{43,5},{40,6},{41,7},{46,8},{47... | collective-permute-start | bytes 98312 | tf_op jit(solution)/shard_map/ppermute | solution.py:230
  18.9 1.3 %collective-permute-start.1 = (bf16[384,128]{1,0:T(8,128)(2,1)S(1)}, bf16[384,128]{1,0:T(8,128)(2,1)S(1)}, u32[]{:S(2)}, u32[]{:S(2)}) collective-permute-start(bf16[384,128]{1,0:T(8,128)(2,1)S(1)} %get-tuple-element.15), channel_id=1, source_target_pairs={{6,0},{7,1},{4,2},{5,3},{10,4},{11,5},{8,6},{9,7},{14,8},{15,9},{1... | collective-permute-start | bytes 294920 | tf_op jit(solution)/shard_map/ppermute | solution.py:230
  20.2 1.3 %collective-permute-start.2 = (bf16[128,384]{1,0:T(8,128)(2,1)S(1)}, bf16[128,384]{1,0:T(8,128)(2,1)S(1)}, u32[]{:S(2)}, u32[]{:S(2)}) collective-permute-start(bf16[128,384]{1,0:T(8,128)(2,1)S(1)} %get-tuple-element.16), channel_id=1, source_target_pairs={{32,0},{33,1},{34,2},{35,3},{36,4},{37,5},{38,6},{39,7},{40,8},{41... | collective-permute-start | bytes 294920 | tf_op jit(solution)/shard_map/ppermute | solution.py:230
  21.5 1.5 %shard_map.87 = (bf16[512,512]{1,0:T(8,128)(2,1)S(1)}, bf16[512,448]{1,0:T(8,128)(2,1)S(1)}, bf16[96,256]{1,0:T(8,128)(2,1)S(1)}, bf16[512,384]{1,0:T(8,128)(2,1)S(1)}, bf16[1,384,384]{2,1,0:T(8,128)(2,1)S(1)}) custom-call(bf16[512,512]{1,0:T(8,128)(2,1)} %constant.12.clone.refs_0_, bf16[512,448]{1,0:T(8,128)(2,1)} %constant.13.clone.refs_1_, ...), custom_call_target="tpu_custom_call" | custom-call | flops 10000000000 | bytes 2097152 | tf_op jit(solution)/shard_map/pallas_call | solution.py:254
  23.0 3.2 %collective-permute-done.refs_0_ = bf16[128,128]{1,0:T(8,128)(2,1)S(1)} collective-permute-done((bf16[128,128]{1,0:T(8,128)(2,1)S(1)}, bf16[128,128]{1,0:T(8,128)(2,1)S(1)}, u32[]{:S(2)}, u32[]{:S(2)}) %collective-permute-start) | collective-permute-done | bytes 32800 | tf_op jit(solution)/shard_map/ppermute | solution.py:230
  26.1 2.4 %collective-permute-done.1.refs_1_ = bf16[384,128]{1,0:T(8,128)(2,1)S(1)} collective-permute-done((bf16[384,128]{1,0:T(8,128)(2,1)S(1)}, bf16[384,128]{1,0:T(8,128)(2,1)S(1)}, u32[]{:S(2)}, u32[]{:S(2)}) %collective-permute-start.1) | collective-permute-done | bytes 98336 | tf_op jit(solution)/shard_map/ppermute | solution.py:230
  28.5 0.0 collective-permute-done.2.refs_2_
  28.5 0.9 %shard_map.88 = (bf16[512,256]{1,0:T(8,128)(2,1)S(1)}, bf16[2,512,256]{2,1,0:T(8,128)(2,1)S(1)}) custom-call(s32[1]{0:T(128)} %bitcast.member_ref, bf16[128,128]{1,0:T(8,128)(2,1)S(1)} %collective-permute-done.refs_0_, bf16[384,128]{1,0:T(8,128)(2,1)S(1)} %collective-permute-done.1.refs_1_, bf16[128,384]{1,0:T(8,128)(2,1)S(1)} %collective-permute-done.2.refs_2_, ...), custom_call_target="tpu_custom_call" | custom-call | flops 1600000000 | bytes 2097152 | tf_op jit(solution)/shard_map/pallas_call | solution.py:280
  29.4 0.3 all-to-all-done.pixels_ref
  29.7 3.4 %collective-permute-start.3 = (bf16[64,16,128]{2,1,0:T(8,128)(2,1)S(1)}, bf16[64,16,128]{2,1,0:T(8,128)(2,1)S(1)}, u32[]{:S(2)}, u32[]{:S(2)}) collective-permute-start(bf16[64,16,128]{2,1,0:T(8,128)(2,1)S(1)} %all-to-all-done.pixels_ref), channel_id=1, source_target_pairs={{0,1},{1,0},{2,3},{3,2},{4,5},{5,4},{6,7},{7,6},{8,9},{9,8},{10,11... | collective-permute-start | bytes 786440 | tf_op jit(solution)/shard_map/ppermute | solution.py:267
  33.1 1.6 %shard_map.89.mine_ref = bf16[8,512,256]{2,1,0:T(8,128)(2,1)S(1)} custom-call(bf16[64,16,128]{2,1,0:T(8,128)(2,1)S(1)} %all-to-all-done.pixels_ref, bf16[512,512]{1,0:T(8,128)(2,1)S(1)} %get-tuple-element.18.refs_4_.col_ref, bf16[512,448]{1,0:T(8,128)(2,1)S(1)} %get-tuple-element.14.refs_5_.row_ref), custom_call_target="tpu_custom_call" | custom-call | flops 10000000000 | bytes 2097152 | tf_op jit(solution)/shard_map/pallas_call | solution.py:270
  34.6 0.0 collective-permute-done.3.pixels_ref
  34.6 1.6 %shard_map.90.other_ref = bf16[8,512,256]{2,1,0:T(8,128)(2,1)S(1)} custom-call(bf16[64,16,128]{2,1,0:T(8,128)(2,1)S(1)} %collective-permute-done.3.pixels_ref, bf16[512,512]{1,0:T(8,128)(2,1)S(1)} %get-tuple-element.18.refs_4_.col_ref, bf16[512,448]{1,0:T(8,128)(2,1)S(1)} %get-tuple-element.14.refs_5_.row_ref), custom_call_target="tpu_custom_call" | custom-call | flops 10000000000 | bytes 2097152 | tf_op jit(solution)/shard_map/pallas_call | solution.py:270
  36.2 2.1 %shard_map.92 = bf16[2,96,384]{2,1,0:T(8,128)(2,1)S(1)} custom-call(bf16[512,256]{1,0:T(8,128)(2,1)S(1)} %get-tuple-element.23.image_ref, bf16[8,512,256]{2,1,0:T(8,128)(2,1)S(1)} %shard_map.89.mine_ref, bf16[8,512,256]{2,1,0:T(8,128)(2,1)S(1)} %shard_map.90.other_ref, bf16[96,256]{1,0:T(8,128)(2,1)S(1)} %get-tuple-element.21.inv_row_ref, ...), custom_call_target="tpu_custom_call" | custom-call | flops 2000000000 | bytes 2097152 | tf_op jit(solution)/shard_map/pallas_call | solution.py:287
  38.4 0.4 collective-permute-start.4
  38.8 2.7 %shard_map.91.own_ref = f32[2,96,384]{2,1,0:T(8,128)S(1)} custom-call(s32[1]{0:T(128)} %bitcast.member_ref, bf16[512,448]{1,0:T(8,128)(2,1)S(1)} %get-tuple-element.14.refs_5_.row_ref, bf16[2,512,256]{2,1,0:T(8,128)(2,1)S(1)} %get-tuple-element.19.g_ref, bf16[8,512,256]{2,1,0:T(8,128)(2,1)S(1)} %shard_map.89.mine_ref, ...), custom_call_target="tpu_custom_call" | custom-call | flops 2000000000 | bytes 2097152 | tf_op jit(solution)/shard_map/pallas_call | solution.py:294
  41.5 2.5 %collective-permute-done.4.far_ref = bf16[2,96,384]{2,1,0:T(8,128)(2,1)S(1)} collective-permute-done((bf16[2,96,384]{2,1,0:T(8,128)(2,1)S(1)}, bf16[2,96,384]{2,1,0:T(8,128)(2,1)S(1)}, u32[]{:S(2)}, u32[]{:S(2)}) %collective-permute-start.4) | collective-permute-done | bytes 147488 | tf_op jit(solution)/shard_map/ppermute | solution.py:267
  43.9 0.7 %shard_map.93 = (f32[1,96,384]{2,1,0:T(8,128)}, f32[1,96,384]{2,1,0:T(8,128)}) custom-call(f32[2,96,384]{2,1,0:T(8,128)S(1)} %shard_map.91.own_ref, bf16[2,96,384]{2,1,0:T(8,128)(2,1)S(1)} %collective-permute-done.4.far_ref), custom_call_target="tpu_custom_call" | custom-call | bytes 2097152 | tf_op jit(solution)/shard_map/pallas_call | solution.py:302
Async XLA Ops:
  2.4 27.3 %all-to-all-start = ((bf16[64,16,128]{2,1,0:T(8,128)(2,1)}), bf16[64,16,128]{2,1,0:T(8,128)(2,1)S(1)}, u32[]{:S(2)}, u32[]{:S(2)}) async-start(bf16[64,16,128]{2,1,0:T(8,128)(2,1)} %get-tuple-element.20), calls=%async_computation | async-start | bytes 524288 | tf_op jit(solution)/shard_map/all_to_all | solution.py:252
  17.6 8.5 %collective-permute-start = (bf16[128,128]{1,0:T(8,128)(2,1)S(1)}, bf16[128,128]{1,0:T(8,128)(2,1)S(1)}, u32[]{:S(2)}, u32[]{:S(2)}) collective-permute-start(bf16[128,128]{1,0:T(8,128)(2,1)S(1)} %get-tuple-element.13.refs_5_), channel_id=1, source_target_pairs={{38,0},{39,1},{36,2},{37,3},{42,4},{43,5},{40,6},{41,7},{46,8},{47... | collective-permute-start | bytes 98312 | tf_op jit(solution)/shard_map/ppermute | solution.py:230
  18.9 9.7 %collective-permute-start.1 = (bf16[384,128]{1,0:T(8,128)(2,1)S(1)}, bf16[384,128]{1,0:T(8,128)(2,1)S(1)}, u32[]{:S(2)}, u32[]{:S(2)}) collective-permute-start(bf16[384,128]{1,0:T(8,128)(2,1)S(1)} %get-tuple-element.15), channel_id=1, source_target_pairs={{6,0},{7,1},{4,2},{5,3},{10,4},{11,5},{8,6},{9,7},{14,8},{15,9},{1... | collective-permute-start | bytes 294920 | tf_op jit(solution)/shard_map/ppermute | solution.py:230
  20.2 8.4 %collective-permute-start.2 = (bf16[128,384]{1,0:T(8,128)(2,1)S(1)}, bf16[128,384]{1,0:T(8,128)(2,1)S(1)}, u32[]{:S(2)}, u32[]{:S(2)}) collective-permute-start(bf16[128,384]{1,0:T(8,128)(2,1)S(1)} %get-tuple-element.16), channel_id=1, source_target_pairs={{32,0},{33,1},{34,2},{35,3},{36,4},{37,5},{38,6},{39,7},{40,8},{41... | collective-permute-start | bytes 294920 | tf_op jit(solution)/shard_map/ppermute | solution.py:230
  29.7 4.9 %collective-permute-start.3 = (bf16[64,16,128]{2,1,0:T(8,128)(2,1)S(1)}, bf16[64,16,128]{2,1,0:T(8,128)(2,1)S(1)}, u32[]{:S(2)}, u32[]{:S(2)}) collective-permute-start(bf16[64,16,128]{2,1,0:T(8,128)(2,1)S(1)} %all-to-all-done.pixels_ref), channel_id=1, source_target_pairs={{0,1},{1,0},{2,3},{3,2},{4,5},{5,4},{6,7},{7,6},{8,9},{9,8},{10,11... | collective-permute-start | bytes 786440 | tf_op jit(solution)/shard_map/ppermute | solution.py:267
  38.4 5.6 %collective-permute-start.4 = (bf16[2,96,384]{2,1,0:T(8,128)(2,1)S(1)}, bf16[2,96,384]{2,1,0:T(8,128)(2,1)S(1)}, u32[]{:S(2)}, u32[]{:S(2)}) collective-permute-start(bf16[2,96,384]{2,1,0:T(8,128)(2,1)S(1)} %shard_map.92), channel_id=1, source_target_pairs={{0,2},{1,3},{2,0},{3,1},{4,6},{5,7},{6,4},{7,5},{8,10},{9,11},{10,... | collective-permute-start | bytes 442376 | tf_op jit(solution)/shard_map/ppermute | solution.py:267

commit v9 on v8

--- a/solution.py
+++ b/solution.py
@@ -74,18 +74,23 @@
     load_ids.start()
     load_stack.start()
     load_micro.start()
-    row = lax.broadcasted_iota(jnp.int32, (2 * ORI_DEV, 256), 0)
-    lane = lax.broadcasted_iota(jnp.int32, (2 * ORI_DEV, 256), 1)
-    wanted = jnp.zeros((2 * ORI_DEV, 256), jnp.int32)
-    first = lax.axis_index("orient") * ORI_DEV
+    row = lax.broadcasted_iota(jnp.int32, (4 * ORI_DEV, 256), 0)
+    lane = lax.broadcasted_iota(jnp.int32, (4 * ORI_DEV, 256), 1)
+    wanted = jnp.zeros((4 * ORI_DEV, 256), jnp.int32)
+    member, side = lax.axis_index("orient"), lax.axis_index("tile") % 2
     load_ids.wait()
-    for o in range(ORI_DEV):
-        wanted = jnp.where(row % ORI_DEV == o, ids_ref[first + o], wanted)
+    for to_side in range(2):
+        first = (member ^ (CHIP_BIT * (side ^ to_side))) * ORI_DEV
+        for o in range(ORI_DEV):
+            here = (row % ORI_DEV == o) & (row // (2 * ORI_DEV) == to_side)
+            wanted = jnp.where(here, ids_ref[first + o], wanted)
     hot = jnp.where(lane == wanted, 1.0, 0.0).astype(jnp.bfloat16)
     load_stack.wait()
     picked = dot(hot, stack_ref[...])
-    both = jnp.concatenate([picked[:ORI_DEV, :TS], picked[ORI_DEV:, TS:]], 0).astype(jnp.bfloat16)
-    out_ref[...] = jnp.broadcast_to(both[None], out_ref.shape)
+    for to_side in range(2):
+        top, middle, end = (2 * to_side * ORI_DEV + k * ORI_DEV for k in range(3))
+        both = jnp.concatenate([picked[top:middle, :TS], picked[middle:end, TS:]], 0).astype(jnp.bfloat16)
+        out_ref[:, to_side] = jnp.broadcast_to(both[None], (TILES // 2, 2 * ORI_DEV, TS))
     store = pltpu.make_async_copy(out_ref, out_hbm, sems.at[3])
     store.start()
     load_micro.wait()
@@ -110,16 +115,13 @@
     centered = values - mean[None]
     square = jnp.sum(jnp.sum(centered * centered, 0), 1, keepdims=True) / (TS * TS)
     spread = jnp.sqrt(square + 1e-06) * TS
-    shape_ref[...] = (centered / spread[None]).reshape(TS * ORI_DEV, TS)
+    shape_ref[...] = (centered * (1.0 / spread)[None]).reshape(TS * ORI_DEV, TS)
     shapes = [shape_ref[pl.ds(o, TS, stride=ORI_DEV), :].astype(jnp.bfloat16) for o in range(ORI_DEV)]
-    half = ORI_DEV // 2
-    for start in (0, half):
-        together = jnp.concatenate(shapes[start : start + half], 0)
-        g = dot(together, col_ref[:TS]).astype(jnp.bfloat16)
-        for o in range(half):
-            mine = g[o * TS : (o + 1) * TS]
-            mine = jnp.concatenate([mine[:, :HALF], mine[:, HALF:]], 0)
-            out_ref[start + o] = dot(row_ref[:, : 2 * TS], mine).astype(jnp.bfloat16)
+    g = dot(jnp.concatenate(shapes, 0), col_ref[:TS]).astype(jnp.bfloat16)
+    for o in range(ORI_DEV):
+        mine = g[o * TS : (o + 1) * TS]
+        mine = jnp.concatenate([mine[:, :HALF], mine[:, HALF:]], 0)
+        out_ref[o] = dot(row_ref[:, : 2 * TS], mine).astype(jnp.bfloat16)
 
 
 def image_columns(own_ref, right_ref, below_ref, corner_ref, col_ref, g_ref):
@@ -219,6 +221,12 @@
     return pltpu.with_memory_space_constraint(jnp.asarray(array), pltpu.HBM)
 
 
+def near_groups():
+    return [
+        [t * MEMBERS + (chip ^ (CHIP_BIT * (t % 2))) + core for t in range(TILES)] for chip in (0, CHIP_BIT) for core in (0, 1)
+    ]
+
+
 def halo(block, distance):
     route = []
     crosses = distance % GRID_W
@@ -234,7 +242,7 @@
     spread, right, below, corner = call(
         prepare_kernel,
         (
-            shape_of((TILES, 2 * ORI_DEV, TS)),
+            shape_of((TILES // 2, 2, 2 * ORI_DEV, TS)),
             shape_of((CORE, TS)),
             shape_of((TS, CORE)),
             shape_of((TS, TS)),
@@ -244,12 +252,14 @@
             pltpu.SMEM((MEMBERS * ORI_DEV,), jnp.int32),
             pltpu.VMEM((CORE, CORE), jnp.bfloat16),
             pltpu.VMEM((256, 256), jnp.bfloat16),
-            pltpu.VMEM((TILES, 2 * ORI_DEV, TS), jnp.bfloat16),
+            pltpu.VMEM((TILES // 2, 2, 2 * ORI_DEV, TS), jnp.bfloat16),
             pltpu.SemaphoreType.DMA((4,)),
         ],
         out_specs=(HBM, VMEM, VMEM, VMEM),
     )(pinned(orient_list), pinned(micrograph), pinned(template_stack))
-    pixels = lax.all_to_all(spread, "tile", 0, 0)
+    pixels = lax.all_to_all(
+        spread.reshape(TILES, 2 * ORI_DEV, TS), ("tile", "orient"), 0, 0, axis_index_groups=near_groups()
+    )
     kept = [column_table(), row_table(), inverse_row_table(), inverse_column_table(), micrograph]
     columns, rows, *tables, own_block = call(
         load_kernel,

time: 44.9 us -> 44 us (0.980)
  starting transfers between devices: 22.8 us -> 22.1 us
where the time goes in v9:
time: 44 us; the launch traced here: 43.8 us
  starting transfers between devices  22.1 us (50%)
  Pallas kernels  12.5 us (28%)
  waiting for transfers between devices  8.36 us (19%)
  between operations  0.74 us (2%)
    all_to_all x1, starting transfers between devices, shards(): lax.all_to_all(spread.reshape(TILES, 2 * ORI_DEV, TS), ('tile', 'orient')...  14.9 us
    ppermute x3, waiting for transfers between devices, halo(): return lax.ppermute(block, ('tile', 'orient'), route)  5.42 us
    ppermute x3, starting transfers between devices, halo(): return lax.ppermute(block, ('tile', 'orient'), route)  3.88 us
    ppermute x2, starting transfers between devices, sent(): lax.ppermute(piece, 'orient', [(i, i ^ bits) for i in range(MEMBERS)])  3.39 us
    pallas_call x2, Pallas kernels, shards(): call(template_kernel, shape_of((ORI_DEV, 4 * PAIRS, HALF)), [VMEM] * 3, [...  2.84 us
    pallas_call x1, Pallas kernels, shards(): call(own_kernel, shape_of((2, ROWS, CORE), jnp.float32), [SMEM] + [VMEM]...  2.7 us
    ppermute x2, waiting for transfers between devices, sent(): lax.ppermute(piece, 'orient', [(i, i ^ bits) for i in range(MEMBERS)])  2.69 us
    pallas_call x1, Pallas kernels, shards(): call(far_kernel, shape_of((2, ROWS, CORE)), [VMEM] * 5, [inner], flops=20...  2.15 us
  transfers between devices with their start and end apart: 6, of which 4 were waited for; matrix products, arithmetic and copies ran while one was open for 0% of the time, Pallas kernels for 15%

profile of v9, /device:TPU:1, one launch (start us, length us, event | category | flops | bytes accessed | tf_op | source)
XLA Modules:
  0.0 43.8 jit_solution(18264192811199150625)
XLA Ops:
  0.6 1.8 %shard_map.86 = (bf16[32,2,16,128]{3,2,1,0:T(8,128)(2,1)}, bf16[384,128]{1,0:T(8,128)(2,1)S(1)}, bf16[128,384]{1,0:T(8,128)(2,1)S(1)}, bf16[128,128]{1,0:T(8,128)(2,1)S(1)}) custom-call(s32[32]{0:T(128)} %ids_hbm.1, bf16[1,384,384]{2,1,0:T(8,128)(2,1)} %refs_4_.1, bf16[256,256]{1,0:T(8,128)(2,1)} %stack_hbm.1), custom_call_target="tpu_custom_call" | custom-call | bytes 2097152 | tf_op jit(solution)/shard_map/pallas_call | solution.py:242
  2.4 14.9 %all-to-all-start = ((bf16[64,16,128]{2,1,0:T(8,128)(2,1)}), bf16[64,16,128]{2,1,0:T(8,128)(2,1)S(1)}, u32[]{:S(2)}, u32[]{:S(2)}) async-start(bf16[64,16,128]{2,1,0:T(8,128)(2,1)} %bitcast.1), calls=%async_computation | async-start | bytes 524288 | tf_op jit(solution)/shard_map/all_to_all | solution.py:260
  17.3 1.3 %collective-permute-start = (bf16[128,128]{1,0:T(8,128)(2,1)S(1)}, bf16[128,128]{1,0:T(8,128)(2,1)S(1)}, u32[]{:S(2)}, u32[]{:S(2)}) collective-permute-start(bf16[128,128]{1,0:T(8,128)(2,1)S(1)} %get-tuple-element.13.refs_5_), channel_id=1, source_target_pairs={{38,0},{39,1},{36,2},{37,3},{42,4},{43,5},{40,6},{41,7},{46,8},{47... | collective-permute-start | bytes 98312 | tf_op jit(solution)/shard_map/ppermute | solution.py:238
  18.6 1.3 %collective-permute-start.1 = (bf16[384,128]{1,0:T(8,128)(2,1)S(1)}, bf16[384,128]{1,0:T(8,128)(2,1)S(1)}, u32[]{:S(2)}, u32[]{:S(2)}) collective-permute-start(bf16[384,128]{1,0:T(8,128)(2,1)S(1)} %get-tuple-element.15), channel_id=1, source_target_pairs={{6,0},{7,1},{4,2},{5,3},{10,4},{11,5},{8,6},{9,7},{14,8},{15,9},{1... | collective-permute-start | bytes 294920 | tf_op jit(solution)/shard_map/ppermute | solution.py:238
  19.9 1.3 %collective-permute-start.2 = (bf16[128,384]{1,0:T(8,128)(2,1)S(1)}, bf16[128,384]{1,0:T(8,128)(2,1)S(1)}, u32[]{:S(2)}, u32[]{:S(2)}) collective-permute-start(bf16[128,384]{1,0:T(8,128)(2,1)S(1)} %get-tuple-element.16), channel_id=1, source_target_pairs={{32,0},{33,1},{34,2},{35,3},{36,4},{37,5},{38,6},{39,7},{40,8},{41... | collective-permute-start | bytes 294920 | tf_op jit(solution)/shard_map/ppermute | solution.py:238
  21.2 1.5 %shard_map.87 = (bf16[512,512]{1,0:T(8,128)(2,1)S(1)}, bf16[512,448]{1,0:T(8,128)(2,1)S(1)}, bf16[96,256]{1,0:T(8,128)(2,1)S(1)}, bf16[512,384]{1,0:T(8,128)(2,1)S(1)}, bf16[1,384,384]{2,1,0:T(8,128)(2,1)S(1)}) custom-call(bf16[512,512]{1,0:T(8,128)(2,1)} %constant.12.clone.refs_0_, bf16[512,448]{1,0:T(8,128)(2,1)} %constant.13.clone.refs_1_, ...), custom_call_target="tpu_custom_call" | custom-call | flops 10000000000 | bytes 2097152 | tf_op jit(solution)/shard_map/pallas_call | solution.py:264
  22.7 3.1 %collective-permute-done.refs_0_ = bf16[128,128]{1,0:T(8,128)(2,1)S(1)} collective-permute-done((bf16[128,128]{1,0:T(8,128)(2,1)S(1)}, bf16[128,128]{1,0:T(8,128)(2,1)S(1)}, u32[]{:S(2)}, u32[]{:S(2)}) %collective-permute-start) | collective-permute-done | bytes 32800 | tf_op jit(solution)/shard_map/ppermute | solution.py:238
  25.8 2.3 %collective-permute-done.1.refs_1_ = bf16[384,128]{1,0:T(8,128)(2,1)S(1)} collective-permute-done((bf16[384,128]{1,0:T(8,128)(2,1)S(1)}, bf16[384,128]{1,0:T(8,128)(2,1)S(1)}, u32[]{:S(2)}, u32[]{:S(2)}) %collective-permute-start.1) | collective-permute-done | bytes 98336 | tf_op jit(solution)/shard_map/ppermute | solution.py:238
  28.1 0.0 collective-permute-done.2.refs_2_
  28.1 0.9 %shard_map.88 = (bf16[512,256]{1,0:T(8,128)(2,1)S(1)}, bf16[2,512,256]{2,1,0:T(8,128)(2,1)S(1)}) custom-call(s32[1]{0:T(128)} %bitcast.member_ref, bf16[128,128]{1,0:T(8,128)(2,1)S(1)} %collective-permute-done.refs_0_, bf16[384,128]{1,0:T(8,128)(2,1)S(1)} %collective-permute-done.1.refs_1_, bf16[128,384]{1,0:T(8,128)(2,1)S(1)} %collective-permute-done.2.refs_2_, ...), custom_call_target="tpu_custom_call" | custom-call | flops 1600000000 | bytes 2097152 | tf_op jit(solution)/shard_map/pallas_call | solution.py:290
  29.0 0.3 all-to-all-done.pixels_ref
  29.2 3.3 %collective-permute-start.3 = (bf16[64,16,128]{2,1,0:T(8,128)(2,1)S(1)}, bf16[64,16,128]{2,1,0:T(8,128)(2,1)S(1)}, u32[]{:S(2)}, u32[]{:S(2)}) collective-permute-start(bf16[64,16,128]{2,1,0:T(8,128)(2,1)S(1)} %all-to-all-done.pixels_ref), channel_id=1, source_target_pairs={{0,1},{1,0},{2,3},{3,2},{4,5},{5,4},{6,7},{7,6},{8,9},{9,8},{10,11... | collective-permute-start | bytes 786440 | tf_op jit(solution)/shard_map/ppermute | solution.py:277
  32.5 1.4 %shard_map.89.mine_ref = bf16[8,512,256]{2,1,0:T(8,128)(2,1)S(1)} custom-call(bf16[64,16,128]{2,1,0:T(8,128)(2,1)S(1)} %all-to-all-done.pixels_ref, bf16[512,512]{1,0:T(8,128)(2,1)S(1)} %get-tuple-element.18.refs_4_.col_ref, bf16[512,448]{1,0:T(8,128)(2,1)S(1)} %get-tuple-element.14.refs_5_.row_ref), custom_call_target="tpu_custom_call" | custom-call | flops 10000000000 | bytes 2097152 | tf_op jit(solution)/shard_map/pallas_call | solution.py:280
  34.0 0.0 collective-permute-done.3.pixels_ref
  34.0 1.4 %shard_map.90.other_ref = bf16[8,512,256]{2,1,0:T(8,128)(2,1)S(1)} custom-call(bf16[64,16,128]{2,1,0:T(8,128)(2,1)S(1)} %collective-permute-done.3.pixels_ref, bf16[512,512]{1,0:T(8,128)(2,1)S(1)} %get-tuple-element.18.refs_4_.col_ref, bf16[512,448]{1,0:T(8,128)(2,1)S(1)} %get-tuple-element.14.refs_5_.row_ref), custom_call_target="tpu_custom_call" | custom-call | flops 10000000000 | bytes 2097152 | tf_op jit(solution)/shard_map/pallas_call | solution.py:280
  35.4 2.1 %shard_map.92 = bf16[2,96,384]{2,1,0:T(8,128)(2,1)S(1)} custom-call(bf16[512,256]{1,0:T(8,128)(2,1)S(1)} %get-tuple-element.23.image_ref, bf16[8,512,256]{2,1,0:T(8,128)(2,1)S(1)} %shard_map.89.mine_ref, bf16[8,512,256]{2,1,0:T(8,128)(2,1)S(1)} %shard_map.90.other_ref, bf16[96,256]{1,0:T(8,128)(2,1)S(1)} %get-tuple-element.21.inv_row_ref, ...), custom_call_target="tpu_custom_call" | custom-call | flops 2000000000 | bytes 2097152 | tf_op jit(solution)/shard_map/pallas_call | solution.py:297
  37.5 0.1 collective-permute-start.4
  37.6 2.7 %shard_map.91.own_ref = f32[2,96,384]{2,1,0:T(8,128)S(1)} custom-call(s32[1]{0:T(128)} %bitcast.member_ref, bf16[512,448]{1,0:T(8,128)(2,1)S(1)} %get-tuple-element.14.refs_5_.row_ref, bf16[2,512,256]{2,1,0:T(8,128)(2,1)S(1)} %get-tuple-element.19.g_ref, bf16[8,512,256]{2,1,0:T(8,128)(2,1)S(1)} %shard_map.89.mine_ref, ...), custom_call_target="tpu_custom_call" | custom-call | flops 2000000000 | bytes 2097152 | tf_op jit(solution)/shard_map/pallas_call | solution.py:304
  40.3 2.7 %collective-permute-done.4.far_ref = bf16[2,96,384]{2,1,0:T(8,128)(2,1)S(1)} collective-permute-done((bf16[2,96,384]{2,1,0:T(8,128)(2,1)S(1)}, bf16[2,96,384]{2,1,0:T(8,128)(2,1)S(1)}, u32[]{:S(2)}, u32[]{:S(2)}) %collective-permute-start.4) | collective-permute-done | bytes 147488 | tf_op jit(solution)/shard_map/ppermute | solution.py:277
  43.0 0.7 %shard_map.93 = (f32[1,96,384]{2,1,0:T(8,128)}, f32[1,96,384]{2,1,0:T(8,128)}) custom-call(f32[2,96,384]{2,1,0:T(8,128)S(1)} %shard_map.91.own_ref, bf16[2,96,384]{2,1,0:T(8,128)(2,1)S(1)} %collective-permute-done.4.far_ref), custom_call_target="tpu_custom_call" | custom-call | bytes 2097152 | tf_op jit(solution)/shard_map/pallas_call | solution.py:312
Async XLA Ops:
  2.4 26.8 %all-to-all-start = ((bf16[64,16,128]{2,1,0:T(8,128)(2,1)}), bf16[64,16,128]{2,1,0:T(8,128)(2,1)S(1)}, u32[]{:S(2)}, u32[]{:S(2)}) async-start(bf16[64,16,128]{2,1,0:T(8,128)(2,1)} %bitcast.1), calls=%async_computation | async-start | bytes 524288 | tf_op jit(solution)/shard_map/all_to_all | solution.py:260
  17.3 8.5 %collective-permute-start = (bf16[128,128]{1,0:T(8,128)(2,1)S(1)}, bf16[128,128]{1,0:T(8,128)(2,1)S(1)}, u32[]{:S(2)}, u32[]{:S(2)}) collective-permute-start(bf16[128,128]{1,0:T(8,128)(2,1)S(1)} %get-tuple-element.13.refs_5_), channel_id=1, source_target_pairs={{38,0},{39,1},{36,2},{37,3},{42,4},{43,5},{40,6},{41,7},{46,8},{47... | collective-permute-start | bytes 98312 | tf_op jit(solution)/shard_map/ppermute | solution.py:238
  18.6 9.5 %collective-permute-start.1 = (bf16[384,128]{1,0:T(8,128)(2,1)S(1)}, bf16[384,128]{1,0:T(8,128)(2,1)S(1)}, u32[]{:S(2)}, u32[]{:S(2)}) collective-permute-start(bf16[384,128]{1,0:T(8,128)(2,1)S(1)} %get-tuple-element.15), channel_id=1, source_target_pairs={{6,0},{7,1},{4,2},{5,3},{10,4},{11,5},{8,6},{9,7},{14,8},{15,9},{1... | collective-permute-start | bytes 294920 | tf_op jit(solution)/shard_map/ppermute | solution.py:238
  19.9 8.2 %collective-permute-start.2 = (bf16[128,384]{1,0:T(8,128)(2,1)S(1)}, bf16[128,384]{1,0:T(8,128)(2,1)S(1)}, u32[]{:S(2)}, u32[]{:S(2)}) collective-permute-start(bf16[128,384]{1,0:T(8,128)(2,1)S(1)} %get-tuple-element.16), channel_id=1, source_target_pairs={{32,0},{33,1},{34,2},{35,3},{36,4},{37,5},{38,6},{39,7},{40,8},{41... | collective-permute-start | bytes 294920 | tf_op jit(solution)/shard_map/ppermute | solution.py:238
  29.2 4.7 %collective-permute-start.3 = (bf16[64,16,128]{2,1,0:T(8,128)(2,1)S(1)}, bf16[64,16,128]{2,1,0:T(8,128)(2,1)S(1)}, u32[]{:S(2)}, u32[]{:S(2)}) collective-permute-start(bf16[64,16,128]{2,1,0:T(8,128)(2,1)S(1)} %all-to-all-done.pixels_ref), channel_id=1, source_target_pairs={{0,1},{1,0},{2,3},{3,2},{4,5},{5,4},{6,7},{7,6},{8,9},{9,8},{10,11... | collective-permute-start | bytes 786440 | tf_op jit(solution)/shard_map/ppermute | solution.py:277
  37.5 5.5 %collective-permute-start.4 = (bf16[2,96,384]{2,1,0:T(8,128)(2,1)S(1)}, bf16[2,96,384]{2,1,0:T(8,128)(2,1)S(1)}, u32[]{:S(2)}, u32[]{:S(2)}) collective-permute-start(bf16[2,96,384]{2,1,0:T(8,128)(2,1)S(1)} %shard_map.92), channel_id=1, source_target_pairs={{0,2},{1,3},{2,0},{3,1},{4,6},{5,7},{6,4},{7,5},{8,10},{9,11},{10,... | collective-permute-start | bytes 442376 | tf_op jit(solution)/shard_map/ppermute | solution.py:277

commit v10 on v9

--- a/solution.py
+++ b/solution.py
@@ -166,20 +166,29 @@
         out = dot(inner_ref[...], inv_col_ref[...]).reshape(ORI_DEV, ROWS, CORE)
         return jnp.max(out, 0), jnp.sum(out, 0)
 
-    high_a, sum_a = corr(template_refs[0])
-    high_b, sum_b = corr(template_refs[1])
-    out_ref[0] = jnp.maximum(high_a, high_b).astype(out_ref.dtype)
-    out_ref[1] = (sum_a + sum_b).astype(out_ref.dtype)
+    high, total = corr(template_refs[0])
+    for template_ref in template_refs[1:]:
+        more, added = corr(template_ref)
+        high, total = jnp.maximum(high, more), total + added
+    out_ref[0] = high.astype(out_ref.dtype)
+    out_ref[1] = total.astype(out_ref.dtype)
 
 
 def image_kernel(member_ref, *refs):
-    corner_ref, right_ref, below_ref, own_ref, col_ref, row_ref, far_ref, g_ref = refs
+    corner_ref, right_ref, below_ref, own_ref, col_ref, row_ref, across_ref, same_ref, g_ref = refs
     image_columns(own_ref, right_ref, below_ref, corner_ref, col_ref, g_ref)
-    image_rows(member_ref, row_ref, g_ref, CHIP_BIT, far_ref)
-
-
-def far_kernel(image_ref, mine_ref, other_ref, inv_row_ref, inv_col_ref, out_ref, inner_ref):
-    block(image_ref, (mine_ref, other_ref), inv_row_ref, inv_col_ref, out_ref, inner_ref)
+    image_rows(member_ref, row_ref, g_ref, CHIP_BIT + CORE_BIT, across_ref)
+    image_rows(member_ref, row_ref, g_ref, CHIP_BIT, same_ref)
+
+
+def far_kernel(image_ref, template_ref, inv_row_ref, inv_col_ref, out_ref, inner_ref):
+    block(image_ref, (template_ref,), inv_row_ref, inv_col_ref, out_ref, inner_ref)
+
+
+def merge_kernel(mine_ref, other_ref, out_ref):
+    other = other_ref[...].astype(jnp.float32)
+    out_ref[0] = jnp.maximum(mine_ref[0], other[0]).astype(out_ref.dtype)
+    out_ref[1] = (mine_ref[1] + other[1]).astype(out_ref.dtype)
 
 
 def own_kernel(member_ref, row_ref, g_ref, mine_ref, other_ref, inv_row_ref, inv_col_ref, out_ref, image_ref, inner_ref):
@@ -276,40 +285,44 @@
     def sent(piece, bits):
         return lax.ppermute(piece, "orient", [(i, i ^ bits) for i in range(MEMBERS)])
 
-    templates = [
-        call(
+
+    def spectra(group):
+        return call(
             template_kernel,
             shape_of((ORI_DEV, 4 * PAIRS, HALF)),
             [VMEM] * 3,
             [pltpu.VMEM((TS * ORI_DEV, TS), jnp.float32)],
             flops=10000000000,
         )(group, columns, rows)
-        for group in (pixels, sent(pixels, CORE_BIT))
-    ]
+
     spectrum = shape_of((4 * PAIRS, HALF))
-    image, g = call(
+    image_across, image_same, g = call(
         image_kernel,
-        (spectrum, shape_of((2, TILE, HALF))),
+        (spectrum, spectrum, shape_of((2, TILE, HALF))),
         [SMEM] + [VMEM] * 6,
         flops=1600000000,
     )(member, corner, right, below, own_block, columns, rows)
     inner = pltpu.VMEM((ORI_DEV * ROWS, TILE), jnp.bfloat16)
-    far = call(
-        far_kernel,
-        shape_of((2, ROWS, CORE)),
-        [VMEM] * 5,
-        [inner],
-        flops=2000000000,
-    )(image, *templates, *tables)
+    piece, wide = shape_of((2, ROWS, CORE)), shape_of((2, ROWS, CORE), jnp.float32)
+
+    def far(image, out):
+        return call(far_kernel, out, [VMEM] * 4, [inner], flops=1000000000)(image, mine, *tables)
+
+    mine = spectra(pixels)
+    across = sent(far(image_across, piece), CORE_BIT)
+    same = far(image_same, wide)
+    merged = call(merge_kernel, piece, [VMEM] * 2, flops=100000000)(same, across)
+    merged = sent(merged, CHIP_BIT)
+    other = spectra(sent(pixels, CORE_BIT))
     own = call(
         own_kernel,
-        shape_of((2, ROWS, CORE), jnp.float32),
+        wide,
         [SMEM] + [VMEM] * 6,
         [pltpu.VMEM((4 * PAIRS, HALF), jnp.bfloat16), inner],
         flops=2000000000,
-    )(member, rows, g, *templates, *tables)
+    )(member, rows, g, mine, other, *tables)
     out = shape_of((1, ROWS, CORE), jnp.float32)
-    return call(finish_kernel, (out, out), [VMEM] * 2)(own, sent(far, CHIP_BIT))
+    return call(finish_kernel, (out, out), [VMEM] * 2)(own, merged)
 
 
 def solution(mesh):

time: 44 us -> 42.8 us (0.973)
  waiting for transfers between devices: 8.36 us -> 6.76 us
    ppermute x2 -> x3, waiting for transfers between devices: 2.69 us -> 1.23 us  [sent(): lax.ppermute(piece, 'orient', [(i, i ^ bits) for i in range(MEMBERS)])]
    pallas_call x6 -> x8, Pallas kernels: 9.27 us -> 9.54 us  [the longest x2 2.84 us: spectra(): call(template_kernel, shape_of((ORI_DEV, 4 * PAIRS, HALF)), [VMEM] * 3, [...]
    ppermute x2 -> x3, starting transfers between devices: 3.39 us -> 3.48 us  [sent(): lax.ppermute(piece, 'orient', [(i, i ^ bits) for i in range(MEMBERS)])]
  transfers between devices with their start and end apart: 6 -> 7, of which waited for: 4 -> 5; matrix products, arithmetic and copies ran while one was open for 0% -> 0% of each run, Pallas kernels for 15% -> 24%
where the time goes in v10:
time: 42.8 us; the launch traced here: 42.6 us
  starting transfers between devices  22.2 us (52%)
  Pallas kernels  12.8 us (30%)
  waiting for transfers between devices  6.76 us (16%)
  between operations  0.76 us (2%)
    all_to_all x1, starting transfers between devices, shards(): lax.all_to_all(spread.reshape(TILES, 2 * ORI_DEV, TS), ('tile', 'orient')...  14.9 us
    ppermute x3, waiting for transfers between devices, halo(): return lax.ppermute(block, ('tile', 'orient'), route)  5.42 us
    ppermute x3, starting transfers between devices, halo(): return lax.ppermute(block, ('tile', 'orient'), route)  3.88 us
    ppermute x3, starting transfers between devices, sent(): lax.ppermute(piece, 'orient', [(i, i ^ bits) for i in range(MEMBERS)])  3.48 us
    pallas_call x2, Pallas kernels, spectra(): call(template_kernel, shape_of((ORI_DEV, 4 * PAIRS, HALF)), [VMEM] * 3, [...  2.84 us
    pallas_call x1, Pallas kernels, shards(): call(own_kernel, wide, [SMEM] + [VMEM] * 6, [pltpu.VMEM((4 * PAIRS, HALF)...  2.69 us
    pallas_call x2, Pallas kernels, far(): call(far_kernel, out, [VMEM] * 4, [inner], flops=1000000000)  2.26 us
    pallas_call x1, Pallas kernels, shards(): call(prepare_kernel, (shape_of((TILES // 2, 2, 2 * ORI_DEV, TS)), shape_o...  1.82 us
  transfers between devices with their start and end apart: 7, of which 5 were waited for; matrix products, arithmetic and copies ran while one was open for 0% of the time, Pallas kernels for 24%

profile of v10, /device:TPU:1, one launch (start us, length us, event | category | flops | bytes accessed | tf_op | source)
XLA Modules:
  0.0 42.6 jit_solution(10098325903199444025)
XLA Ops:
  0.6 1.8 %shard_map.86 = (bf16[32,2,16,128]{3,2,1,0:T(8,128)(2,1)}, bf16[384,128]{1,0:T(8,128)(2,1)S(1)}, bf16[128,384]{1,0:T(8,128)(2,1)S(1)}, bf16[128,128]{1,0:T(8,128)(2,1)S(1)}) custom-call(s32[32]{0:T(128)} %ids_hbm.1, bf16[1,384,384]{2,1,0:T(8,128)(2,1)} %refs_4_.1, bf16[256,256]{1,0:T(8,128)(2,1)} %stack_hbm.1), custom_call_target="tpu_custom_call" | custom-call | bytes 2097152 | tf_op jit(solution)/shard_map/pallas_call | solution.py:251
  2.5 14.9 %all-to-all-start = ((bf16[64,16,128]{2,1,0:T(8,128)(2,1)}), bf16[64,16,128]{2,1,0:T(8,128)(2,1)S(1)}, u32[]{:S(2)}, u32[]{:S(2)}) async-start(bf16[64,16,128]{2,1,0:T(8,128)(2,1)} %bitcast.1), calls=%async_computation | async-start | bytes 524288 | tf_op jit(solution)/shard_map/all_to_all | solution.py:269
  17.3 1.3 %collective-permute-start = (bf16[128,128]{1,0:T(8,128)(2,1)S(1)}, bf16[128,128]{1,0:T(8,128)(2,1)S(1)}, u32[]{:S(2)}, u32[]{:S(2)}) collective-permute-start(bf16[128,128]{1,0:T(8,128)(2,1)S(1)} %get-tuple-element.14.refs_5_), channel_id=1, source_target_pairs={{38,0},{39,1},{36,2},{37,3},{42,4},{43,5},{40,6},{41,7},{46,8},{47... | collective-permute-start | bytes 98312 | tf_op jit(solution)/shard_map/ppermute | solution.py:247
  18.6 1.3 %collective-permute-start.1 = (bf16[384,128]{1,0:T(8,128)(2,1)S(1)}, bf16[384,128]{1,0:T(8,128)(2,1)S(1)}, u32[]{:S(2)}, u32[]{:S(2)}) collective-permute-start(bf16[384,128]{1,0:T(8,128)(2,1)S(1)} %get-tuple-element.16), channel_id=1, source_target_pairs={{6,0},{7,1},{4,2},{5,3},{10,4},{11,5},{8,6},{9,7},{14,8},{15,9},{1... | collective-permute-start | bytes 294920 | tf_op jit(solution)/shard_map/ppermute | solution.py:247
  19.9 1.3 %collective-permute-start.2 = (bf16[128,384]{1,0:T(8,128)(2,1)S(1)}, bf16[128,384]{1,0:T(8,128)(2,1)S(1)}, u32[]{:S(2)}, u32[]{:S(2)}) collective-permute-start(bf16[128,384]{1,0:T(8,128)(2,1)S(1)} %get-tuple-element.17), channel_id=1, source_target_pairs={{32,0},{33,1},{34,2},{35,3},{36,4},{37,5},{38,6},{39,7},{40,8},{41... | collective-permute-start | bytes 294920 | tf_op jit(solution)/shard_map/ppermute | solution.py:247
  21.2 1.5 %shard_map.87 = (bf16[512,512]{1,0:T(8,128)(2,1)S(1)}, bf16[512,448]{1,0:T(8,128)(2,1)S(1)}, bf16[96,256]{1,0:T(8,128)(2,1)S(1)}, bf16[512,384]{1,0:T(8,128)(2,1)S(1)}, bf16[1,384,384]{2,1,0:T(8,128)(2,1)S(1)}) custom-call(bf16[512,512]{1,0:T(8,128)(2,1)} %constant.12.clone.refs_0_, bf16[512,448]{1,0:T(8,128)(2,1)} %constant.13.clone.refs_1_, ...), custom_call_target="tpu_custom_call" | custom-call | flops 10000000000 | bytes 2097152 | tf_op jit(solution)/shard_map/pallas_call | solution.py:273
  22.7 3.1 %collective-permute-done.refs_0_ = bf16[128,128]{1,0:T(8,128)(2,1)S(1)} collective-permute-done((bf16[128,128]{1,0:T(8,128)(2,1)S(1)}, bf16[128,128]{1,0:T(8,128)(2,1)S(1)}, u32[]{:S(2)}, u32[]{:S(2)}) %collective-permute-start) | collective-permute-done | bytes 32800 | tf_op jit(solution)/shard_map/ppermute | solution.py:247
  25.8 2.3 %collective-permute-done.1.refs_1_ = bf16[384,128]{1,0:T(8,128)(2,1)S(1)} collective-permute-done((bf16[384,128]{1,0:T(8,128)(2,1)S(1)}, bf16[384,128]{1,0:T(8,128)(2,1)S(1)}, u32[]{:S(2)}, u32[]{:S(2)}) %collective-permute-start.1) | collective-permute-done | bytes 98336 | tf_op jit(solution)/shard_map/ppermute | solution.py:247
  28.1 0.0 collective-permute-done.2.refs_2_
  28.1 1.0 %shard_map.88 = (bf16[512,256]{1,0:T(8,128)(2,1)S(1)}, bf16[512,256]{1,0:T(8,128)(2,1)S(1)}, bf16[2,512,256]{2,1,0:T(8,128)(2,1)S(1)}) custom-call(s32[1]{0:T(128)} %bitcast.member_ref, bf16[128,128]{1,0:T(8,128)(2,1)S(1)} %collective-permute-done.refs_0_, bf16[384,128]{1,0:T(8,128)(2,1)S(1)} %collective-permute-done.1.refs_1_, ...), custom_call_target="tpu_custom_call" | custom-call | flops 1600000000 | bytes 2097152 | tf_op jit(solution)/shard_map/pallas_call | solution.py:299
  29.1 0.1 all-to-all-done.pixels_ref
  29.2 3.3 %collective-permute-start.3 = (bf16[64,16,128]{2,1,0:T(8,128)(2,1)S(1)}, bf16[64,16,128]{2,1,0:T(8,128)(2,1)S(1)}, u32[]{:S(2)}, u32[]{:S(2)}) collective-permute-start(bf16[64,16,128]{2,1,0:T(8,128)(2,1)S(1)} %all-to-all-done.pixels_ref), channel_id=1, source_target_pairs={{0,1},{1,0},{2,3},{3,2},{4,5},{5,4},{6,7},{7,6},{8,9},{9,8},{10,11... | collective-permute-start | bytes 786440 | tf_op jit(solution)/shard_map/ppermute | solution.py:286
  32.5 1.4 %shard_map.89.mine_ref.template_ref = bf16[8,512,256]{2,1,0:T(8,128)(2,1)S(1)} custom-call(bf16[64,16,128]{2,1,0:T(8,128)(2,1)S(1)} %all-to-all-done.pixels_ref, bf16[512,512]{1,0:T(8,128)(2,1)S(1)} %get-tuple-element.19.refs_4_.col_ref, bf16[512,448]{1,0:T(8,128)(2,1)S(1)} %get-tuple-element.15.refs_5_.row_ref), custom_call_target="tpu_custom_call" | custom-call | flops 10000000000 | bytes 2097152 | tf_op jit(solution)/shard_map/pallas_call | solution.py:290
  34.0 1.1 %shard_map.93 = bf16[2,96,384]{2,1,0:T(8,128)(2,1)S(1)} custom-call(bf16[512,256]{1,0:T(8,128)(2,1)S(1)} %get-tuple-element.25.image_ref, bf16[8,512,256]{2,1,0:T(8,128)(2,1)S(1)} %shard_map.89.mine_ref.template_ref, bf16[96,256]{1,0:T(8,128)(2,1)S(1)} %get-tuple-element.22.inv_row_ref, bf16[512,384]{1,0:T(8,128)(2,1)S(1)} %get-tuple-element.23.inv_col_ref), custom_call_target="tpu_custom_call" | custom-call | flops 1000000000 | bytes 2097152 | tf_op jit(solution)/shard_map/pallas_call | solution.py:309
  35.1 0.1 collective-permute-start.4
  35.2 1.1 %shard_map.92.mine_ref = f32[2,96,384]{2,1,0:T(8,128)S(1)} custom-call(bf16[512,256]{1,0:T(8,128)(2,1)S(1)} %get-tuple-element.24.image_ref, bf16[8,512,256]{2,1,0:T(8,128)(2,1)S(1)} %shard_map.89.mine_ref.template_ref, bf16[96,256]{1,0:T(8,128)(2,1)S(1)} %get-tuple-element.22.inv_row_ref, bf16[512,384]{1,0:T(8,128)(2,1)S(1)} %get-tuple-element.23.inv_col_ref), custom_call_target="tpu_custom_call" | custom-call | flops 1000000000 | bytes 2097152 | tf_op jit(solution)/shard_map/pallas_call | solution.py:309
  36.3 0.2 collective-permute-done.4.other_ref
  36.6 0.1 collective-permute-start.5
  36.7 0.0 collective-permute-done.3.pixels_ref
  36.7 1.4 %shard_map.90.other_ref = bf16[8,512,256]{2,1,0:T(8,128)(2,1)S(1)} custom-call(bf16[64,16,128]{2,1,0:T(8,128)(2,1)S(1)} %collective-permute-done.3.pixels_ref, bf16[512,512]{1,0:T(8,128)(2,1)S(1)} %get-tuple-element.19.refs_4_.col_ref, bf16[512,448]{1,0:T(8,128)(2,1)S(1)} %get-tuple-element.15.refs_5_.row_ref), custom_call_target="tpu_custom_call" | custom-call | flops 10000000000 | bytes 2097152 | tf_op jit(solution)/shard_map/pallas_call | solution.py:290
  38.1 2.7 %shard_map.91.own_ref = f32[2,96,384]{2,1,0:T(8,128)S(1)} custom-call(s32[1]{0:T(128)} %bitcast.member_ref, bf16[512,448]{1,0:T(8,128)(2,1)S(1)} %get-tuple-element.15.refs_5_.row_ref, bf16[2,512,256]{2,1,0:T(8,128)(2,1)S(1)} %get-tuple-element.20.g_ref, bf16[8,512,256]{2,1,0:T(8,128)(2,1)S(1)} %shard_map.89.mine_ref.template_ref, ...), custom_call_target="tpu_custom_call" | custom-call | flops 2000000000 | bytes 2097152 | tf_op jit(solution)/shard_map/pallas_call | solution.py:317
  40.8 1.0 %collective-permute-done.5.far_ref = bf16[2,96,384]{2,1,0:T(8,128)(2,1)S(1)} collective-permute-done((bf16[2,96,384]{2,1,0:T(8,128)(2,1)S(1)}, bf16[2,96,384]{2,1,0:T(8,128)(2,1)S(1)}, u32[]{:S(2)}, u32[]{:S(2)}) %collective-permute-start.5) | collective-permute-done | bytes 147488 | tf_op jit(solution)/shard_map/ppermute | solution.py:286
  41.8 0.7 %shard_map.95 = (f32[1,96,384]{2,1,0:T(8,128)}, f32[1,96,384]{2,1,0:T(8,128)}) custom-call(f32[2,96,384]{2,1,0:T(8,128)S(1)} %shard_map.91.own_ref, bf16[2,96,384]{2,1,0:T(8,128)(2,1)S(1)} %collective-permute-done.5.far_ref), custom_call_target="tpu_custom_call" | custom-call | bytes 2097152 | tf_op jit(solution)/shard_map/pallas_call | solution.py:325
  (1 shorter events, 0.0 us)
Async XLA Ops:
  2.5 26.8 %all-to-all-start = ((bf16[64,16,128]{2,1,0:T(8,128)(2,1)}), bf16[64,16,128]{2,1,0:T(8,128)(2,1)S(1)}, u32[]{:S(2)}, u32[]{:S(2)}) async-start(bf16[64,16,128]{2,1,0:T(8,128)(2,1)} %bitcast.1), calls=%async_computation | async-start | bytes 524288 | tf_op jit(solution)/shard_map/all_to_all | solution.py:269
  17.3 8.5 %collective-permute-start = (bf16[128,128]{1,0:T(8,128)(2,1)S(1)}, bf16[128,128]{1,0:T(8,128)(2,1)S(1)}, u32[]{:S(2)}, u32[]{:S(2)}) collective-permute-start(bf16[128,128]{1,0:T(8,128)(2,1)S(1)} %get-tuple-element.14.refs_5_), channel_id=1, source_target_pairs={{38,0},{39,1},{36,2},{37,3},{42,4},{43,5},{40,6},{41,7},{46,8},{47... | collective-permute-start | bytes 98312 | tf_op jit(solution)/shard_map/ppermute | solution.py:247
  18.6 9.5 %collective-permute-start.1 = (bf16[384,128]{1,0:T(8,128)(2,1)S(1)}, bf16[384,128]{1,0:T(8,128)(2,1)S(1)}, u32[]{:S(2)}, u32[]{:S(2)}) collective-permute-start(bf16[384,128]{1,0:T(8,128)(2,1)S(1)} %get-tuple-element.16), channel_id=1, source_target_pairs={{6,0},{7,1},{4,2},{5,3},{10,4},{11,5},{8,6},{9,7},{14,8},{15,9},{1... | collective-permute-start | bytes 294920 | tf_op jit(solution)/shard_map/ppermute | solution.py:247
  19.9 8.2 %collective-permute-start.2 = (bf16[128,384]{1,0:T(8,128)(2,1)S(1)}, bf16[128,384]{1,0:T(8,128)(2,1)S(1)}, u32[]{:S(2)}, u32[]{:S(2)}) collective-permute-start(bf16[128,384]{1,0:T(8,128)(2,1)S(1)} %get-tuple-element.17), channel_id=1, source_target_pairs={{32,0},{33,1},{34,2},{35,3},{36,4},{37,5},{38,6},{39,7},{40,8},{41... | collective-permute-start | bytes 294920 | tf_op jit(solution)/shard_map/ppermute | solution.py:247
  29.2 7.5 %collective-permute-start.3 = (bf16[64,16,128]{2,1,0:T(8,128)(2,1)S(1)}, bf16[64,16,128]{2,1,0:T(8,128)(2,1)S(1)}, u32[]{:S(2)}, u32[]{:S(2)}) collective-permute-start(bf16[64,16,128]{2,1,0:T(8,128)(2,1)S(1)} %all-to-all-done.pixels_ref), channel_id=1, source_target_pairs={{0,1},{1,0},{2,3},{3,2},{4,5},{5,4},{6,7},{7,6},{8,9},{9,8},{10,11... | collective-permute-start | bytes 786440 | tf_op jit(solution)/shard_map/ppermute | solution.py:286
  35.1 1.5 %collective-permute-start.4 = (bf16[2,96,384]{2,1,0:T(8,128)(2,1)S(1)}, bf16[2,96,384]{2,1,0:T(8,128)(2,1)S(1)}, u32[]{:S(2)}, u32[]{:S(2)}) collective-permute-start(bf16[2,96,384]{2,1,0:T(8,128)(2,1)S(1)} %shard_map.93), channel_id=1, source_target_pairs={{0,1},{1,0},{2,3},{3,2},{4,5},{5,4},{6,7},{7,6},{8,9},{9,8},{10,11... | collective-permute-start | bytes 442376 | tf_op jit(solution)/shard_map/ppermute | solution.py:286
  36.6 5.2 %collective-permute-start.5 = (bf16[2,96,384]{2,1,0:T(8,128)(2,1)S(1)}, bf16[2,96,384]{2,1,0:T(8,128)(2,1)S(1)}, u32[]{:S(2)}, u32[]{:S(2)}) collective-permute-start(bf16[2,96,384]{2,1,0:T(8,128)(2,1)S(1)} %shard_map.94), channel_id=1, source_target_pairs={{0,2},{1,3},{2,0},{3,1},{4,6},{5,7},{6,4},{7,5},{8,10},{9,11},{10,... | collective-permute-start | bytes 442376 | tf_op jit(solution)/shard_map/ppermute | solution.py:286

commit v11 on v10

--- a/solution.py
+++ b/solution.py
@@ -292,7 +292,7 @@
             shape_of((ORI_DEV, 4 * PAIRS, HALF)),
             [VMEM] * 3,
             [pltpu.VMEM((TS * ORI_DEV, TS), jnp.float32)],
-            flops=10000000000,
+            flops=1000000000,
         )(group, columns, rows)
 
     spectrum = shape_of((4 * PAIRS, HALF))
@@ -306,7 +306,7 @@
     piece, wide = shape_of((2, ROWS, CORE)), shape_of((2, ROWS, CORE), jnp.float32)
 
     def far(image, out):
-        return call(far_kernel, out, [VMEM] * 4, [inner], flops=1000000000)(image, mine, *tables)
+        return call(far_kernel, out, [VMEM] * 4, [inner], flops=10000000000)(image, mine, *tables)
 
     mine = spectra(pixels)
     across = sent(far(image_across, piece), CORE_BIT)

time: 42.8 us -> 42.6 us (level)
  transfers between devices with their start and end apart: 7 -> 7, of which waited for: 5 -> 5; matrix products, arithmetic and copies ran while one was open for 0% -> 0% of each run, Pallas kernels for 24% -> 18%
where the time goes in v11:
time: 42.6 us; the launch traced here: 42.3 us
  starting transfers between devices  22.3 us (52%)
  Pallas kernels  12.8 us (30%)
  waiting for transfers between devices  6.41 us (15%)
  between operations  0.76 us (2%)
    all_to_all x1, starting transfers between devices, shards(): lax.all_to_all(spread.reshape(TILES, 2 * ORI_DEV, TS), ('tile', 'orient')...  14.9 us
    ppermute x3, waiting for transfers between devices, halo(): return lax.ppermute(block, ('tile', 'orient'), route)  5.42 us
    ppermute x3, starting transfers between devices, halo(): return lax.ppermute(block, ('tile', 'orient'), route)  3.88 us
    ppermute x3, starting transfers between devices, sent(): lax.ppermute(piece, 'orient', [(i, i ^ bits) for i in range(MEMBERS)])  3.57 us
    pallas_call x2, Pallas kernels, spectra(): call(template_kernel, shape_of((ORI_DEV, 4 * PAIRS, HALF)), [VMEM] * 3, [...  2.84 us
    pallas_call x1, Pallas kernels, shards(): call(own_kernel, wide, [SMEM] + [VMEM] * 6, [pltpu.VMEM((4 * PAIRS, HALF)...  2.69 us
    pallas_call x2, Pallas kernels, far(): call(far_kernel, out, [VMEM] * 4, [inner], flops=10000000000)  2.26 us
    pallas_call x1, Pallas kernels, shards(): call(prepare_kernel, (shape_of((TILES // 2, 2, 2 * ORI_DEV, TS)), shape_o...  1.82 us
  transfers between devices with their start and end apart: 7, of which 5 were waited for; matrix products, arithmetic and copies ran while one was open for 0% of the time, Pallas kernels for 18%

profile of v11, /device:TPU:1, one launch (start us, length us, event | category | flops | bytes accessed | tf_op | source)
XLA Modules:
  0.0 42.3 jit_solution(7716243533677208603)
XLA Ops:
  0.6 1.8 %shard_map.86 = (bf16[32,2,16,128]{3,2,1,0:T(8,128)(2,1)}, bf16[384,128]{1,0:T(8,128)(2,1)S(1)}, bf16[128,384]{1,0:T(8,128)(2,1)S(1)}, bf16[128,128]{1,0:T(8,128)(2,1)S(1)}) custom-call(s32[32]{0:T(128)} %ids_hbm.1, bf16[1,384,384]{2,1,0:T(8,128)(2,1)} %refs_4_.1, bf16[256,256]{1,0:T(8,128)(2,1)} %stack_hbm.1), custom_call_target="tpu_custom_call" | custom-call | bytes 2097152 | tf_op jit(solution)/shard_map/pallas_call | solution.py:251
  2.5 14.9 %all-to-all-start = ((bf16[64,16,128]{2,1,0:T(8,128)(2,1)}), bf16[64,16,128]{2,1,0:T(8,128)(2,1)S(1)}, u32[]{:S(2)}, u32[]{:S(2)}) async-start(bf16[64,16,128]{2,1,0:T(8,128)(2,1)} %bitcast.1), calls=%async_computation | async-start | bytes 524288 | tf_op jit(solution)/shard_map/all_to_all | solution.py:269
  17.3 1.3 %collective-permute-start = (bf16[128,128]{1,0:T(8,128)(2,1)S(1)}, bf16[128,128]{1,0:T(8,128)(2,1)S(1)}, u32[]{:S(2)}, u32[]{:S(2)}) collective-permute-start(bf16[128,128]{1,0:T(8,128)(2,1)S(1)} %get-tuple-element.14.refs_5_), channel_id=1, source_target_pairs={{38,0},{39,1},{36,2},{37,3},{42,4},{43,5},{40,6},{41,7},{46,8},{47... | collective-permute-start | bytes 98312 | tf_op jit(solution)/shard_map/ppermute | solution.py:247
  18.6 1.3 %collective-permute-start.1 = (bf16[384,128]{1,0:T(8,128)(2,1)S(1)}, bf16[384,128]{1,0:T(8,128)(2,1)S(1)}, u32[]{:S(2)}, u32[]{:S(2)}) collective-permute-start(bf16[384,128]{1,0:T(8,128)(2,1)S(1)} %get-tuple-element.16), channel_id=1, source_target_pairs={{6,0},{7,1},{4,2},{5,3},{10,4},{11,5},{8,6},{9,7},{14,8},{15,9},{1... | collective-permute-start | bytes 294920 | tf_op jit(solution)/shard_map/ppermute | solution.py:247
  19.9 1.3 %collective-permute-start.2 = (bf16[128,384]{1,0:T(8,128)(2,1)S(1)}, bf16[128,384]{1,0:T(8,128)(2,1)S(1)}, u32[]{:S(2)}, u32[]{:S(2)}) collective-permute-start(bf16[128,384]{1,0:T(8,128)(2,1)S(1)} %get-tuple-element.17), channel_id=1, source_target_pairs={{32,0},{33,1},{34,2},{35,3},{36,4},{37,5},{38,6},{39,7},{40,8},{41... | collective-permute-start | bytes 294920 | tf_op jit(solution)/shard_map/ppermute | solution.py:247
  21.2 1.5 %shard_map.87 = (bf16[512,512]{1,0:T(8,128)(2,1)S(1)}, bf16[512,448]{1,0:T(8,128)(2,1)S(1)}, bf16[96,256]{1,0:T(8,128)(2,1)S(1)}, bf16[512,384]{1,0:T(8,128)(2,1)S(1)}, bf16[1,384,384]{2,1,0:T(8,128)(2,1)S(1)}) custom-call(bf16[512,512]{1,0:T(8,128)(2,1)} %constant.12.clone.refs_0_, bf16[512,448]{1,0:T(8,128)(2,1)} %constant.13.clone.refs_1_, ...), custom_call_target="tpu_custom_call" | custom-call | flops 10000000000 | bytes 2097152 | tf_op jit(solution)/shard_map/pallas_call | solution.py:273
  22.7 3.1 %collective-permute-done.refs_0_ = bf16[128,128]{1,0:T(8,128)(2,1)S(1)} collective-permute-done((bf16[128,128]{1,0:T(8,128)(2,1)S(1)}, bf16[128,128]{1,0:T(8,128)(2,1)S(1)}, u32[]{:S(2)}, u32[]{:S(2)}) %collective-permute-start) | collective-permute-done | bytes 32800 | tf_op jit(solution)/shard_map/ppermute | solution.py:247
  25.8 2.3 %collective-permute-done.1.refs_1_ = bf16[384,128]{1,0:T(8,128)(2,1)S(1)} collective-permute-done((bf16[384,128]{1,0:T(8,128)(2,1)S(1)}, bf16[384,128]{1,0:T(8,128)(2,1)S(1)}, u32[]{:S(2)}, u32[]{:S(2)}) %collective-permute-start.1) | collective-permute-done | bytes 98336 | tf_op jit(solution)/shard_map/ppermute | solution.py:247
  28.1 0.0 collective-permute-done.2.refs_2_
  28.1 1.0 %shard_map.88 = (bf16[512,256]{1,0:T(8,128)(2,1)S(1)}, bf16[512,256]{1,0:T(8,128)(2,1)S(1)}, bf16[2,512,256]{2,1,0:T(8,128)(2,1)S(1)}) custom-call(s32[1]{0:T(128)} %bitcast.member_ref, bf16[128,128]{1,0:T(8,128)(2,1)S(1)} %collective-permute-done.refs_0_, bf16[384,128]{1,0:T(8,128)(2,1)S(1)} %collective-permute-done.1.refs_1_, ...), custom_call_target="tpu_custom_call" | custom-call | flops 1600000000 | bytes 2097152 | tf_op jit(solution)/shard_map/pallas_call | solution.py:299
  29.1 0.1 all-to-all-done.pixels_ref
  29.2 1.4 %shard_map.89.mine_ref.template_ref = bf16[8,512,256]{2,1,0:T(8,128)(2,1)S(1)} custom-call(bf16[64,16,128]{2,1,0:T(8,128)(2,1)S(1)} %all-to-all-done.pixels_ref, bf16[512,512]{1,0:T(8,128)(2,1)S(1)} %get-tuple-element.19.refs_4_.col_ref, bf16[512,448]{1,0:T(8,128)(2,1)S(1)} %get-tuple-element.15.refs_5_.row_ref), custom_call_target="tpu_custom_call" | custom-call | flops 1000000000 | bytes 2097152 | tf_op jit(solution)/shard_map/pallas_call | solution.py:290
  30.7 1.1 %shard_map.93 = bf16[2,96,384]{2,1,0:T(8,128)(2,1)S(1)} custom-call(bf16[512,256]{1,0:T(8,128)(2,1)S(1)} %get-tuple-element.25.image_ref, bf16[8,512,256]{2,1,0:T(8,128)(2,1)S(1)} %shard_map.89.mine_ref.template_ref, bf16[96,256]{1,0:T(8,128)(2,1)S(1)} %get-tuple-element.22.inv_row_ref, bf16[512,384]{1,0:T(8,128)(2,1)S(1)} %get-tuple-element.23.inv_col_ref), custom_call_target="tpu_custom_call" | custom-call | flops 10000000000 | bytes 2097152 | tf_op jit(solution)/shard_map/pallas_call | solution.py:309
  31.8 3.4 %collective-permute-start.4 = (bf16[2,96,384]{2,1,0:T(8,128)(2,1)S(1)}, bf16[2,96,384]{2,1,0:T(8,128)(2,1)S(1)}, u32[]{:S(2)}, u32[]{:S(2)}) collective-permute-start(bf16[2,96,384]{2,1,0:T(8,128)(2,1)S(1)} %shard_map.93), channel_id=1, source_target_pairs={{0,1},{1,0},{2,3},{3,2},{4,5},{5,4},{6,7},{7,6},{8,9},{9,8},{10,11... | collective-permute-start | bytes 442376 | tf_op jit(solution)/shard_map/ppermute | solution.py:286
  35.2 0.1 collective-permute-start.3
  35.3 1.1 %shard_map.92.mine_ref = f32[2,96,384]{2,1,0:T(8,128)S(1)} custom-call(bf16[512,256]{1,0:T(8,128)(2,1)S(1)} %get-tuple-element.24.image_ref, bf16[8,512,256]{2,1,0:T(8,128)(2,1)S(1)} %shard_map.89.mine_ref.template_ref, bf16[96,256]{1,0:T(8,128)(2,1)S(1)} %get-tuple-element.22.inv_row_ref, bf16[512,384]{1,0:T(8,128)(2,1)S(1)} %get-tuple-element.23.inv_col_ref), custom_call_target="tpu_custom_call" | custom-call | flops 10000000000 | bytes 2097152 | tf_op jit(solution)/shard_map/pallas_call | solution.py:309
  36.4 0.0 collective-permute-done.4.other_ref
  36.5 0.1 collective-permute-start.5
  36.6 0.2 collective-permute-done.3.pixels_ref
  36.7 1.4 %shard_map.90.other_ref = bf16[8,512,256]{2,1,0:T(8,128)(2,1)S(1)} custom-call(bf16[64,16,128]{2,1,0:T(8,128)(2,1)S(1)} %collective-permute-done.3.pixels_ref, bf16[512,512]{1,0:T(8,128)(2,1)S(1)} %get-tuple-element.19.refs_4_.col_ref, bf16[512,448]{1,0:T(8,128)(2,1)S(1)} %get-tuple-element.15.refs_5_.row_ref), custom_call_target="tpu_custom_call" | custom-call | flops 1000000000 | bytes 2097152 | tf_op jit(solution)/shard_map/pallas_call | solution.py:290
  38.2 2.7 %shard_map.91.own_ref = f32[2,96,384]{2,1,0:T(8,128)S(1)} custom-call(s32[1]{0:T(128)} %bitcast.member_ref, bf16[512,448]{1,0:T(8,128)(2,1)S(1)} %get-tuple-element.15.refs_5_.row_ref, bf16[2,512,256]{2,1,0:T(8,128)(2,1)S(1)} %get-tuple-element.20.g_ref, bf16[8,512,256]{2,1,0:T(8,128)(2,1)S(1)} %shard_map.89.mine_ref.template_ref, ...), custom_call_target="tpu_custom_call" | custom-call | flops 2000000000 | bytes 2097152 | tf_op jit(solution)/shard_map/pallas_call | solution.py:317
  40.9 0.7 %collective-permute-done.5.far_ref = bf16[2,96,384]{2,1,0:T(8,128)(2,1)S(1)} collective-permute-done((bf16[2,96,384]{2,1,0:T(8,128)(2,1)S(1)}, bf16[2,96,384]{2,1,0:T(8,128)(2,1)S(1)}, u32[]{:S(2)}, u32[]{:S(2)}) %collective-permute-start.5) | collective-permute-done | bytes 147488 | tf_op jit(solution)/shard_map/ppermute | solution.py:286
  41.6 0.7 %shard_map.95 = (f32[1,96,384]{2,1,0:T(8,128)}, f32[1,96,384]{2,1,0:T(8,128)}) custom-call(f32[2,96,384]{2,1,0:T(8,128)S(1)} %shard_map.91.own_ref, bf16[2,96,384]{2,1,0:T(8,128)(2,1)S(1)} %collective-permute-done.5.far_ref), custom_call_target="tpu_custom_call" | custom-call | bytes 2097152 | tf_op jit(solution)/shard_map/pallas_call | solution.py:325
  (1 shorter events, 0.0 us)
Async XLA Ops:
  2.5 26.8 %all-to-all-start = ((bf16[64,16,128]{2,1,0:T(8,128)(2,1)}), bf16[64,16,128]{2,1,0:T(8,128)(2,1)S(1)}, u32[]{:S(2)}, u32[]{:S(2)}) async-start(bf16[64,16,128]{2,1,0:T(8,128)(2,1)} %bitcast.1), calls=%async_computation | async-start | bytes 524288 | tf_op jit(solution)/shard_map/all_to_all | solution.py:269
  17.3 8.5 %collective-permute-start = (bf16[128,128]{1,0:T(8,128)(2,1)S(1)}, bf16[128,128]{1,0:T(8,128)(2,1)S(1)}, u32[]{:S(2)}, u32[]{:S(2)}) collective-permute-start(bf16[128,128]{1,0:T(8,128)(2,1)S(1)} %get-tuple-element.14.refs_5_), channel_id=1, source_target_pairs={{38,0},{39,1},{36,2},{37,3},{42,4},{43,5},{40,6},{41,7},{46,8},{47... | collective-permute-start | bytes 98312 | tf_op jit(solution)/shard_map/ppermute | solution.py:247
  18.6 9.5 %collective-permute-start.1 = (bf16[384,128]{1,0:T(8,128)(2,1)S(1)}, bf16[384,128]{1,0:T(8,128)(2,1)S(1)}, u32[]{:S(2)}, u32[]{:S(2)}) collective-permute-start(bf16[384,128]{1,0:T(8,128)(2,1)S(1)} %get-tuple-element.16), channel_id=1, source_target_pairs={{6,0},{7,1},{4,2},{5,3},{10,4},{11,5},{8,6},{9,7},{14,8},{15,9},{1... | collective-permute-start | bytes 294920 | tf_op jit(solution)/shard_map/ppermute | solution.py:247
  19.9 8.2 %collective-permute-start.2 = (bf16[128,384]{1,0:T(8,128)(2,1)S(1)}, bf16[128,384]{1,0:T(8,128)(2,1)S(1)}, u32[]{:S(2)}, u32[]{:S(2)}) collective-permute-start(bf16[128,384]{1,0:T(8,128)(2,1)S(1)} %get-tuple-element.17), channel_id=1, source_target_pairs={{32,0},{33,1},{34,2},{35,3},{36,4},{37,5},{38,6},{39,7},{40,8},{41... | collective-permute-start | bytes 294920 | tf_op jit(solution)/shard_map/ppermute | solution.py:247
  31.8 4.6 %collective-permute-start.4 = (bf16[2,96,384]{2,1,0:T(8,128)(2,1)S(1)}, bf16[2,96,384]{2,1,0:T(8,128)(2,1)S(1)}, u32[]{:S(2)}, u32[]{:S(2)}) collective-permute-start(bf16[2,96,384]{2,1,0:T(8,128)(2,1)S(1)} %shard_map.93), channel_id=1, source_target_pairs={{0,1},{1,0},{2,3},{3,2},{4,5},{5,4},{6,7},{7,6},{8,9},{9,8},{10,11... | collective-permute-start | bytes 442376 | tf_op jit(solution)/shard_map/ppermute | solution.py:286
  35.2 1.5 %collective-permute-start.3 = (bf16[64,16,128]{2,1,0:T(8,128)(2,1)S(1)}, bf16[64,16,128]{2,1,0:T(8,128)(2,1)S(1)}, u32[]{:S(2)}, u32[]{:S(2)}) collective-permute-start(bf16[64,16,128]{2,1,0:T(8,128)(2,1)S(1)} %all-to-all-done.pixels_ref), channel_id=1, source_target_pairs={{0,1},{1,0},{2,3},{3,2},{4,5},{5,4},{6,7},{7,6},{8,9},{9,8},{10,11... | collective-permute-start | bytes 786440 | tf_op jit(solution)/shard_map/ppermute | solution.py:286
  36.5 5.1 %collective-permute-start.5 = (bf16[2,96,384]{2,1,0:T(8,128)(2,1)S(1)}, bf16[2,96,384]{2,1,0:T(8,128)(2,1)S(1)}, u32[]{:S(2)}, u32[]{:S(2)}) collective-permute-start(bf16[2,96,384]{2,1,0:T(8,128)(2,1)S(1)} %shard_map.94), channel_id=1, source_target_pairs={{0,2},{1,3},{2,0},{3,1},{4,6},{5,7},{6,4},{7,5},{8,10},{9,11},{10,... | collective-permute-start | bytes 442376 | tf_op jit(solution)/shard_map/ppermute | solution.py:286

commit v12 on v11

--- a/solution.py
+++ b/solution.py
@@ -191,9 +191,15 @@
     out_ref[1] = (mine_ref[1] + other[1]).astype(out_ref.dtype)
 
 
-def own_kernel(member_ref, row_ref, g_ref, mine_ref, other_ref, inv_row_ref, inv_col_ref, out_ref, image_ref, inner_ref):
+def own_kernel(member_ref, row_ref, g_ref, template_ref, inv_row_ref, inv_col_ref, _, out_ref, image_ref, inner_ref):
     image_rows(member_ref, row_ref, g_ref, 0, image_ref)
-    block(image_ref, (mine_ref, other_ref), inv_row_ref, inv_col_ref, out_ref, inner_ref)
+    block(image_ref, (template_ref,), inv_row_ref, inv_col_ref, out_ref, inner_ref)
+
+
+def rest_kernel(image_ref, template_ref, inv_row_ref, inv_col_ref, part_ref, out_ref, inner_ref):
+    block(image_ref, (template_ref,), inv_row_ref, inv_col_ref, out_ref, inner_ref)
+    out_ref[0] = jnp.maximum(out_ref[0], part_ref[0])
+    out_ref[1] = out_ref[1] + part_ref[1]
 
 
 def finish_kernel(own_ref, far_ref, peak_ref, excess_ref):
@@ -312,15 +318,16 @@
     across = sent(far(image_across, piece), CORE_BIT)
     same = far(image_same, wide)
     merged = call(merge_kernel, piece, [VMEM] * 2, flops=100000000)(same, across)
+    part, image_own = call(
+        own_kernel,
+        (wide, spectrum),
+        [SMEM] + [VMEM] * 5 + [ANY],
+        [inner],
+        flops=20000000000,
+    )(member, rows, g, mine, *tables, merged)
     merged = sent(merged, CHIP_BIT)
     other = spectra(sent(pixels, CORE_BIT))
-    own = call(
-        own_kernel,
-        wide,
-        [SMEM] + [VMEM] * 6,
-        [pltpu.VMEM((4 * PAIRS, HALF), jnp.bfloat16), inner],
-        flops=2000000000,
-    )(member, rows, g, mine, other, *tables)
+    own = call(rest_kernel, wide, [VMEM] * 5, [inner], flops=1000000000)(image_own, other, *tables, part)
     out = shape_of((1, ROWS, CORE), jnp.float32)
     return call(finish_kernel, (out, out), [VMEM] * 2)(own, merged)
 

time: 42.6 us -> 51.5 us (1.21)
  starting transfers between devices: 22.3 us -> 27.5 us
  waiting for transfers between devices: 6.41 us -> 9.97 us
    all_to_all x1, waiting for transfers between devices: 0.12 us -> 9.33 us  [shards(): lax.all_to_all(spread.reshape(TILES, 2 * ORI_DEV, TS), ('tile', 'orient')...]
    ppermute x3, waiting for transfers between devices: 5.42 us -> 0.01 us  [halo(): return lax.ppermute(block, ('tile', 'orient'), route)]
    all_to_all x1, starting transfers between devices: 14.9 us -> 19.7 us  [shards(): lax.all_to_all(spread.reshape(TILES, 2 * ORI_DEV, TS), ('tile', 'orient')...]
    pallas_call x1 -> x2, Pallas kernels: 2.69 us -> 2.83 us  [the longest x1 1.69 us: shards(): call(own_kernel, (wide, spectrum), [SMEM] + [VMEM] * 5 + [ANY], [inner],...]
  transfers between devices with their start and end apart: 7 -> 7, of which waited for: 5 -> 2; matrix products, arithmetic and copies ran while one was open for 0% -> 0% of each run, Pallas kernels for 18% -> 15%
where the time goes in v12:
time: 51.5 us; the launch traced here: 51.2 us
  starting transfers between devices  27.5 us (53%)
  Pallas kernels  13 us (25%)
  waiting for transfers between devices  9.97 us (19%)
  between operations  0.79 us (2%)
    all_to_all x1, starting transfers between devices, shards(): lax.all_to_all(spread.reshape(TILES, 2 * ORI_DEV, TS), ('tile', 'orient')...  19.7 us
    all_to_all x1, waiting for transfers between devices, shards(): lax.all_to_all(spread.reshape(TILES, 2 * ORI_DEV, TS), ('tile', 'orient')...  9.33 us
    ppermute x3, starting transfers between devices, sent(): lax.ppermute(piece, 'orient', [(i, i ^ bits) for i in range(MEMBERS)])  3.92 us
    ppermute x3, starting transfers between devices, halo(): return lax.ppermute(block, ('tile', 'orient'), route)  3.88 us
    pallas_call x2, Pallas kernels, spectra(): call(template_kernel, shape_of((ORI_DEV, 4 * PAIRS, HALF)), [VMEM] * 3, [...  2.84 us
    pallas_call x2, Pallas kernels, far(): call(far_kernel, out, [VMEM] * 4, [inner], flops=10000000000)  2.26 us
    pallas_call x1, Pallas kernels, shards(): call(prepare_kernel, (shape_of((TILES // 2, 2, 2 * ORI_DEV, TS)), shape_o...  1.81 us
    pallas_call x1, Pallas kernels, shards(): call(own_kernel, (wide, spectrum), [SMEM] + [VMEM] * 5 + [ANY], [inner],...  1.69 us
  transfers between devices with their start and end apart: 7, of which 2 were waited for; matrix products, arithmetic and copies ran while one was open for 0% of the time, Pallas kernels for 15%

profile of v12, /device:TPU:1, one launch (start us, length us, event | category | flops | bytes accessed | tf_op | source)
XLA Modules:
  0.0 51.2 jit_solution(12001661106147619023)
XLA Ops:
  0.6 1.8 %shard_map.86 = (bf16[32,2,16,128]{3,2,1,0:T(8,128)(2,1)}, bf16[384,128]{1,0:T(8,128)(2,1)S(1)}, bf16[128,384]{1,0:T(8,128)(2,1)S(1)}, bf16[128,128]{1,0:T(8,128)(2,1)S(1)}) custom-call(s32[32]{0:T(128)} %ids_hbm.1, bf16[1,384,384]{2,1,0:T(8,128)(2,1)} %refs_4_.1, bf16[256,256]{1,0:T(8,128)(2,1)} %stack_hbm.1), custom_call_target="tpu_custom_call" | custom-call | bytes 2097152 | tf_op jit(solution)/shard_map/pallas_call | solution.py:257
  2.5 1.3 %collective-permute-start = (bf16[128,128]{1,0:T(8,128)(2,1)S(1)}, bf16[128,128]{1,0:T(8,128)(2,1)S(1)}, u32[]{:S(2)}, u32[]{:S(2)}) collective-permute-start(bf16[128,128]{1,0:T(8,128)(2,1)S(1)} %get-tuple-element.16.refs_5_), channel_id=1, source_target_pairs={{38,0},{39,1},{36,2},{37,3},{42,4},{43,5},{40,6},{41,7},{46,8},{47... | collective-permute-start | bytes 98312 | tf_op jit(solution)/shard_map/ppermute | solution.py:253
  3.8 1.3 %collective-permute-start.1 = (bf16[384,128]{1,0:T(8,128)(2,1)S(1)}, bf16[384,128]{1,0:T(8,128)(2,1)S(1)}, u32[]{:S(2)}, u32[]{:S(2)}) collective-permute-start(bf16[384,128]{1,0:T(8,128)(2,1)S(1)} %get-tuple-element.18), channel_id=1, source_target_pairs={{6,0},{7,1},{4,2},{5,3},{10,4},{11,5},{8,6},{9,7},{14,8},{15,9},{1... | collective-permute-start | bytes 294920 | tf_op jit(solution)/shard_map/ppermute | solution.py:253
  5.1 1.3 %collective-permute-start.2 = (bf16[128,384]{1,0:T(8,128)(2,1)S(1)}, bf16[128,384]{1,0:T(8,128)(2,1)S(1)}, u32[]{:S(2)}, u32[]{:S(2)}) collective-permute-start(bf16[128,384]{1,0:T(8,128)(2,1)S(1)} %get-tuple-element.19), channel_id=1, source_target_pairs={{32,0},{33,1},{34,2},{35,3},{36,4},{37,5},{38,6},{39,7},{40,8},{41... | collective-permute-start | bytes 294920 | tf_op jit(solution)/shard_map/ppermute | solution.py:253
  6.4 19.7 %all-to-all-start = ((bf16[64,16,128]{2,1,0:T(8,128)(2,1)}), bf16[64,16,128]{2,1,0:T(8,128)(2,1)S(1)}, u32[]{:S(2)}, u32[]{:S(2)}) async-start(bf16[64,16,128]{2,1,0:T(8,128)(2,1)} %bitcast.1), calls=%async_computation | async-start | bytes 524288 | tf_op jit(solution)/shard_map/all_to_all | solution.py:275
  26.0 1.5 %shard_map.87 = (bf16[512,512]{1,0:T(8,128)(2,1)S(1)}, bf16[512,448]{1,0:T(8,128)(2,1)S(1)}, bf16[96,256]{1,0:T(8,128)(2,1)S(1)}, bf16[512,384]{1,0:T(8,128)(2,1)S(1)}, bf16[1,384,384]{2,1,0:T(8,128)(2,1)S(1)}) custom-call(bf16[512,512]{1,0:T(8,128)(2,1)} %constant.12.clone.refs_0_, bf16[512,448]{1,0:T(8,128)(2,1)} %constant.13.clone.refs_1_, ...), custom_call_target="tpu_custom_call" | custom-call | flops 10000000000 | bytes 2097152 | tf_op jit(solution)/shard_map/pallas_call | solution.py:279
  27.5 0.0 collective-permute-done.refs_0_
  27.5 0.0 collective-permute-done.1.refs_1_
  27.5 0.0 collective-permute-done.2.refs_2_
  27.5 1.0 %shard_map.88 = (bf16[512,256]{1,0:T(8,128)(2,1)S(1)}, bf16[512,256]{1,0:T(8,128)(2,1)S(1)}, bf16[2,512,256]{2,1,0:T(8,128)(2,1)S(1)}) custom-call(s32[1]{0:T(128)} %bitcast.member_ref, bf16[128,128]{1,0:T(8,128)(2,1)S(1)} %collective-permute-done.refs_0_, bf16[384,128]{1,0:T(8,128)(2,1)S(1)} %collective-permute-done.1.refs_1_, ...), custom_call_target="tpu_custom_call" | custom-call | flops 1600000000 | bytes 2097152 | tf_op jit(solution)/shard_map/pallas_call | solution.py:305
  28.5 9.3 %all-to-all-done.pixels_ref = bf16[64,16,128]{2,1,0:T(8,128)(2,1)S(1)} async-done(((bf16[64,16,128]{2,1,0:T(8,128)(2,1)}), bf16[64,16,128]{2,1,0:T(8,128)(2,1)S(1)}, u32[]{:S(2)}, u32[]{:S(2)}) %all-to-all-start) | async-done | bytes 262176 | tf_op jit(solution)/shard_map/all_to_all | solution.py:275
  37.9 1.4 %shard_map.89.template_ref = bf16[8,512,256]{2,1,0:T(8,128)(2,1)S(1)} custom-call(bf16[64,16,128]{2,1,0:T(8,128)(2,1)S(1)} %all-to-all-done.pixels_ref, bf16[512,512]{1,0:T(8,128)(2,1)S(1)} %get-tuple-element.21.refs_4_.col_ref, bf16[512,448]{1,0:T(8,128)(2,1)S(1)} %get-tuple-element.17.refs_5_.row_ref), custom_call_target="tpu_custom_call" | custom-call | flops 1000000000 | bytes 2097152 | tf_op jit(solution)/shard_map/pallas_call | solution.py:296
  39.3 1.1 %shard_map.91 = bf16[2,96,384]{2,1,0:T(8,128)(2,1)S(1)} custom-call(bf16[512,256]{1,0:T(8,128)(2,1)S(1)} %get-tuple-element.27.image_ref, bf16[8,512,256]{2,1,0:T(8,128)(2,1)S(1)} %shard_map.89.template_ref, bf16[96,256]{1,0:T(8,128)(2,1)S(1)} %get-tuple-element.24.inv_row_ref, bf16[512,384]{1,0:T(8,128)(2,1)S(1)} %get-tuple-element.25.inv_col_ref), custom_call_target="tpu_custom_call" | custom-call | flops 10000000000 | bytes 2097152 | tf_op jit(solution)/shard_map/pallas_call | solution.py:315
  40.4 3.7 %collective-permute-start.3 = (bf16[2,96,384]{2,1,0:T(8,128)(2,1)S(1)}, bf16[2,96,384]{2,1,0:T(8,128)(2,1)S(1)}, u32[]{:S(2)}, u32[]{:S(2)}) collective-permute-start(bf16[2,96,384]{2,1,0:T(8,128)(2,1)S(1)} %shard_map.91), channel_id=1, source_target_pairs={{0,1},{1,0},{2,3},{3,2},{4,5},{5,4},{6,7},{7,6},{8,9},{9,8},{10,11... | collective-permute-start | bytes 442376 | tf_op jit(solution)/shard_map/ppermute | solution.py:292
  44.2 1.1 %shard_map.90.mine_ref = f32[2,96,384]{2,1,0:T(8,128)S(1)} custom-call(bf16[512,256]{1,0:T(8,128)(2,1)S(1)} %get-tuple-element.26.image_ref, bf16[8,512,256]{2,1,0:T(8,128)(2,1)S(1)} %shard_map.89.template_ref, bf16[96,256]{1,0:T(8,128)(2,1)S(1)} %get-tuple-element.24.inv_row_ref, bf16[512,384]{1,0:T(8,128)(2,1)S(1)} %get-tuple-element.25.inv_col_ref), custom_call_target="tpu_custom_call" | custom-call | flops 10000000000 | bytes 2097152 | tf_op jit(solution)/shard_map/pallas_call | solution.py:315
  45.3 0.1 collective-permute-start.4
  45.4 0.0 collective-permute-done.3.other_ref
  45.4 0.1 collective-permute-start.5
  45.5 1.7 %shard_map.93 = (f32[2,96,384]{2,1,0:T(8,128)S(1)}, bf16[512,256]{1,0:T(8,128)(2,1)S(1)}) custom-call(s32[1]{0:T(128)} %bitcast.member_ref, bf16[512,448]{1,0:T(8,128)(2,1)S(1)} %get-tuple-element.17.refs_5_.row_ref, bf16[2,512,256]{2,1,0:T(8,128)(2,1)S(1)} %get-tuple-element.22.g_ref, bf16[8,512,256]{2,1,0:T(8,128)(2,1)S(1)} %shard_map.89.template_ref, ...), custom_call_target="tpu_custom_call" | custom-call | flops 20000000000 | bytes 2097152 | tf_op jit(solution)/shard_map/pallas_call | solution.py:321
  47.2 0.0 collective-permute-done.4.pixels_ref
  47.2 1.4 %shard_map.94.template_ref = bf16[8,512,256]{2,1,0:T(8,128)(2,1)S(1)} custom-call(bf16[64,16,128]{2,1,0:T(8,128)(2,1)S(1)} %collective-permute-done.4.pixels_ref, bf16[512,512]{1,0:T(8,128)(2,1)S(1)} %get-tuple-element.21.refs_4_.col_ref, bf16[512,448]{1,0:T(8,128)(2,1)S(1)} %get-tuple-element.17.refs_5_.row_ref), custom_call_target="tpu_custom_call" | custom-call | flops 1000000000 | bytes 2097152 | tf_op jit(solution)/shard_map/pallas_call | solution.py:296
  48.7 1.1 %shard_map.95.own_ref = f32[2,96,384]{2,1,0:T(8,128)S(1)} custom-call(bf16[512,256]{1,0:T(8,128)(2,1)S(1)} %get-tuple-element.28.image_ref, bf16[8,512,256]{2,1,0:T(8,128)(2,1)S(1)} %shard_map.94.template_ref, bf16[96,256]{1,0:T(8,128)(2,1)S(1)} %get-tuple-element.24.inv_row_ref, bf16[512,384]{1,0:T(8,128)(2,1)S(1)} %get-tuple-element.25.inv_col_ref, ...), custom_call_target="tpu_custom_call" | custom-call | flops 1000000000 | bytes 2097152 | tf_op jit(solution)/shard_map/pallas_call | solution.py:330
  49.8 0.6 %collective-permute-done.5.far_ref = bf16[2,96,384]{2,1,0:T(8,128)(2,1)S(1)} collective-permute-done((bf16[2,96,384]{2,1,0:T(8,128)(2,1)S(1)}, bf16[2,96,384]{2,1,0:T(8,128)(2,1)S(1)}, u32[]{:S(2)}, u32[]{:S(2)}) %collective-permute-start.5) | collective-permute-done | bytes 147488 | tf_op jit(solution)/shard_map/ppermute | solution.py:292
  50.5 0.7 %shard_map.96 = (f32[1,96,384]{2,1,0:T(8,128)}, f32[1,96,384]{2,1,0:T(8,128)}) custom-call(f32[2,96,384]{2,1,0:T(8,128)S(1)} %shard_map.95.own_ref, bf16[2,96,384]{2,1,0:T(8,128)(2,1)S(1)} %collective-permute-done.5.far_ref), custom_call_target="tpu_custom_call" | custom-call | bytes 2097152 | tf_op jit(solution)/shard_map/pallas_call | solution.py:332
  (1 shorter events, 0.0 us)
Async XLA Ops:
  2.5 25.1 %collective-permute-start = (bf16[128,128]{1,0:T(8,128)(2,1)S(1)}, bf16[128,128]{1,0:T(8,128)(2,1)S(1)}, u32[]{:S(2)}, u32[]{:S(2)}) collective-permute-start(bf16[128,128]{1,0:T(8,128)(2,1)S(1)} %get-tuple-element.16.refs_5_), channel_id=1, source_target_pairs={{38,0},{39,1},{36,2},{37,3},{42,4},{43,5},{40,6},{41,7},{46,8},{47... | collective-permute-start | bytes 98312 | tf_op jit(solution)/shard_map/ppermute | solution.py:253
  3.8 23.8 %collective-permute-start.1 = (bf16[384,128]{1,0:T(8,128)(2,1)S(1)}, bf16[384,128]{1,0:T(8,128)(2,1)S(1)}, u32[]{:S(2)}, u32[]{:S(2)}) collective-permute-start(bf16[384,128]{1,0:T(8,128)(2,1)S(1)} %get-tuple-element.18), channel_id=1, source_target_pairs={{6,0},{7,1},{4,2},{5,3},{10,4},{11,5},{8,6},{9,7},{14,8},{15,9},{1... | collective-permute-start | bytes 294920 | tf_op jit(solution)/shard_map/ppermute | solution.py:253
  5.1 22.5 %collective-permute-start.2 = (bf16[128,384]{1,0:T(8,128)(2,1)S(1)}, bf16[128,384]{1,0:T(8,128)(2,1)S(1)}, u32[]{:S(2)}, u32[]{:S(2)}) collective-permute-start(bf16[128,384]{1,0:T(8,128)(2,1)S(1)} %get-tuple-element.19), channel_id=1, source_target_pairs={{32,0},{33,1},{34,2},{35,3},{36,4},{37,5},{38,6},{39,7},{40,8},{41... | collective-permute-start | bytes 294920 | tf_op jit(solution)/shard_map/ppermute | solution.py:253
  6.4 31.5 %all-to-all-start = ((bf16[64,16,128]{2,1,0:T(8,128)(2,1)}), bf16[64,16,128]{2,1,0:T(8,128)(2,1)S(1)}, u32[]{:S(2)}, u32[]{:S(2)}) async-start(bf16[64,16,128]{2,1,0:T(8,128)(2,1)} %bitcast.1), calls=%async_computation | async-start | bytes 524288 | tf_op jit(solution)/shard_map/all_to_all | solution.py:275
  40.4 5.0 %collective-permute-start.3 = (bf16[2,96,384]{2,1,0:T(8,128)(2,1)S(1)}, bf16[2,96,384]{2,1,0:T(8,128)(2,1)S(1)}, u32[]{:S(2)}, u32[]{:S(2)}) collective-permute-start(bf16[2,96,384]{2,1,0:T(8,128)(2,1)S(1)} %shard_map.91), channel_id=1, source_target_pairs={{0,1},{1,0},{2,3},{3,2},{4,5},{5,4},{6,7},{7,6},{8,9},{9,8},{10,11... | collective-permute-start | bytes 442376 | tf_op jit(solution)/shard_map/ppermute | solution.py:292
  45.3 1.9 %collective-permute-start.4 = (bf16[64,16,128]{2,1,0:T(8,128)(2,1)S(1)}, bf16[64,16,128]{2,1,0:T(8,128)(2,1)S(1)}, u32[]{:S(2)}, u32[]{:S(2)}) collective-permute-start(bf16[64,16,128]{2,1,0:T(8,128)(2,1)S(1)} %all-to-all-done.pixels_ref), channel_id=1, source_target_pairs={{0,1},{1,0},{2,3},{3,2},{4,5},{5,4},{6,7},{7,6},{8,9},{9,8},{10,11... | collective-permute-start | bytes 786440 | tf_op jit(solution)/shard_map/ppermute | solution.py:292
  45.4 5.0 %collective-permute-start.5 = (bf16[2,96,384]{2,1,0:T(8,128)(2,1)S(1)}, bf16[2,96,384]{2,1,0:T(8,128)(2,1)S(1)}, u32[]{:S(2)}, u32[]{:S(2)}) collective-permute-start(bf16[2,96,384]{2,1,0:T(8,128)(2,1)S(1)} %shard_map.92._), channel_id=1, source_target_pairs={{0,2},{1,3},{2,0},{3,1},{4,6},{5,7},{6,4},{7,5},{8,10},{9,11},{10,... | collective-permute-start | bytes 442376 | tf_op jit(solution)/shard_map/ppermute | solution.py:292

commit v13 on v12

--- a/solution.py
+++ b/solution.py
@@ -185,7 +185,8 @@
     block(image_ref, (template_ref,), inv_row_ref, inv_col_ref, out_ref, inner_ref)
 
 
-def merge_kernel(mine_ref, other_ref, out_ref):
+def merge_kernel(mine_ref, other_ref, pixels_ref, out_ref, copy_ref):
+    copy_ref[...] = pixels_ref[...]
     other = other_ref[...].astype(jnp.float32)
     out_ref[0] = jnp.maximum(mine_ref[0], other[0]).astype(out_ref.dtype)
     out_ref[1] = (mine_ref[1] + other[1]).astype(out_ref.dtype)
@@ -317,7 +318,7 @@
     mine = spectra(pixels)
     across = sent(far(image_across, piece), CORE_BIT)
     same = far(image_same, wide)
-    merged = call(merge_kernel, piece, [VMEM] * 2, flops=100000000)(same, across)
+    merged, again = call(merge_kernel, (piece, shape_of(pixels.shape)), [VMEM] * 3, flops=100000000)(same, across, pixels)
     part, image_own = call(
         own_kernel,
         (wide, spectrum),
@@ -326,7 +327,7 @@
         flops=20000000000,
     )(member, rows, g, mine, *tables, merged)
     merged = sent(merged, CHIP_BIT)
-    other = spectra(sent(pixels, CORE_BIT))
+    other = spectra(sent(again, CORE_BIT))
     own = call(rest_kernel, wide, [VMEM] * 5, [inner], flops=1000000000)(image_own, other, *tables, part)
     out = shape_of((1, ROWS, CORE), jnp.float32)
     return call(finish_kernel, (out, out), [VMEM] * 2)(own, merged)

time: 51.5 us -> 42.7 us (0.83)
  starting transfers between devices: 27.5 us -> 22.5 us
  waiting for transfers between devices: 9.97 us -> 6.18 us
    all_to_all x1, waiting for transfers between devices: 9.33 us -> 0.12 us  [shards(): lax.all_to_all(spread.reshape(TILES, 2 * ORI_DEV, TS), ('tile', 'orient')...]
    ppermute x3, waiting for transfers between devices: 0.01 us -> 5.42 us  [halo(): return lax.ppermute(block, ('tile', 'orient'), route)]
    all_to_all x1, starting transfers between devices: 19.7 us -> 14.9 us  [shards(): lax.all_to_all(spread.reshape(TILES, 2 * ORI_DEV, TS), ('tile', 'orient')...]
  transfers between devices with their start and end apart: 7 -> 7, of which waited for: 2 -> 4; matrix products, arithmetic and copies ran while one was open for 0% -> 0% of each run, Pallas kernels for 15% -> 18%
where the time goes in v13:
time: 42.7 us; the launch traced here: 42.4 us
  starting transfers between devices  22.5 us (53%)
  Pallas kernels  13 us (30%)
  waiting for transfers between devices  6.18 us (14%)
  between operations  0.77 us (2%)
    all_to_all x1, starting transfers between devices, shards(): lax.all_to_all(spread.reshape(TILES, 2 * ORI_DEV, TS), ('tile', 'orient')...  14.9 us
    ppermute x3, waiting for transfers between devices, halo(): return lax.ppermute(block, ('tile', 'orient'), route)  5.42 us
    ppermute x3, starting transfers between devices, halo(): return lax.ppermute(block, ('tile', 'orient'), route)  3.88 us
    ppermute x3, starting transfers between devices, sent(): lax.ppermute(piece, 'orient', [(i, i ^ bits) for i in range(MEMBERS)])  3.78 us
    pallas_call x2, Pallas kernels, spectra(): call(template_kernel, shape_of((ORI_DEV, 4 * PAIRS, HALF)), [VMEM] * 3, [...  2.84 us
    pallas_call x2, Pallas kernels, far(): call(far_kernel, out, [VMEM] * 4, [inner], flops=10000000000)  2.26 us
    pallas_call x1, Pallas kernels, shards(): call(prepare_kernel, (shape_of((TILES // 2, 2, 2 * ORI_DEV, TS)), shape_o...  1.81 us
    pallas_call x1, Pallas kernels, shards(): call(own_kernel, (wide, spectrum), [SMEM] + [VMEM] * 5 + [ANY], [inner],...  1.68 us
  transfers between devices with their start and end apart: 7, of which 4 were waited for; matrix products, arithmetic and copies ran while one was open for 0% of the time, Pallas kernels for 18%

profile of v13, /device:TPU:1, one launch (start us, length us, event | category | flops | bytes accessed | tf_op | source)
XLA Modules:
  0.0 42.4 jit_solution(17553757136382930972)
XLA Ops:
  0.6 1.8 %shard_map.86 = (bf16[32,2,16,128]{3,2,1,0:T(8,128)(2,1)}, bf16[384,128]{1,0:T(8,128)(2,1)S(1)}, bf16[128,384]{1,0:T(8,128)(2,1)S(1)}, bf16[128,128]{1,0:T(8,128)(2,1)S(1)}) custom-call(s32[32]{0:T(128)} %ids_hbm.1, bf16[1,384,384]{2,1,0:T(8,128)(2,1)} %refs_4_.1, bf16[256,256]{1,0:T(8,128)(2,1)} %stack_hbm.1), custom_call_target="tpu_custom_call" | custom-call | bytes 2097152 | tf_op jit(solution)/shard_map/pallas_call | solution.py:258
  2.4 14.9 %all-to-all-start = ((bf16[64,16,128]{2,1,0:T(8,128)(2,1)}), bf16[64,16,128]{2,1,0:T(8,128)(2,1)S(1)}, u32[]{:S(2)}, u32[]{:S(2)}) async-start(bf16[64,16,128]{2,1,0:T(8,128)(2,1)} %bitcast.1), calls=%async_computation | async-start | bytes 524288 | tf_op jit(solution)/shard_map/all_to_all | solution.py:276
  17.3 1.3 %collective-permute-start = (bf16[128,128]{1,0:T(8,128)(2,1)S(1)}, bf16[128,128]{1,0:T(8,128)(2,1)S(1)}, u32[]{:S(2)}, u32[]{:S(2)}) collective-permute-start(bf16[128,128]{1,0:T(8,128)(2,1)S(1)} %get-tuple-element.18.refs_5_), channel_id=1, source_target_pairs={{38,0},{39,1},{36,2},{37,3},{42,4},{43,5},{40,6},{41,7},{46,8},{47... | collective-permute-start | bytes 98312 | tf_op jit(solution)/shard_map/ppermute | solution.py:254
  18.6 1.3 %collective-permute-start.1 = (bf16[384,128]{1,0:T(8,128)(2,1)S(1)}, bf16[384,128]{1,0:T(8,128)(2,1)S(1)}, u32[]{:S(2)}, u32[]{:S(2)}) collective-permute-start(bf16[384,128]{1,0:T(8,128)(2,1)S(1)} %get-tuple-element.20), channel_id=1, source_target_pairs={{6,0},{7,1},{4,2},{5,3},{10,4},{11,5},{8,6},{9,7},{14,8},{15,9},{1... | collective-permute-start | bytes 294920 | tf_op jit(solution)/shard_map/ppermute | solution.py:254
  19.9 1.3 %collective-permute-start.2 = (bf16[128,384]{1,0:T(8,128)(2,1)S(1)}, bf16[128,384]{1,0:T(8,128)(2,1)S(1)}, u32[]{:S(2)}, u32[]{:S(2)}) collective-permute-start(bf16[128,384]{1,0:T(8,128)(2,1)S(1)} %get-tuple-element.21), channel_id=1, source_target_pairs={{32,0},{33,1},{34,2},{35,3},{36,4},{37,5},{38,6},{39,7},{40,8},{41... | collective-permute-start | bytes 294920 | tf_op jit(solution)/shard_map/ppermute | solution.py:254
  21.2 1.5 %shard_map.87 = (bf16[512,512]{1,0:T(8,128)(2,1)S(1)}, bf16[512,448]{1,0:T(8,128)(2,1)S(1)}, bf16[96,256]{1,0:T(8,128)(2,1)S(1)}, bf16[512,384]{1,0:T(8,128)(2,1)S(1)}, bf16[1,384,384]{2,1,0:T(8,128)(2,1)S(1)}) custom-call(bf16[512,512]{1,0:T(8,128)(2,1)} %constant.12.clone.refs_0_, bf16[512,448]{1,0:T(8,128)(2,1)} %constant.13.clone.refs_1_, ...), custom_call_target="tpu_custom_call" | custom-call | flops 10000000000 | bytes 2097152 | tf_op jit(solution)/shard_map/pallas_call | solution.py:280
  22.7 3.1 %collective-permute-done.refs_0_ = bf16[128,128]{1,0:T(8,128)(2,1)S(1)} collective-permute-done((bf16[128,128]{1,0:T(8,128)(2,1)S(1)}, bf16[128,128]{1,0:T(8,128)(2,1)S(1)}, u32[]{:S(2)}, u32[]{:S(2)}) %collective-permute-start) | collective-permute-done | bytes 32800 | tf_op jit(solution)/shard_map/ppermute | solution.py:254
  25.8 2.3 %collective-permute-done.1.refs_1_ = bf16[384,128]{1,0:T(8,128)(2,1)S(1)} collective-permute-done((bf16[384,128]{1,0:T(8,128)(2,1)S(1)}, bf16[384,128]{1,0:T(8,128)(2,1)S(1)}, u32[]{:S(2)}, u32[]{:S(2)}) %collective-permute-start.1) | collective-permute-done | bytes 98336 | tf_op jit(solution)/shard_map/ppermute | solution.py:254
  28.1 0.0 collective-permute-done.2.refs_2_
  28.1 1.0 %shard_map.88 = (bf16[512,256]{1,0:T(8,128)(2,1)S(1)}, bf16[512,256]{1,0:T(8,128)(2,1)S(1)}, bf16[2,512,256]{2,1,0:T(8,128)(2,1)S(1)}) custom-call(s32[1]{0:T(128)} %bitcast.member_ref, bf16[128,128]{1,0:T(8,128)(2,1)S(1)} %collective-permute-done.refs_0_, bf16[384,128]{1,0:T(8,128)(2,1)S(1)} %collective-permute-done.1.refs_1_, ...), custom_call_target="tpu_custom_call" | custom-call | flops 1600000000 | bytes 2097152 | tf_op jit(solution)/shard_map/pallas_call | solution.py:306
  29.1 0.1 all-to-all-done.pixels_ref
  29.2 1.4 %shard_map.89.template_ref = bf16[8,512,256]{2,1,0:T(8,128)(2,1)S(1)} custom-call(bf16[64,16,128]{2,1,0:T(8,128)(2,1)S(1)} %all-to-all-done.pixels_ref, bf16[512,512]{1,0:T(8,128)(2,1)S(1)} %get-tuple-element.23.refs_4_.col_ref, bf16[512,448]{1,0:T(8,128)(2,1)S(1)} %get-tuple-element.19.refs_5_.row_ref), custom_call_target="tpu_custom_call" | custom-call | flops 1000000000 | bytes 2097152 | tf_op jit(solution)/shard_map/pallas_call | solution.py:297
  30.7 1.1 %shard_map.91 = bf16[2,96,384]{2,1,0:T(8,128)(2,1)S(1)} custom-call(bf16[512,256]{1,0:T(8,128)(2,1)S(1)} %get-tuple-element.29.image_ref, bf16[8,512,256]{2,1,0:T(8,128)(2,1)S(1)} %shard_map.89.template_ref, bf16[96,256]{1,0:T(8,128)(2,1)S(1)} %get-tuple-element.26.inv_row_ref, bf16[512,384]{1,0:T(8,128)(2,1)S(1)} %get-tuple-element.27.inv_col_ref), custom_call_target="tpu_custom_call" | custom-call | flops 10000000000 | bytes 2097152 | tf_op jit(solution)/shard_map/pallas_call | solution.py:316
  31.8 3.4 %collective-permute-start.3 = (bf16[2,96,384]{2,1,0:T(8,128)(2,1)S(1)}, bf16[2,96,384]{2,1,0:T(8,128)(2,1)S(1)}, u32[]{:S(2)}, u32[]{:S(2)}) collective-permute-start(bf16[2,96,384]{2,1,0:T(8,128)(2,1)S(1)} %shard_map.91), channel_id=1, source_target_pairs={{0,1},{1,0},{2,3},{3,2},{4,5},{5,4},{6,7},{7,6},{8,9},{9,8},{10,11... | collective-permute-start | bytes 442376 | tf_op jit(solution)/shard_map/ppermute | solution.py:293
  35.2 1.1 %shard_map.90.mine_ref = f32[2,96,384]{2,1,0:T(8,128)S(1)} custom-call(bf16[512,256]{1,0:T(8,128)(2,1)S(1)} %get-tuple-element.28.image_ref, bf16[8,512,256]{2,1,0:T(8,128)(2,1)S(1)} %shard_map.89.template_ref, bf16[96,256]{1,0:T(8,128)(2,1)S(1)} %get-tuple-element.26.inv_row_ref, bf16[512,384]{1,0:T(8,128)(2,1)S(1)} %get-tuple-element.27.inv_col_ref), custom_call_target="tpu_custom_call" | custom-call | flops 10000000000 | bytes 2097152 | tf_op jit(solution)/shard_map/pallas_call | solution.py:316
  36.3 0.0 collective-permute-done.3.other_ref
  36.4 0.1 collective-permute-start.5
  36.5 0.3 collective-permute-start.4
  36.8 1.7 %shard_map.93 = (f32[2,96,384]{2,1,0:T(8,128)S(1)}, bf16[512,256]{1,0:T(8,128)(2,1)S(1)}) custom-call(s32[1]{0:T(128)} %bitcast.member_ref, bf16[512,448]{1,0:T(8,128)(2,1)S(1)} %get-tuple-element.19.refs_5_.row_ref, bf16[2,512,256]{2,1,0:T(8,128)(2,1)S(1)} %get-tuple-element.24.g_ref, bf16[8,512,256]{2,1,0:T(8,128)(2,1)S(1)} %shard_map.89.template_ref, ...), custom_call_target="tpu_custom_call" | custom-call | flops 20000000000 | bytes 2097152 | tf_op jit(solution)/shard_map/pallas_call | solution.py:322
  38.5 0.0 collective-permute-done.4.pixels_ref
  38.5 1.4 %shard_map.94.template_ref = bf16[8,512,256]{2,1,0:T(8,128)(2,1)S(1)} custom-call(bf16[64,16,128]{2,1,0:T(8,128)(2,1)S(1)} %collective-permute-done.4.pixels_ref, bf16[512,512]{1,0:T(8,128)(2,1)S(1)} %get-tuple-element.23.refs_4_.col_ref, bf16[512,448]{1,0:T(8,128)(2,1)S(1)} %get-tuple-element.19.refs_5_.row_ref), custom_call_target="tpu_custom_call" | custom-call | flops 1000000000 | bytes 2097152 | tf_op jit(solution)/shard_map/pallas_call | solution.py:297
  39.9 1.1 %shard_map.95.own_ref = f32[2,96,384]{2,1,0:T(8,128)S(1)} custom-call(bf16[512,256]{1,0:T(8,128)(2,1)S(1)} %get-tuple-element.31.image_ref, bf16[8,512,256]{2,1,0:T(8,128)(2,1)S(1)} %shard_map.94.template_ref, bf16[96,256]{1,0:T(8,128)(2,1)S(1)} %get-tuple-element.26.inv_row_ref, bf16[512,384]{1,0:T(8,128)(2,1)S(1)} %get-tuple-element.27.inv_col_ref, ...), custom_call_target="tpu_custom_call" | custom-call | flops 1000000000 | bytes 2097152 | tf_op jit(solution)/shard_map/pallas_call | solution.py:331
  41.1 0.6 %collective-permute-done.5.far_ref = bf16[2,96,384]{2,1,0:T(8,128)(2,1)S(1)} collective-permute-done((bf16[2,96,384]{2,1,0:T(8,128)(2,1)S(1)}, bf16[2,96,384]{2,1,0:T(8,128)(2,1)S(1)}, u32[]{:S(2)}, u32[]{:S(2)}) %collective-permute-start.5) | collective-permute-done | bytes 147488 | tf_op jit(solution)/shard_map/ppermute | solution.py:293
  41.7 0.7 %shard_map.96 = (f32[1,96,384]{2,1,0:T(8,128)}, f32[1,96,384]{2,1,0:T(8,128)}) custom-call(f32[2,96,384]{2,1,0:T(8,128)S(1)} %shard_map.95.own_ref, bf16[2,96,384]{2,1,0:T(8,128)(2,1)S(1)} %collective-permute-done.5.far_ref), custom_call_target="tpu_custom_call" | custom-call | bytes 2097152 | tf_op jit(solution)/shard_map/pallas_call | solution.py:333
  (1 shorter events, 0.0 us)
Async XLA Ops:
  2.4 26.8 %all-to-all-start = ((bf16[64,16,128]{2,1,0:T(8,128)(2,1)}), bf16[64,16,128]{2,1,0:T(8,128)(2,1)S(1)}, u32[]{:S(2)}, u32[]{:S(2)}) async-start(bf16[64,16,128]{2,1,0:T(8,128)(2,1)} %bitcast.1), calls=%async_computation | async-start | bytes 524288 | tf_op jit(solution)/shard_map/all_to_all | solution.py:276
  17.3 8.5 %collective-permute-start = (bf16[128,128]{1,0:T(8,128)(2,1)S(1)}, bf16[128,128]{1,0:T(8,128)(2,1)S(1)}, u32[]{:S(2)}, u32[]{:S(2)}) collective-permute-start(bf16[128,128]{1,0:T(8,128)(2,1)S(1)} %get-tuple-element.18.refs_5_), channel_id=1, source_target_pairs={{38,0},{39,1},{36,2},{37,3},{42,4},{43,5},{40,6},{41,7},{46,8},{47... | collective-permute-start | bytes 98312 | tf_op jit(solution)/shard_map/ppermute | solution.py:254
  18.6 9.5 %collective-permute-start.1 = (bf16[384,128]{1,0:T(8,128)(2,1)S(1)}, bf16[384,128]{1,0:T(8,128)(2,1)S(1)}, u32[]{:S(2)}, u32[]{:S(2)}) collective-permute-start(bf16[384,128]{1,0:T(8,128)(2,1)S(1)} %get-tuple-element.20), channel_id=1, source_target_pairs={{6,0},{7,1},{4,2},{5,3},{10,4},{11,5},{8,6},{9,7},{14,8},{15,9},{1... | collective-permute-start | bytes 294920 | tf_op jit(solution)/shard_map/ppermute | solution.py:254
  19.9 8.2 %collective-permute-start.2 = (bf16[128,384]{1,0:T(8,128)(2,1)S(1)}, bf16[128,384]{1,0:T(8,128)(2,1)S(1)}, u32[]{:S(2)}, u32[]{:S(2)}) collective-permute-start(bf16[128,384]{1,0:T(8,128)(2,1)S(1)} %get-tuple-element.21), channel_id=1, source_target_pairs={{32,0},{33,1},{34,2},{35,3},{36,4},{37,5},{38,6},{39,7},{40,8},{41... | collective-permute-start | bytes 294920 | tf_op jit(solution)/shard_map/ppermute | solution.py:254
  31.8 4.5 %collective-permute-start.3 = (bf16[2,96,384]{2,1,0:T(8,128)(2,1)S(1)}, bf16[2,96,384]{2,1,0:T(8,128)(2,1)S(1)}, u32[]{:S(2)}, u32[]{:S(2)}) collective-permute-start(bf16[2,96,384]{2,1,0:T(8,128)(2,1)S(1)} %shard_map.91), channel_id=1, source_target_pairs={{0,1},{1,0},{2,3},{3,2},{4,5},{5,4},{6,7},{7,6},{8,9},{9,8},{10,11... | collective-permute-start | bytes 442376 | tf_op jit(solution)/shard_map/ppermute | solution.py:293
  36.4 5.3 %collective-permute-start.5 = (bf16[2,96,384]{2,1,0:T(8,128)(2,1)S(1)}, bf16[2,96,384]{2,1,0:T(8,128)(2,1)S(1)}, u32[]{:S(2)}, u32[]{:S(2)}) collective-permute-start(bf16[2,96,384]{2,1,0:T(8,128)(2,1)S(1)} %get-tuple-element.30._), channel_id=1, source_target_pairs={{0,2},{1,3},{2,0},{3,1},{4,6},{5,7},{6,4},{7,5},{8,10},{9,11},{10,... | collective-permute-start | bytes 442376 | tf_op jit(solution)/shard_map/ppermute | solution.py:293
  36.5 2.0 %collective-permute-start.4 = (bf16[64,16,128]{2,1,0:T(8,128)(2,1)S(1)}, bf16[64,16,128]{2,1,0:T(8,128)(2,1)S(1)}, u32[]{:S(2)}, u32[]{:S(2)}) collective-permute-start(bf16[64,16,128]{2,1,0:T(8,128)(2,1)S(1)} %get-tuple-element.32), channel_id=1, source_target_pairs={{0,1},{1,0},{2,3},{3,2},{4,5},{5,4},{6,7},{7,6},{8,9},{9,8},{10,11... | collective-permute-start | bytes 786440 | tf_op jit(solution)/shard_map/ppermute | solution.py:293

commit v14 on v11

--- a/solution.py
+++ b/solution.py
@@ -175,7 +175,7 @@
 
 
 def image_kernel(member_ref, *refs):
-    corner_ref, right_ref, below_ref, own_ref, col_ref, row_ref, across_ref, same_ref, g_ref = refs
+    corner_ref, below_ref, right_ref, own_ref, col_ref, row_ref, across_ref, same_ref, g_ref = refs
     image_columns(own_ref, right_ref, below_ref, corner_ref, col_ref, g_ref)
     image_rows(member_ref, row_ref, g_ref, CHIP_BIT + CORE_BIT, across_ref)
     image_rows(member_ref, row_ref, g_ref, CHIP_BIT, same_ref)
@@ -278,8 +278,8 @@
         flops=10000000000,
     )(*[pinned(array) for array in kept], corner)
     corner = halo(corner, GRID_W + 1)
+    below = halo(below, GRID_W)
     right = halo(right, 1)
-    below = halo(below, GRID_W)
     member = lax.axis_index("orient")[None]
 
     def sent(piece, bits):
@@ -301,7 +301,7 @@
         (spectrum, spectrum, shape_of((2, TILE, HALF))),
         [SMEM] + [VMEM] * 6,
         flops=1600000000,
-    )(member, corner, right, below, own_block, columns, rows)
+    )(member, corner, below, right, own_block, columns, rows)
     inner = pltpu.VMEM((ORI_DEV * ROWS, TILE), jnp.bfloat16)
     piece, wide = shape_of((2, ROWS, CORE)), shape_of((2, ROWS, CORE), jnp.float32)
 

time: 42.6 us -> 43.1 us (1.012); the launches traced: 42.3 us -> 42.3 us
  transfers between devices with their start and end apart: 7 -> 7, of which waited for: 5 -> 6; matrix products, arithmetic and copies ran while one was open for 0% -> 0% of each run, Pallas kernels for 18% -> 18%
where the time goes in v14:
time: 43.1 us; the launch traced here: 42.3 us
  starting transfers between devices  22.3 us (52%)
  Pallas kernels  12.8 us (30%)
  waiting for transfers between devices  6.38 us (15%)
  between operations  0.76 us (2%)
    all_to_all x1, starting transfers between devices, shards(): lax.all_to_all(spread.reshape(TILES, 2 * ORI_DEV, TS), ('tile', 'orient')...  14.9 us
    ppermute x3, waiting for transfers between devices, halo(): return lax.ppermute(block, ('tile', 'orient'), route)  5.01 us
    ppermute x3, starting transfers between devices, halo(): return lax.ppermute(block, ('tile', 'orient'), route)  3.88 us
    ppermute x3, starting transfers between devices, sent(): lax.ppermute(piece, 'orient', [(i, i ^ bits) for i in range(MEMBERS)])  3.6 us
    pallas_call x2, Pallas kernels, spectra(): call(template_kernel, shape_of((ORI_DEV, 4 * PAIRS, HALF)), [VMEM] * 3, [...  2.85 us
    pallas_call x1, Pallas kernels, shards(): call(own_kernel, wide, [SMEM] + [VMEM] * 6, [pltpu.VMEM((4 * PAIRS, HALF)...  2.69 us
    pallas_call x2, Pallas kernels, far(): call(far_kernel, out, [VMEM] * 4, [inner], flops=10000000000)  2.26 us
    pallas_call x1, Pallas kernels, shards(): call(prepare_kernel, (shape_of((TILES // 2, 2, 2 * ORI_DEV, TS)), shape_o...  1.82 us
  transfers between devices with their start and end apart: 7, of which 6 were waited for; matrix products, arithmetic and copies ran while one was open for 0% of the time, Pallas kernels for 18%

profile of v14, /device:TPU:1, one launch (start us, length us, event | category | flops | bytes accessed | tf_op | source)
XLA Modules:
  0.0 42.3 jit_solution(478747712194754282)
XLA Ops:
  0.6 1.8 %shard_map.86 = (bf16[32,2,16,128]{3,2,1,0:T(8,128)(2,1)}, bf16[384,128]{1,0:T(8,128)(2,1)S(1)}, bf16[128,384]{1,0:T(8,128)(2,1)S(1)}, bf16[128,128]{1,0:T(8,128)(2,1)S(1)}) custom-call(s32[32]{0:T(128)} %ids_hbm.1, bf16[1,384,384]{2,1,0:T(8,128)(2,1)} %refs_4_.1, bf16[256,256]{1,0:T(8,128)(2,1)} %stack_hbm.1), custom_call_target="tpu_custom_call" | custom-call | bytes 2097152 | tf_op jit(solution)/shard_map/pallas_call | solution.py:251
  2.5 14.9 %all-to-all-start = ((bf16[64,16,128]{2,1,0:T(8,128)(2,1)}), bf16[64,16,128]{2,1,0:T(8,128)(2,1)S(1)}, u32[]{:S(2)}, u32[]{:S(2)}) async-start(bf16[64,16,128]{2,1,0:T(8,128)(2,1)} %bitcast.1), calls=%async_computation | async-start | bytes 524288 | tf_op jit(solution)/shard_map/all_to_all | solution.py:269
  17.3 1.3 %collective-permute-start = (bf16[128,128]{1,0:T(8,128)(2,1)S(1)}, bf16[128,128]{1,0:T(8,128)(2,1)S(1)}, u32[]{:S(2)}, u32[]{:S(2)}) collective-permute-start(bf16[128,128]{1,0:T(8,128)(2,1)S(1)} %get-tuple-element.14.refs_5_), channel_id=1, source_target_pairs={{38,0},{39,1},{36,2},{37,3},{42,4},{43,5},{40,6},{41,7},{46,8},{47... | collective-permute-start | bytes 98312 | tf_op jit(solution)/shard_map/ppermute | solution.py:247
  18.6 1.3 %collective-permute-start.1 = (bf16[128,384]{1,0:T(8,128)(2,1)S(1)}, bf16[128,384]{1,0:T(8,128)(2,1)S(1)}, u32[]{:S(2)}, u32[]{:S(2)}) collective-permute-start(bf16[128,384]{1,0:T(8,128)(2,1)S(1)} %get-tuple-element.16), channel_id=1, source_target_pairs={{32,0},{33,1},{34,2},{35,3},{36,4},{37,5},{38,6},{39,7},{40,8},{41... | collective-permute-start | bytes 294920 | tf_op jit(solution)/shard_map/ppermute | solution.py:247
  19.9 1.3 %collective-permute-start.2 = (bf16[384,128]{1,0:T(8,128)(2,1)S(1)}, bf16[384,128]{1,0:T(8,128)(2,1)S(1)}, u32[]{:S(2)}, u32[]{:S(2)}) collective-permute-start(bf16[384,128]{1,0:T(8,128)(2,1)S(1)} %get-tuple-element.17), channel_id=1, source_target_pairs={{6,0},{7,1},{4,2},{5,3},{10,4},{11,5},{8,6},{9,7},{14,8},{15,9},{1... | collective-permute-start | bytes 294920 | tf_op jit(solution)/shard_map/ppermute | solution.py:247
  21.2 1.5 %shard_map.87 = (bf16[512,512]{1,0:T(8,128)(2,1)S(1)}, bf16[512,448]{1,0:T(8,128)(2,1)S(1)}, bf16[96,256]{1,0:T(8,128)(2,1)S(1)}, bf16[512,384]{1,0:T(8,128)(2,1)S(1)}, bf16[1,384,384]{2,1,0:T(8,128)(2,1)S(1)}) custom-call(bf16[512,512]{1,0:T(8,128)(2,1)} %constant.12.clone.refs_0_, bf16[512,448]{1,0:T(8,128)(2,1)} %constant.13.clone.refs_1_, ...), custom_call_target="tpu_custom_call" | custom-call | flops 10000000000 | bytes 2097152 | tf_op jit(solution)/shard_map/pallas_call | solution.py:273
  22.7 3.1 %collective-permute-done.refs_0_ = bf16[128,128]{1,0:T(8,128)(2,1)S(1)} collective-permute-done((bf16[128,128]{1,0:T(8,128)(2,1)S(1)}, bf16[128,128]{1,0:T(8,128)(2,1)S(1)}, u32[]{:S(2)}, u32[]{:S(2)}) %collective-permute-start) | collective-permute-done | bytes 32800 | tf_op jit(solution)/shard_map/ppermute | solution.py:247
  25.8 0.5 %collective-permute-done.1.refs_1_ = bf16[128,384]{1,0:T(8,128)(2,1)S(1)} collective-permute-done((bf16[128,384]{1,0:T(8,128)(2,1)S(1)}, bf16[128,384]{1,0:T(8,128)(2,1)S(1)}, u32[]{:S(2)}, u32[]{:S(2)}) %collective-permute-start.1) | collective-permute-done | bytes 98336 | tf_op jit(solution)/shard_map/ppermute | solution.py:247
  26.3 1.4 %collective-permute-done.2.refs_2_ = bf16[384,128]{1,0:T(8,128)(2,1)S(1)} collective-permute-done((bf16[384,128]{1,0:T(8,128)(2,1)S(1)}, bf16[384,128]{1,0:T(8,128)(2,1)S(1)}, u32[]{:S(2)}, u32[]{:S(2)}) %collective-permute-start.2) | collective-permute-done | bytes 98336 | tf_op jit(solution)/shard_map/ppermute | solution.py:247
  27.7 1.0 %shard_map.88 = (bf16[512,256]{1,0:T(8,128)(2,1)S(1)}, bf16[512,256]{1,0:T(8,128)(2,1)S(1)}, bf16[2,512,256]{2,1,0:T(8,128)(2,1)S(1)}) custom-call(s32[1]{0:T(128)} %bitcast.member_ref, bf16[128,128]{1,0:T(8,128)(2,1)S(1)} %collective-permute-done.refs_0_, bf16[128,384]{1,0:T(8,128)(2,1)S(1)} %collective-permute-done.1.refs_1_, ...), custom_call_target="tpu_custom_call" | custom-call | flops 1600000000 | bytes 2097152 | tf_op jit(solution)/shard_map/pallas_call | solution.py:299
  28.7 0.5 %all-to-all-done.pixels_ref = bf16[64,16,128]{2,1,0:T(8,128)(2,1)S(1)} async-done(((bf16[64,16,128]{2,1,0:T(8,128)(2,1)}), bf16[64,16,128]{2,1,0:T(8,128)(2,1)S(1)}, u32[]{:S(2)}, u32[]{:S(2)}) %all-to-all-start) | async-done | bytes 262176 | tf_op jit(solution)/shard_map/all_to_all | solution.py:269
  29.2 1.4 %shard_map.89.mine_ref.template_ref = bf16[8,512,256]{2,1,0:T(8,128)(2,1)S(1)} custom-call(bf16[64,16,128]{2,1,0:T(8,128)(2,1)S(1)} %all-to-all-done.pixels_ref, bf16[512,512]{1,0:T(8,128)(2,1)S(1)} %get-tuple-element.19.refs_4_.col_ref, bf16[512,448]{1,0:T(8,128)(2,1)S(1)} %get-tuple-element.15.refs_5_.row_ref), custom_call_target="tpu_custom_call" | custom-call | flops 1000000000 | bytes 2097152 | tf_op jit(solution)/shard_map/pallas_call | solution.py:290
  30.6 1.1 %shard_map.93 = bf16[2,96,384]{2,1,0:T(8,128)(2,1)S(1)} custom-call(bf16[512,256]{1,0:T(8,128)(2,1)S(1)} %get-tuple-element.25.image_ref, bf16[8,512,256]{2,1,0:T(8,128)(2,1)S(1)} %shard_map.89.mine_ref.template_ref, bf16[96,256]{1,0:T(8,128)(2,1)S(1)} %get-tuple-element.22.inv_row_ref, bf16[512,384]{1,0:T(8,128)(2,1)S(1)} %get-tuple-element.23.inv_col_ref), custom_call_target="tpu_custom_call" | custom-call | flops 10000000000 | bytes 2097152 | tf_op jit(solution)/shard_map/pallas_call | solution.py:309
  31.8 3.4 %collective-permute-start.4 = (bf16[2,96,384]{2,1,0:T(8,128)(2,1)S(1)}, bf16[2,96,384]{2,1,0:T(8,128)(2,1)S(1)}, u32[]{:S(2)}, u32[]{:S(2)}) collective-permute-start(bf16[2,96,384]{2,1,0:T(8,128)(2,1)S(1)} %shard_map.93), channel_id=1, source_target_pairs={{0,1},{1,0},{2,3},{3,2},{4,5},{5,4},{6,7},{7,6},{8,9},{9,8},{10,11... | collective-permute-start | bytes 442376 | tf_op jit(solution)/shard_map/ppermute | solution.py:286
  35.2 0.1 collective-permute-start.3
  35.3 1.1 %shard_map.92.mine_ref = f32[2,96,384]{2,1,0:T(8,128)S(1)} custom-call(bf16[512,256]{1,0:T(8,128)(2,1)S(1)} %get-tuple-element.24.image_ref, bf16[8,512,256]{2,1,0:T(8,128)(2,1)S(1)} %shard_map.89.mine_ref.template_ref, bf16[96,256]{1,0:T(8,128)(2,1)S(1)} %get-tuple-element.22.inv_row_ref, bf16[512,384]{1,0:T(8,128)(2,1)S(1)} %get-tuple-element.23.inv_col_ref), custom_call_target="tpu_custom_call" | custom-call | flops 10000000000 | bytes 2097152 | tf_op jit(solution)/shard_map/pallas_call | solution.py:309
  36.4 0.0 collective-permute-done.4.other_ref
  36.5 0.1 collective-permute-start.5
  36.6 0.2 collective-permute-done.3.pixels_ref
  36.7 1.4 %shard_map.90.other_ref = bf16[8,512,256]{2,1,0:T(8,128)(2,1)S(1)} custom-call(bf16[64,16,128]{2,1,0:T(8,128)(2,1)S(1)} %collective-permute-done.3.pixels_ref, bf16[512,512]{1,0:T(8,128)(2,1)S(1)} %get-tuple-element.19.refs_4_.col_ref, bf16[512,448]{1,0:T(8,128)(2,1)S(1)} %get-tuple-element.15.refs_5_.row_ref), custom_call_target="tpu_custom_call" | custom-call | flops 1000000000 | bytes 2097152 | tf_op jit(solution)/shard_map/pallas_call | solution.py:290
  38.2 2.7 %shard_map.91.own_ref = f32[2,96,384]{2,1,0:T(8,128)S(1)} custom-call(s32[1]{0:T(128)} %bitcast.member_ref, bf16[512,448]{1,0:T(8,128)(2,1)S(1)} %get-tuple-element.15.refs_5_.row_ref, bf16[2,512,256]{2,1,0:T(8,128)(2,1)S(1)} %get-tuple-element.20.g_ref, bf16[8,512,256]{2,1,0:T(8,128)(2,1)S(1)} %shard_map.89.mine_ref.template_ref, ...), custom_call_target="tpu_custom_call" | custom-call | flops 2000000000 | bytes 2097152 | tf_op jit(solution)/shard_map/pallas_call | solution.py:317
  40.9 0.7 %collective-permute-done.5.far_ref = bf16[2,96,384]{2,1,0:T(8,128)(2,1)S(1)} collective-permute-done((bf16[2,96,384]{2,1,0:T(8,128)(2,1)S(1)}, bf16[2,96,384]{2,1,0:T(8,128)(2,1)S(1)}, u32[]{:S(2)}, u32[]{:S(2)}) %collective-permute-start.5) | collective-permute-done | bytes 147488 | tf_op jit(solution)/shard_map/ppermute | solution.py:286
  41.6 0.7 %shard_map.95 = (f32[1,96,384]{2,1,0:T(8,128)}, f32[1,96,384]{2,1,0:T(8,128)}) custom-call(f32[2,96,384]{2,1,0:T(8,128)S(1)} %shard_map.91.own_ref, bf16[2,96,384]{2,1,0:T(8,128)(2,1)S(1)} %collective-permute-done.5.far_ref), custom_call_target="tpu_custom_call" | custom-call | bytes 2097152 | tf_op jit(solution)/shard_map/pallas_call | solution.py:325
  (1 shorter events, 0.0 us)
Async XLA Ops:
  2.5 26.8 %all-to-all-start = ((bf16[64,16,128]{2,1,0:T(8,128)(2,1)}), bf16[64,16,128]{2,1,0:T(8,128)(2,1)S(1)}, u32[]{:S(2)}, u32[]{:S(2)}) async-start(bf16[64,16,128]{2,1,0:T(8,128)(2,1)} %bitcast.1), calls=%async_computation | async-start | bytes 524288 | tf_op jit(solution)/shard_map/all_to_all | solution.py:269
  17.3 8.5 %collective-permute-start = (bf16[128,128]{1,0:T(8,128)(2,1)S(1)}, bf16[128,128]{1,0:T(8,128)(2,1)S(1)}, u32[]{:S(2)}, u32[]{:S(2)}) collective-permute-start(bf16[128,128]{1,0:T(8,128)(2,1)S(1)} %get-tuple-element.14.refs_5_), channel_id=1, source_target_pairs={{38,0},{39,1},{36,2},{37,3},{42,4},{43,5},{40,6},{41,7},{46,8},{47... | collective-permute-start | bytes 98312 | tf_op jit(solution)/shard_map/ppermute | solution.py:247
  18.6 7.7 %collective-permute-start.1 = (bf16[128,384]{1,0:T(8,128)(2,1)S(1)}, bf16[128,384]{1,0:T(8,128)(2,1)S(1)}, u32[]{:S(2)}, u32[]{:S(2)}) collective-permute-start(bf16[128,384]{1,0:T(8,128)(2,1)S(1)} %get-tuple-element.16), channel_id=1, source_target_pairs={{32,0},{33,1},{34,2},{35,3},{36,4},{37,5},{38,6},{39,7},{40,8},{41... | collective-permute-start | bytes 294920 | tf_op jit(solution)/shard_map/ppermute | solution.py:247
  19.9 7.8 %collective-permute-start.2 = (bf16[384,128]{1,0:T(8,128)(2,1)S(1)}, bf16[384,128]{1,0:T(8,128)(2,1)S(1)}, u32[]{:S(2)}, u32[]{:S(2)}) collective-permute-start(bf16[384,128]{1,0:T(8,128)(2,1)S(1)} %get-tuple-element.17), channel_id=1, source_target_pairs={{6,0},{7,1},{4,2},{5,3},{10,4},{11,5},{8,6},{9,7},{14,8},{15,9},{1... | collective-permute-start | bytes 294920 | tf_op jit(solution)/shard_map/ppermute | solution.py:247
  31.8 4.6 %collective-permute-start.4 = (bf16[2,96,384]{2,1,0:T(8,128)(2,1)S(1)}, bf16[2,96,384]{2,1,0:T(8,128)(2,1)S(1)}, u32[]{:S(2)}, u32[]{:S(2)}) collective-permute-start(bf16[2,96,384]{2,1,0:T(8,128)(2,1)S(1)} %shard_map.93), channel_id=1, source_target_pairs={{0,1},{1,0},{2,3},{3,2},{4,5},{5,4},{6,7},{7,6},{8,9},{9,8},{10,11... | collective-permute-start | bytes 442376 | tf_op jit(solution)/shard_map/ppermute | solution.py:286
  35.2 1.5 %collective-permute-start.3 = (bf16[64,16,128]{2,1,0:T(8,128)(2,1)S(1)}, bf16[64,16,128]{2,1,0:T(8,128)(2,1)S(1)}, u32[]{:S(2)}, u32[]{:S(2)}) collective-permute-start(bf16[64,16,128]{2,1,0:T(8,128)(2,1)S(1)} %all-to-all-done.pixels_ref), channel_id=1, source_target_pairs={{0,1},{1,0},{2,3},{3,2},{4,5},{5,4},{6,7},{7,6},{8,9},{9,8},{10,11... | collective-permute-start | bytes 786440 | tf_op jit(solution)/shard_map/ppermute | solution.py:286
  36.5 5.1 %collective-permute-start.5 = (bf16[2,96,384]{2,1,0:T(8,128)(2,1)S(1)}, bf16[2,96,384]{2,1,0:T(8,128)(2,1)S(1)}, u32[]{:S(2)}, u32[]{:S(2)}) collective-permute-start(bf16[2,96,384]{2,1,0:T(8,128)(2,1)S(1)} %shard_map.94), channel_id=1, source_target_pairs={{0,2},{1,3},{2,0},{3,1},{4,6},{5,7},{6,4},{7,5},{8,10},{9,11},{10,... | collective-permute-start | bytes 442376 | tf_op jit(solution)/shard_map/ppermute | solution.py:286

commit v15 on v11

--- a/solution.py
+++ b/solution.py
@@ -196,11 +196,21 @@
     block(image_ref, (mine_ref, other_ref), inv_row_ref, inv_col_ref, out_ref, inner_ref)
 
 
-def finish_kernel(own_ref, far_ref, peak_ref, excess_ref):
-    far = far_ref[...].astype(jnp.float32)
-    peak = jnp.maximum(own_ref[0], far[0])
-    peak_ref[0] = peak
-    excess_ref[0] = peak - (own_ref[1] + far[1]) / (MEMBERS * ORI_DEV)
+def finish_kernel(own_ref, far_ref, peak_hbm, excess_hbm, out_ref, sems):
+    half = ROWS // 2
+    stores = []
+    for k in range(2):
+        rows = pl.ds(k * half, half)
+        peak = jnp.maximum(own_ref[0, rows], far_ref[0, rows].astype(jnp.float32))
+        total = own_ref[1, rows] + far_ref[1, rows].astype(jnp.float32)
+        out_ref[0, rows] = peak
+        out_ref[1, rows] = peak - total * (1.0 / (MEMBERS * ORI_DEV))
+        for i, target in enumerate((peak_hbm, excess_hbm)):
+            store = pltpu.make_async_copy(out_ref.at[i, rows], target.at[0, rows], sems.at[2 * k + i])
+            store.start()
+            stores.append(store)
+    for store in stores:
+        store.wait()
 
 
 VMEM = pl.BlockSpec(memory_space=pltpu.VMEM)
@@ -322,7 +332,8 @@
         flops=2000000000,
     )(member, rows, g, mine, other, *tables)
     out = shape_of((1, ROWS, CORE), jnp.float32)
-    return call(finish_kernel, (out, out), [VMEM] * 2)(own, merged)
+    scratch = [pltpu.VMEM((2, ROWS, CORE), jnp.float32), pltpu.SemaphoreType.DMA((4,))]
+    return call(finish_kernel, (out, out), [VMEM] * 2, scratch, out_specs=(HBM, HBM))(own, merged)
 
 
 def solution(mesh):

time: 42.6 us -> 42.6 us (level)
  no operation moved by 1% of the time
where the time goes in v15:
time: 42.6 us; the launch traced here: 42.3 us
  starting transfers between devices  22.3 us (52%)
  Pallas kernels  12.9 us (30%)
  waiting for transfers between devices  6.41 us (15%)
  between operations  0.76 us (2%)
    all_to_all x1, starting transfers between devices, shards(): lax.all_to_all(spread.reshape(TILES, 2 * ORI_DEV, TS), ('tile', 'orient')...  14.9 us
    ppermute x3, waiting for transfers between devices, halo(): return lax.ppermute(block, ('tile', 'orient'), route)  5.42 us
    ppermute x3, starting transfers between devices, halo(): return lax.ppermute(block, ('tile', 'orient'), route)  3.88 us
    ppermute x3, starting transfers between devices, sent(): lax.ppermute(piece, 'orient', [(i, i ^ bits) for i in range(MEMBERS)])  3.57 us
    pallas_call x2, Pallas kernels, spectra(): call(template_kernel, shape_of((ORI_DEV, 4 * PAIRS, HALF)), [VMEM] * 3, [...  2.84 us
    pallas_call x1, Pallas kernels, shards(): call(own_kernel, wide, [SMEM] + [VMEM] * 6, [pltpu.VMEM((4 * PAIRS, HALF)...  2.69 us
    pallas_call x2, Pallas kernels, far(): call(far_kernel, out, [VMEM] * 4, [inner], flops=10000000000)  2.26 us
    pallas_call x1, Pallas kernels, shards(): call(prepare_kernel, (shape_of((TILES // 2, 2, 2 * ORI_DEV, TS)), shape_o...  1.82 us
  transfers between devices with their start and end apart: 7, of which 5 were waited for; matrix products, arithmetic and copies ran while one was open for 0% of the time, Pallas kernels for 18%

profile of v15, /device:TPU:1, one launch (start us, length us, event | category | flops | bytes accessed | tf_op | source)
XLA Modules:
  0.0 42.3 jit_solution(1714116165893784745)
XLA Ops:
  0.6 1.8 %shard_map.86 = (bf16[32,2,16,128]{3,2,1,0:T(8,128)(2,1)}, bf16[384,128]{1,0:T(8,128)(2,1)S(1)}, bf16[128,384]{1,0:T(8,128)(2,1)S(1)}, bf16[128,128]{1,0:T(8,128)(2,1)S(1)}) custom-call(s32[32]{0:T(128)} %ids_hbm.1, bf16[1,384,384]{2,1,0:T(8,128)(2,1)} %refs_4_.1, bf16[256,256]{1,0:T(8,128)(2,1)} %stack_hbm.1), custom_call_target="tpu_custom_call" | custom-call | bytes 2097152 | tf_op jit(solution)/shard_map/pallas_call | solution.py:261
  2.5 14.9 %all-to-all-start = ((bf16[64,16,128]{2,1,0:T(8,128)(2,1)}), bf16[64,16,128]{2,1,0:T(8,128)(2,1)S(1)}, u32[]{:S(2)}, u32[]{:S(2)}) async-start(bf16[64,16,128]{2,1,0:T(8,128)(2,1)} %bitcast.1), calls=%async_computation | async-start | bytes 524288 | tf_op jit(solution)/shard_map/all_to_all | solution.py:279
  17.3 1.3 %collective-permute-start = (bf16[128,128]{1,0:T(8,128)(2,1)S(1)}, bf16[128,128]{1,0:T(8,128)(2,1)S(1)}, u32[]{:S(2)}, u32[]{:S(2)}) collective-permute-start(bf16[128,128]{1,0:T(8,128)(2,1)S(1)} %get-tuple-element.14.refs_5_), channel_id=1, source_target_pairs={{38,0},{39,1},{36,2},{37,3},{42,4},{43,5},{40,6},{41,7},{46,8},{47... | collective-permute-start | bytes 98312 | tf_op jit(solution)/shard_map/ppermute | solution.py:257
  18.6 1.3 %collective-permute-start.1 = (bf16[384,128]{1,0:T(8,128)(2,1)S(1)}, bf16[384,128]{1,0:T(8,128)(2,1)S(1)}, u32[]{:S(2)}, u32[]{:S(2)}) collective-permute-start(bf16[384,128]{1,0:T(8,128)(2,1)S(1)} %get-tuple-element.16), channel_id=1, source_target_pairs={{6,0},{7,1},{4,2},{5,3},{10,4},{11,5},{8,6},{9,7},{14,8},{15,9},{1... | collective-permute-start | bytes 294920 | tf_op jit(solution)/shard_map/ppermute | solution.py:257
  19.9 1.3 %collective-permute-start.2 = (bf16[128,384]{1,0:T(8,128)(2,1)S(1)}, bf16[128,384]{1,0:T(8,128)(2,1)S(1)}, u32[]{:S(2)}, u32[]{:S(2)}) collective-permute-start(bf16[128,384]{1,0:T(8,128)(2,1)S(1)} %get-tuple-element.17), channel_id=1, source_target_pairs={{32,0},{33,1},{34,2},{35,3},{36,4},{37,5},{38,6},{39,7},{40,8},{41... | collective-permute-start | bytes 294920 | tf_op jit(solution)/shard_map/ppermute | solution.py:257
  21.2 1.5 %shard_map.87 = (bf16[512,512]{1,0:T(8,128)(2,1)S(1)}, bf16[512,448]{1,0:T(8,128)(2,1)S(1)}, bf16[96,256]{1,0:T(8,128)(2,1)S(1)}, bf16[512,384]{1,0:T(8,128)(2,1)S(1)}, bf16[1,384,384]{2,1,0:T(8,128)(2,1)S(1)}) custom-call(bf16[512,512]{1,0:T(8,128)(2,1)} %constant.12.clone.refs_0_, bf16[512,448]{1,0:T(8,128)(2,1)} %constant.13.clone.refs_1_, ...), custom_call_target="tpu_custom_call" | custom-call | flops 10000000000 | bytes 2097152 | tf_op jit(solution)/shard_map/pallas_call | solution.py:283
  22.7 3.1 %collective-permute-done.refs_0_ = bf16[128,128]{1,0:T(8,128)(2,1)S(1)} collective-permute-done((bf16[128,128]{1,0:T(8,128)(2,1)S(1)}, bf16[128,128]{1,0:T(8,128)(2,1)S(1)}, u32[]{:S(2)}, u32[]{:S(2)}) %collective-permute-start) | collective-permute-done | bytes 32800 | tf_op jit(solution)/shard_map/ppermute | solution.py:257
  25.8 2.3 %collective-permute-done.1.refs_1_ = bf16[384,128]{1,0:T(8,128)(2,1)S(1)} collective-permute-done((bf16[384,128]{1,0:T(8,128)(2,1)S(1)}, bf16[384,128]{1,0:T(8,128)(2,1)S(1)}, u32[]{:S(2)}, u32[]{:S(2)}) %collective-permute-start.1) | collective-permute-done | bytes 98336 | tf_op jit(solution)/shard_map/ppermute | solution.py:257
  28.1 0.0 collective-permute-done.2.refs_2_
  28.1 1.0 %shard_map.88 = (bf16[512,256]{1,0:T(8,128)(2,1)S(1)}, bf16[512,256]{1,0:T(8,128)(2,1)S(1)}, bf16[2,512,256]{2,1,0:T(8,128)(2,1)S(1)}) custom-call(s32[1]{0:T(128)} %bitcast.member_ref, bf16[128,128]{1,0:T(8,128)(2,1)S(1)} %collective-permute-done.refs_0_, bf16[384,128]{1,0:T(8,128)(2,1)S(1)} %collective-permute-done.1.refs_1_, ...), custom_call_target="tpu_custom_call" | custom-call | flops 1600000000 | bytes 2097152 | tf_op jit(solution)/shard_map/pallas_call | solution.py:309
  29.1 0.1 all-to-all-done.pixels_ref
  29.2 1.4 %shard_map.89.mine_ref.template_ref = bf16[8,512,256]{2,1,0:T(8,128)(2,1)S(1)} custom-call(bf16[64,16,128]{2,1,0:T(8,128)(2,1)S(1)} %all-to-all-done.pixels_ref, bf16[512,512]{1,0:T(8,128)(2,1)S(1)} %get-tuple-element.19.refs_4_.col_ref, bf16[512,448]{1,0:T(8,128)(2,1)S(1)} %get-tuple-element.15.refs_5_.row_ref), custom_call_target="tpu_custom_call" | custom-call | flops 1000000000 | bytes 2097152 | tf_op jit(solution)/shard_map/pallas_call | solution.py:300
  30.7 1.1 %shard_map.93 = bf16[2,96,384]{2,1,0:T(8,128)(2,1)S(1)} custom-call(bf16[512,256]{1,0:T(8,128)(2,1)S(1)} %get-tuple-element.25.image_ref, bf16[8,512,256]{2,1,0:T(8,128)(2,1)S(1)} %shard_map.89.mine_ref.template_ref, bf16[96,256]{1,0:T(8,128)(2,1)S(1)} %get-tuple-element.22.inv_row_ref, bf16[512,384]{1,0:T(8,128)(2,1)S(1)} %get-tuple-element.23.inv_col_ref), custom_call_target="tpu_custom_call" | custom-call | flops 10000000000 | bytes 2097152 | tf_op jit(solution)/shard_map/pallas_call | solution.py:319
  31.8 3.4 %collective-permute-start.4 = (bf16[2,96,384]{2,1,0:T(8,128)(2,1)S(1)}, bf16[2,96,384]{2,1,0:T(8,128)(2,1)S(1)}, u32[]{:S(2)}, u32[]{:S(2)}) collective-permute-start(bf16[2,96,384]{2,1,0:T(8,128)(2,1)S(1)} %shard_map.93), channel_id=1, source_target_pairs={{0,1},{1,0},{2,3},{3,2},{4,5},{5,4},{6,7},{7,6},{8,9},{9,8},{10,11... | collective-permute-start | bytes 442376 | tf_op jit(solution)/shard_map/ppermute | solution.py:296
  35.2 0.1 collective-permute-start.3
  35.3 1.1 %shard_map.92.mine_ref = f32[2,96,384]{2,1,0:T(8,128)S(1)} custom-call(bf16[512,256]{1,0:T(8,128)(2,1)S(1)} %get-tuple-element.24.image_ref, bf16[8,512,256]{2,1,0:T(8,128)(2,1)S(1)} %shard_map.89.mine_ref.template_ref, bf16[96,256]{1,0:T(8,128)(2,1)S(1)} %get-tuple-element.22.inv_row_ref, bf16[512,384]{1,0:T(8,128)(2,1)S(1)} %get-tuple-element.23.inv_col_ref), custom_call_target="tpu_custom_call" | custom-call | flops 10000000000 | bytes 2097152 | tf_op jit(solution)/shard_map/pallas_call | solution.py:319
  36.4 0.0 collective-permute-done.4.other_ref
  36.5 0.1 collective-permute-start.5
  36.6 0.2 collective-permute-done.3.pixels_ref
  36.7 1.4 %shard_map.90.other_ref = bf16[8,512,256]{2,1,0:T(8,128)(2,1)S(1)} custom-call(bf16[64,16,128]{2,1,0:T(8,128)(2,1)S(1)} %collective-permute-done.3.pixels_ref, bf16[512,512]{1,0:T(8,128)(2,1)S(1)} %get-tuple-element.19.refs_4_.col_ref, bf16[512,448]{1,0:T(8,128)(2,1)S(1)} %get-tuple-element.15.refs_5_.row_ref), custom_call_target="tpu_custom_call" | custom-call | flops 1000000000 | bytes 2097152 | tf_op jit(solution)/shard_map/pallas_call | solution.py:300
  38.2 2.7 %shard_map.91.own_ref = f32[2,96,384]{2,1,0:T(8,128)S(1)} custom-call(s32[1]{0:T(128)} %bitcast.member_ref, bf16[512,448]{1,0:T(8,128)(2,1)S(1)} %get-tuple-element.15.refs_5_.row_ref, bf16[2,512,256]{2,1,0:T(8,128)(2,1)S(1)} %get-tuple-element.20.g_ref, bf16[8,512,256]{2,1,0:T(8,128)(2,1)S(1)} %shard_map.89.mine_ref.template_ref, ...), custom_call_target="tpu_custom_call" | custom-call | flops 2000000000 | bytes 2097152 | tf_op jit(solution)/shard_map/pallas_call | solution.py:327
  40.9 0.7 %collective-permute-done.5.far_ref = bf16[2,96,384]{2,1,0:T(8,128)(2,1)S(1)} collective-permute-done((bf16[2,96,384]{2,1,0:T(8,128)(2,1)S(1)}, bf16[2,96,384]{2,1,0:T(8,128)(2,1)S(1)}, u32[]{:S(2)}, u32[]{:S(2)}) %collective-permute-start.5) | collective-permute-done | bytes 147488 | tf_op jit(solution)/shard_map/ppermute | solution.py:296
  41.6 0.8 %shard_map.95 = (f32[1,96,384]{2,1,0:T(8,128)}, f32[1,96,384]{2,1,0:T(8,128)}) custom-call(f32[2,96,384]{2,1,0:T(8,128)S(1)} %shard_map.91.own_ref, bf16[2,96,384]{2,1,0:T(8,128)(2,1)S(1)} %collective-permute-done.5.far_ref), custom_call_target="tpu_custom_call" | custom-call | bytes 2097152 | tf_op jit(solution)/shard_map/pallas_call | solution.py:336
  (1 shorter events, 0.0 us)
Async XLA Ops:
  2.5 26.8 %all-to-all-start = ((bf16[64,16,128]{2,1,0:T(8,128)(2,1)}), bf16[64,16,128]{2,1,0:T(8,128)(2,1)S(1)}, u32[]{:S(2)}, u32[]{:S(2)}) async-start(bf16[64,16,128]{2,1,0:T(8,128)(2,1)} %bitcast.1), calls=%async_computation | async-start | bytes 524288 | tf_op jit(solution)/shard_map/all_to_all | solution.py:279
  17.3 8.5 %collective-permute-start = (bf16[128,128]{1,0:T(8,128)(2,1)S(1)}, bf16[128,128]{1,0:T(8,128)(2,1)S(1)}, u32[]{:S(2)}, u32[]{:S(2)}) collective-permute-start(bf16[128,128]{1,0:T(8,128)(2,1)S(1)} %get-tuple-element.14.refs_5_), channel_id=1, source_target_pairs={{38,0},{39,1},{36,2},{37,3},{42,4},{43,5},{40,6},{41,7},{46,8},{47... | collective-permute-start | bytes 98312 | tf_op jit(solution)/shard_map/ppermute | solution.py:257
  18.6 9.5 %collective-permute-start.1 = (bf16[384,128]{1,0:T(8,128)(2,1)S(1)}, bf16[384,128]{1,0:T(8,128)(2,1)S(1)}, u32[]{:S(2)}, u32[]{:S(2)}) collective-permute-start(bf16[384,128]{1,0:T(8,128)(2,1)S(1)} %get-tuple-element.16), channel_id=1, source_target_pairs={{6,0},{7,1},{4,2},{5,3},{10,4},{11,5},{8,6},{9,7},{14,8},{15,9},{1... | collective-permute-start | bytes 294920 | tf_op jit(solution)/shard_map/ppermute | solution.py:257
  19.9 8.2 %collective-permute-start.2 = (bf16[128,384]{1,0:T(8,128)(2,1)S(1)}, bf16[128,384]{1,0:T(8,128)(2,1)S(1)}, u32[]{:S(2)}, u32[]{:S(2)}) collective-permute-start(bf16[128,384]{1,0:T(8,128)(2,1)S(1)} %get-tuple-element.17), channel_id=1, source_target_pairs={{32,0},{33,1},{34,2},{35,3},{36,4},{37,5},{38,6},{39,7},{40,8},{41... | collective-permute-start | bytes 294920 | tf_op jit(solution)/shard_map/ppermute | solution.py:257
  31.8 4.6 %collective-permute-start.4 = (bf16[2,96,384]{2,1,0:T(8,128)(2,1)S(1)}, bf16[2,96,384]{2,1,0:T(8,128)(2,1)S(1)}, u32[]{:S(2)}, u32[]{:S(2)}) collective-permute-start(bf16[2,96,384]{2,1,0:T(8,128)(2,1)S(1)} %shard_map.93), channel_id=1, source_target_pairs={{0,1},{1,0},{2,3},{3,2},{4,5},{5,4},{6,7},{7,6},{8,9},{9,8},{10,11... | collective-permute-start | bytes 442376 | tf_op jit(solution)/shard_map/ppermute | solution.py:296
  35.2 1.5 %collective-permute-start.3 = (bf16[64,16,128]{2,1,0:T(8,128)(2,1)S(1)}, bf16[64,16,128]{2,1,0:T(8,128)(2,1)S(1)}, u32[]{:S(2)}, u32[]{:S(2)}) collective-permute-start(bf16[64,16,128]{2,1,0:T(8,128)(2,1)S(1)} %all-to-all-done.pixels_ref), channel_id=1, source_target_pairs={{0,1},{1,0},{2,3},{3,2},{4,5},{5,4},{6,7},{7,6},{8,9},{9,8},{10,11... | collective-permute-start | bytes 786440 | tf_op jit(solution)/shard_map/ppermute | solution.py:296
  36.5 5.1 %collective-permute-start.5 = (bf16[2,96,384]{2,1,0:T(8,128)(2,1)S(1)}, bf16[2,96,384]{2,1,0:T(8,128)(2,1)S(1)}, u32[]{:S(2)}, u32[]{:S(2)}) collective-permute-start(bf16[2,96,384]{2,1,0:T(8,128)(2,1)S(1)} %shard_map.94), channel_id=1, source_target_pairs={{0,2},{1,3},{2,0},{3,1},{4,6},{5,7},{6,4},{7,5},{8,10},{9,11},{10,... | collective-permute-start | bytes 442376 | tf_op jit(solution)/shard_map/ppermute | solution.py:296
